TPU v7x, 512 devices: a whole 4x4x16 slice. The times are simulated.
512 devices in a mesh: dp: 32 (over y, z_hi, x), tensor: 16 (over z_lo, core).
Axes of the slice: x: 4, y: 4, z: 16 (z_hi: 2, z_lo: 8; z = z_hi * 8 + z_lo), core: 2. Of those that a mesh axis runs over, the one named last changes fastest.
Arguments:
- activations: bfloat16 [4096, 4096], P('dp'), may hold values from -6 to 6
- act_basis: bfloat16 [4096, 4096], P('tensor'), may hold values from -0.09375 to 0.09375
- out_grads: bfloat16 [4096, 14336], P('dp', 'tensor'), may hold values from -3 to 3
- grad_basis: bfloat16 [14336, 14336], P('dp', 'tensor'), may hold values from -0.046875 to 0.046875
Outputs:
- rotated_gradient: float32 [14336, 4096], P('dp', 'tensor')
- scaling: float32 [14336, 4096], P('dp', 'tensor')
All inputs are finite; a program needn't handle non-finite values.
Results may differ from a plain program's by a relative error of at most 0.035.
Values may be sent and summed in bfloat16 or wider, within the bound.
No kernel may reach another device: no remote copies, remote signals or barrier semaphores. Data moves between devices by JAX's collectives and lax.ppermute only.
A program may use at most 64 MiB of HBM per device.

v0:
```python
import jax
import jax.numpy as jnp
from jax import lax
from jax.sharding import PartitionSpec as P


def square_round(values):
    wide = values.astype(jnp.float32)
    return (wide * wide).astype(jnp.bfloat16)


def body(activations, act_basis, out_grads, grad_basis):
    rotated_acts = lax.dot_general(
        activations, act_basis, (((1,), (1,)), ((), ())), preferred_element_type=jnp.float32
    ).astype(jnp.bfloat16)
    block_terms = lax.dot_general(
        grad_basis,
        lax.all_gather(out_grads, "dp", axis=0, tiled=True),
        (((1,), (1,)), ((), ())),
        preferred_element_type=jnp.float32,
    )
    shares = lax.psum_scatter(
        block_terms.astype(jnp.bfloat16), "tensor", scatter_dimension=1, tiled=True
    )
    rotated_grads = lax.all_gather(shares, "tensor", axis=1, tiled=True)
    grad_squares = square_round(rotated_grads)
    token_count = rotated_grads.shape[1]
    all_acts = lax.all_gather(rotated_acts, "dp", axis=0, tiled=True)
    gradient = jnp.dot(rotated_grads, all_acts, preferred_element_type=jnp.float32)
    summed = jnp.dot(grad_squares, square_round(all_acts), preferred_element_type=jnp.float32)
    return (gradient, summed / token_count)


def solution(mesh):
    return jax.shard_map(
        body,
        mesh=mesh,
        in_specs=(P("dp", None), P("tensor", None), P("dp", "tensor"), P("dp", "tensor")),
        out_specs=(P("dp", "tensor"), P("dp", "tensor")),
        check_vma=False,
    )
```

profile of v0, /device:TPU:1, one launch (start us, length us, event | category | flops | bytes accessed | tf_op | source)
XLA Modules:
  0.0 590.2 jit_solution(8815794991216815138)
XLA Ops:
  7.2 0.0 copy-start
  7.2 0.0 all-gather.4.cloned.1.call-start
  7.2 0.7 all-gather.4.cloned.1.call-update
  7.9 0.0 reduce-scatter.2.cloned.1.call-start
  8.0 238.8 %all-gather.4.cloned.1.call-done = bf16[4096,896]{1,0:T(8,128)(2,1)} async-done(((bf16[128,896]{1,0:T(8,128)(2,1)}), bf16[4096,896]{1,0:T(8,128)(2,1)}) %all-gather.4.cloned.1.call-update) | async-done | bytes 7340048 | tf_op jit(solution)/shard_map/all_gather | solution.py:18
  246.8 9.2 %convolution_convert_fusion = bf16[448,4096]{1,0:T(8,128)(2,1)} fusion(bf16[448,896]{1,0:T(8,128)(2,1)} %param.7, bf16[4096,896]{1,0:T(8,128)(2,1)} %all-gather.4.cloned.1.call-done), kind=kOutput, calls=%fused_computation.1 | convolution fusion | flops 3290169344 | bytes 11812864 | tf_op jit(solution)/shard_map/dot_general | solution.py:16
  256.0 0.0 copy-start.1
  256.0 0.0 reduce-scatter.2.cloned.1.call-update
  256.1 0.0 all-gather.8.cloned.1.call-start
  256.1 0.0 copy-done
  256.1 1.1 copy-done.1
  257.3 1.5 convolution_convert_fusion.1
  258.7 0.0 all-gather.8.cloned.1.call-update
  258.8 0.0 all-gather.6.cloned.1.call-start
  258.8 98.0 %reduce-scatter.2.cloned.1.call-done = bf16[448,256]{1,0:T(8,128)(2,1)} async-done(((bf16[448,4096]{1,0:T(8,128)(2,1)}), bf16[448,256]{1,0:T(8,128)(2,1)}) %reduce-scatter.2.cloned.1.call-update) | async-done | bytes 229392 | tf_op jit(solution)/shard_map/reduce_scatter | solution.py:22
  356.8 0.0 all-gather.6.cloned.1.call-update
  356.9 136.7 %all-gather.8.cloned.1.call-done = bf16[4096,256]{1,0:T(8,128)(2,1)} async-done(((bf16[128,256]{1,0:T(8,128)(2,1)}), bf16[4096,256]{1,0:T(8,128)(2,1)}) %all-gather.8.cloned.1.call-update) | async-done | bytes 2097168 | tf_op jit(solution)/shard_map/all_gather | solution.py:28
  493.5 83.5 %all-gather.6.cloned.1.call-done = bf16[448,4096]{1,0:T(8,128)(2,1)} async-done(((bf16[448,256]{1,0:T(8,128)(2,1)}), bf16[448,4096]{1,0:T(8,128)(2,1)}) %all-gather.6.cloned.1.call-update) | async-done | bytes 3670032 | tf_op jit(solution)/shard_map/all_gather | solution.py:25
  577.0 0.0 copy-start.2
  577.0 0.0 copy-start.3
  577.0 4.8 fusion.1
  581.8 0.0 copy-done.2
  581.8 0.0 copy-done.3
  581.8 1.9 fusion.2
Async XLA Ops:
  7.2 249.0 %copy-start = (bf16[256,4096]{1,0:T(8,128)(2,1)S(1)}, bf16[256,4096]{1,0:T(8,128)(2,1)}, u32[]{:S(2)}) copy-start(bf16[256,4096]{1,0:T(8,128)(2,1)} %param.5) | copy-start | bytes 6291460
  7.2 239.6 %all-gather.4.cloned.1.call-start = ((), (), s32[]{:S(2)}) async-start(), calls=%async_computation.1 | async-start | bytes 7569408 | tf_op jit(solution)/shard_map/all_gather | solution.py:18
  7.9 348.9 %reduce-scatter.2.cloned.1.call-start = ((), (), s32[]{:S(2)}) async-start(), calls=%async_computation.2 | async-start | bytes 3899392 | tf_op jit(solution)/shard_map/reduce_scatter | solution.py:22
  256.0 1.2 copy-start.1
  256.1 237.5 %all-gather.8.cloned.1.call-start = ((), (), s32[]{:S(2)}) async-start(), calls=%async_computation.4 | async-start | bytes 2162688 | tf_op jit(solution)/shard_map/all_gather | solution.py:28
  258.8 318.3 %all-gather.6.cloned.1.call-start = ((), (), s32[]{:S(2)}) async-start(), calls=%async_computation.3 | async-start | bytes 3899392 | tf_op jit(solution)/shard_map/all_gather | solution.py:25
  577.0 4.8 copy-start.2
  577.0 4.8 copy-start.3
Sparse Core Ops, SparseCore 0:
  12.3 234.4 all-gather.3
  256.2 100.6 reduce-scatter.1
  361.8 131.6 all-gather.7
  495.4 81.5 all-gather.5
where the time goes:
time: 591 us; the launch traced here: 590 us
  waiting for transfers between devices  558 us (94%)
  matrix products  17.4 us (3%)
  between operations  13.8 us (2%)
    all_gather x1, waiting for transfers between devices, body(): lax.all_gather(out_grads, 'dp', axis=0, tiled=True)  239 us
    all_gather x1, waiting for transfers between devices, body(): all_acts = lax.all_gather(rotated_acts, 'dp', axis=0, tiled=True)  137 us
    reduce_scatter x1, waiting for transfers between devices, body(): lax.psum_scatter(block_terms.astype(jnp.bfloat16), 'tensor', scatter_dime...  98 us
    all_gather x1, waiting for transfers between devices, body(): rotated_grads = lax.all_gather(shares, 'tensor', axis=1, tiled=True)  83.5 us
  transfers between devices with their start and end apart: 4, of which 4 were waited for; matrix products, arithmetic and copies ran while one was open for 0% of the time, Pallas kernels for 0%

commit v1 on v0

v1 whole, which is shorter than its diff:
```python
import jax
import jax.numpy as jnp
from jax import lax
from jax.experimental import pallas as pl
from jax.experimental.pallas import tpu as pltpu
from jax.sharding import Mesh, PartitionSpec as P

F32 = jnp.float32
BF16 = jnp.bfloat16
NX, NY, NM = 4, 4, 4
VMEM = pl.BlockSpec(memory_space=pltpu.VMEM)
SMEM = pl.BlockSpec(memory_space=pltpu.SMEM)


def params():
    return pltpu.CompilerParams(vmem_limit_bytes=40 * 1024 * 1024)


def cost(flops, nbytes):
    return pl.CostEstimate(flops=flops, bytes_accessed=nbytes, transcendentals=0)


def from_rel(value, axis, step, size):
    return lax.ppermute(value, axis, [((i + step) % size, i) for i in range(size)])


def block_kernel(where_ref, *refs):
    tokens, basis = refs[:8], refs[8:12]
    own_ref, other_ref, half_ref = refs[12:]
    here, half, parity = where_ref[0], where_ref[1], where_ref[2]
    rows = tokens[0].shape[0]
    for j in range(NY):

        @pl.when(half == 0)
        def _():
            half_ref[j * rows : (j + 1) * rows] = tokens[j][...]

        @pl.when(half == 1)
        def _():
            half_ref[j * rows : (j + 1) * rows] = tokens[NY + j][...]

    width = 2 * rows
    for j in range(NX):
        home = lax.rem(here + j, NX)
        left = basis[j][...]
        for rel, out in ((1, other_ref), (0, own_ref)):
            start = pl.multiple_of(lax.rem(parity + rel, 2) * width, width)
            right = half_ref[pl.ds(start, width)]
            out[home] = lax.dot_general(
                left, right, (((1,), (1,)), ((), ())), preferred_element_type=F32
            ).astype(BF16)


def block_sums(where, tokens, basis):
    rows, depth = tokens[0].shape
    crows = basis[0].shape[0]
    shape = jax.ShapeDtypeStruct((NX, crows, 2 * rows), BF16)
    return pl.pallas_call(
        block_kernel,
        out_shape=(shape, shape),
        in_specs=[SMEM] + [VMEM] * 12,
        out_specs=(VMEM, VMEM),
        scratch_shapes=[pltpu.VMEM((NY * rows, depth), BF16)],
        compiler_params=params(),
        cost_estimate=cost(2 * NX * crows * NY * rows * depth, 9 * 2**20),
        name="block_sums",
    )(where, *tokens, *basis)


def final_kernel(where_ref, mine_ref, mate_ref, acts_ref, grad_ref, scale_ref):
    y, core = where_ref[0], where_ref[1]
    pairs, _, _, piece, width = mine_ref.shape
    rows = acts_ref.shape[3]
    total_tokens = 2 * NY * NX * rows
    first = True
    for side, ref in ((0, mine_ref), (1, mate_ref)):
        half = lax.rem(core + side, 2)
        for parity in range(2):
            for x in range(NX):
                g = ref[:, parity, x].reshape(pairs * piece, width)
                a = jnp.concatenate(
                    [acts_ref[lax.rem(y + 2 * parity + n, NY), x, half] for n in range(2)], axis=0
                )
                gw, aw = g.astype(F32), a.astype(F32)
                g2, a2 = (gw * gw).astype(BF16), (aw * aw).astype(BF16)
                p1 = jnp.dot(g, a, preferred_element_type=F32)
                p2 = jnp.dot(g2, a2, preferred_element_type=F32)
                if first:
                    grad_ref[...] = p1
                    scale_ref[...] = p2
                    first = False
                else:
                    grad_ref[...] += p1
                    scale_ref[...] += p2
    scale_ref[...] = scale_ref[...] / total_tokens


def final(where, mine, mate, acts):
    pairs, _, _, piece, width = mine.shape
    shape = jax.ShapeDtypeStruct((pairs * piece, acts.shape[-1]), F32)
    return pl.pallas_call(
        final_kernel,
        out_shape=(shape, shape),
        in_specs=[SMEM, VMEM, VMEM, VMEM],
        out_specs=(VMEM, VMEM),
        compiler_params=params(),
        cost_estimate=cost(4 * 448 * 4096 * 256, 7 * 2**20),
        name="final_products",
    )(where, mine, mate, acts)


def added(*values):
    total = values[0].astype(F32)
    for v in values[1:]:
        total = total + v.astype(F32)
    return total.astype(BF16)


def body(activations, act_basis, out_grads, grad_basis):
    x, y, core, parity = (lax.axis_index(a) for a in ("x", "y", "c", "p"))
    other_half = lax.ppermute(out_grads, "h", [(0, 1), (1, 0)])
    tokens = [out_grads] + [from_rel(out_grads, "y", j, NY) for j in (1, 2, 3)]
    basis = [grad_basis] + [from_rel(grad_basis, "x", j, NX) for j in (1, 2, 3)]
    tokens += [other_half] + [from_rel(other_half, "y", j, NY) for j in (1, 2, 3)]

    acts = lax.dot_general(
        activations, act_basis, (((1,), (1,)), ((), ())), preferred_element_type=F32
    ).astype(BF16)
    both = jnp.stack([acts, lax.ppermute(acts, "h", [(0, 1), (1, 0)])])
    all_acts = lax.all_gather(both, ("y", "x"), axis=0, tiled=False)
    all_acts = all_acts.reshape(NY, NX, *both.shape)

    swap = lambda v, axis: lax.ppermute(v, axis, [(0, 1), (1, 0)])
    send_own, send_other = block_sums(jnp.stack([x, 1 - core, parity]).astype(jnp.int32), tokens, basis)
    got_other = swap(send_other, "c")
    got_own = swap(send_own, "c")
    mine_own, mine_other = block_sums(jnp.stack([x, core, parity]).astype(jnp.int32), tokens, basis)
    pair = swap(added(mine_other, got_other), "p")
    partial = added(mine_own, got_own, pair)
    crows, width = partial.shape[1:]
    piece = crows // NM
    spread = lax.all_to_all(
        partial.reshape(NX * NM, piece, width), ("x", "m"), split_axis=0, concat_axis=0, tiled=True
    ).reshape(NX, NM, piece, width)
    own = added(*[spread[:, j] for j in range(NM)])
    mine = lax.all_gather(own, ("m", "p"), axis=0, tiled=False).reshape(NM, 2, NX, piece, width)
    mate = swap(mine, "c")
    return final(jnp.stack([y, core]).astype(jnp.int32), mine, mate, all_acts)


def solution(mesh):
    fine = Mesh(mesh.devices.reshape(NY, 2, NX, NM, 2, 2), ("y", "h", "x", "m", "p", "c"))
    dp, tensor = ("y", "h", "x"), ("m", "p", "c")
    return jax.shard_map(
        body,
        mesh=fine,
        in_specs=(P(dp, None), P(tensor, None), P(dp, tensor), P(dp, tensor)),
        out_specs=(P(dp, tensor), P(dp, tensor)),
        check_vma=False,
    )
```

time: 591 us -> 317 us (0.54)
  waiting for transfers between devices: 558 us -> 138 us
  starting transfers between devices: 0.16 us -> 84 us
  blocking collectives: 0 us -> 56.6 us
  matrix products: 17.4 us -> 0.83 us
  Pallas kernels: 0 us -> 12.3 us
  local copies, waits for them, and re-layouts: 1.16 us -> 8.44 us
    all_gather x3 -> x2, waiting for transfers between devices: 459 us -> 99.7 us  [the longest x1 56.1 us: body(): all_acts = lax.all_gather(both, ('y', 'x'), axis=0, tiled=False)]
    reduce_scatter x1 -> x0, waiting for transfers between devices: 98 us -> none  [body(): lax.psum_scatter(block_terms.astype(jnp.bfloat16), 'tensor', scatter_dime...]
    ppermute x0 -> x15, starting transfers between devices: none -> 83.9 us  [the longest x4 32.1 us: body(): swap = lambda v, axis: lax.ppermute(v, axis, [(0, 1), (1, 0)])]
    all_to_all x0 -> x1, blocking collectives: none -> 56.6 us  [body(): lax.all_to_all(partial.reshape(NX * NM, piece, width), ('x', 'm'), split_...]
    ppermute x0 -> x15, waiting for transfers between devices: none -> 38.1 us  [the longest x4 20.3 us: body(): swap = lambda v, axis: lax.ppermute(v, axis, [(0, 1), (1, 0)])]
    dot_general x3 -> x0, matrix products: 15.9 us -> none  [the longest x1 9.25 us: body(): lax.dot_general(grad_basis, lax.all_gather(out_grads, 'dp', axis=0, tiled...]
    pallas_call x0 -> x3, Pallas kernels: none -> 12.3 us  [the longest x2 7.79 us: block_sums(): pl.pallas_call(block_kernel, out_shape=(shape, shape), in_specs=[SMEM] +...]
    unnamed x8 -> x26, local copies, waits for them, and re-layouts: 1.16 us -> 8.44 us
  transfers between devices with their start and end apart: 4 -> 17, of which waited for: 4 -> 8; matrix products, arithmetic and copies ran while one was open for 0% -> 1% of each run, Pallas kernels for 0% -> 1%
where the time goes in v1:
time: 317 us
  waiting for transfers between devices  138 us (44%)
  starting transfers between devices  84 us (26%)
  blocking collectives  56.6 us (18%)
  between operations  14.3 us (5%)
  Pallas kernels  12.3 us (4%)
  local copies, waits for them, and re-layouts  8.44 us (3%)
    all_to_all x1, blocking collectives, body(): lax.all_to_all(partial.reshape(NX * NM, piece, width), ('x', 'm'), split_...  56.6 us
    all_gather x1, waiting for transfers between devices, body(): all_acts = lax.all_gather(both, ('y', 'x'), axis=0, tiled=False)  56.1 us
    all_gather x1, waiting for transfers between devices, body(): lax.all_gather(own, ('m', 'p'), axis=0, tiled=False)  43.6 us
    ppermute x4, starting transfers between devices, body(): swap = lambda v, axis: lax.ppermute(v, axis, [(0, 1), (1, 0)])  32.1 us
    ppermute x9, starting transfers between devices, from_rel(): lax.ppermute(value, axis, [((i + step) % size, i) for i in range(size)])  27.7 us
    ppermute x4, waiting for transfers between devices, body(): swap = lambda v, axis: lax.ppermute(v, axis, [(0, 1), (1, 0)])  20.3 us
    ppermute x1, starting transfers between devices, body(): other_half = lax.ppermute(out_grads, 'h', [(0, 1), (1, 0)])  15.4 us
    ppermute x9, waiting for transfers between devices, from_rel(): lax.ppermute(value, axis, [((i + step) % size, i) for i in range(size)])  11 us
  transfers between devices with their start and end apart: 17, of which 8 were waited for; matrix products, arithmetic and copies ran while one was open for 1% of the time, Pallas kernels for 1%

profile of v1, /device:TPU:1, one launch (start us, length us, event | category | flops | bytes accessed | tf_op | source)
XLA Modules:
  0.0 316.6 jit_solution(8340974557325206664)
XLA Ops:
  7.2 0.0 copy-start
  7.2 0.0 all-gather.5.cloned.1.call-start
  7.2 5.6 %collective-permute-start = (bf16[128,896]{1,0:T(8,128)(2,1)}, bf16[128,896]{1,0:T(8,128)(2,1)S(1)}, u32[]{:S(2)}, u32[]{:S(2)}) collective-permute-start(bf16[128,896]{1,0:T(8,128)(2,1)} %refs_0_.3), channel_id=1, source_target_pairs={{128,0},{256,128},{384,256},{0,384},{129,1},{257,129},{385,257},{1... | collective-permute-start | bytes 688136 | tf_op jit(solution)/shard_map/ppermute | solution.py:24
  12.8 4.4 %collective-permute-start.7 = (bf16[448,896]{1,0:T(8,128)(2,1)}, bf16[448,896]{1,0:T(8,128)(2,1)S(1)}, u32[]{:S(2)}, u32[]{:S(2)}) collective-permute-start(bf16[448,896]{1,0:T(8,128)(2,1)} %refs_8_.3), channel_id=1, source_target_pairs={{16,0},{32,16},{48,32},{0,48},{17,1},{33,17},{49,33},{1,49},{18,2}... | collective-permute-start | bytes 2408456 | tf_op jit(solution)/shard_map/ppermute | solution.py:24
  17.2 2.4 collective-permute-start.8
  19.7 2.5 collective-permute-start.9
  22.2 2.3 collective-permute-start.1
  24.5 0.0 collective-permute-done.refs_1_
  24.5 15.4 %collective-permute-start.3 = (bf16[128,896]{1,0:T(8,128)(2,1)}, bf16[128,896]{1,0:T(8,128)(2,1)}, u32[]{:S(2)}, u32[]{:S(2)}) collective-permute-start(bf16[128,896]{1,0:T(8,128)(2,1)} %refs_0_.3), channel_id=1, source_target_pairs={{0,64},{64,0},{1,65},{65,1},{2,66},{66,2},{3,67},{67,3},{4,68},{68... | collective-permute-start | bytes 688136 | tf_op jit(solution)/shard_map/ppermute | solution.py:121
  39.9 0.0 collective-permute-done.1.refs_2_
  39.9 2.6 collective-permute-start.2
  42.6 1.5 collective-permute-done.3.refs_4_
  44.1 2.7 collective-permute-start.4
  46.8 1.8 collective-permute-done.2.refs_3_
  48.5 0.7 copy-done.7
  49.2 3.3 %collective-permute-start.5 = (bf16[128,896]{1,0:T(8,128)(2,1)}, bf16[128,896]{1,0:T(8,128)(2,1)}, u32[]{:S(2)}, u32[]{:S(2)}) collective-permute-start(bf16[128,896]{1,0:T(8,128)(2,1)} %collective-permute-done.3.refs_4_), channel_id=1, source_target_pairs={{256,0},{384,128},{0,256},{128,384},{257,1},{385,129},{1,257},{129... | collective-permute-start | bytes 688136 | tf_op jit(solution)/shard_map/ppermute | solution.py:24
  52.5 0.0 collective-permute-done.4.refs_5_
  52.5 0.0 copy-start.9
  52.6 0.7 copy-done.9
  53.2 1.9 collective-permute-start.6
  55.2 0.1 add_add_fusion
  55.2 2.6 collective-permute-done.5.refs_6_
  57.8 6.7 %collective-permute-done.6.refs_7_ = bf16[128,896]{1,0:T(8,128)(2,1)} collective-permute-done((bf16[128,896]{1,0:T(8,128)(2,1)}, bf16[128,896]{1,0:T(8,128)(2,1)}, u32[]{:S(2)}, u32[]{:S(2)}) %collective-permute-start.6) | collective-permute-done | bytes 229408 | tf_op jit(solution)/shard_map/ppermute | solution.py:24
  64.5 0.0 collective-permute-done.7.refs_9_
  64.5 0.0 collective-permute-done.8.refs_10_
  64.5 0.0 collective-permute-done.9.refs_11_
  64.5 0.0 copy-start.3
  64.5 1.1 copy-done.3
  65.6 0.9 copy-done.5
  66.6 0.9 copy-done.8
  67.5 0.9 copy-done.10
  68.4 3.9 %block_sums.3 = (bf16[4,448,256]{2,1,0:T(8,128)(2,1)S(1)}, bf16[4,448,256]{2,1,0:T(8,128)(2,1)S(1)}) custom-call(s32[3]{0:T(128)S(1)} %get-tuple-element.11.where_ref, bf16[128,896]{1,0:T(8,128)(2,1)S(1)} %copy-done.5, bf16[128,896]{1,0:T(8,128)(2,1)S(1)} %collective-permute-done.refs_1_, bf16[128,896]{1,0:T(8,128)(2,1)S(1)} %collective-permute-done.1.refs_2_, ...), custom_call_target="tpu_custom_call" | custom-call | flops 1644167168 | bytes 9437184 | tf_op jit(solution)/shard_map/block_sums/pallas_call | solution.py:58
  72.4 4.4 %collective-permute-start.11 = (bf16[4,448,256]{2,1,0:T(8,128)(2,1)S(1)}, bf16[4,448,256]{2,1,0:T(8,128)(2,1)S(1)}, u32[]{:S(2)}, u32[]{:S(2)}) collective-permute-start(bf16[4,448,256]{2,1,0:T(8,128)(2,1)S(1)} %get-tuple-element.9), channel_id=1, source_target_pairs={{0,1},{1,0},{2,3},{3,2},{4,5},{5,4},{6,7},{7,6},{8,9},{9,8},{10,11... | collective-permute-start | bytes 2752520 | tf_op jit(solution)/shard_map/ppermute | solution.py:133
  76.8 1.9 collective-permute-start.10
  78.8 0.0 copy-done.4
  78.8 0.0 copy-done.6
  78.8 0.0 copy-done.11
  78.8 3.9 %block_sums.2 = (bf16[4,448,256]{2,1,0:T(8,128)(2,1)S(1)}, bf16[4,448,256]{2,1,0:T(8,128)(2,1)S(1)}) custom-call(s32[3]{0:T(128)S(1)} %get-tuple-element.10.where_ref, bf16[128,896]{1,0:T(8,128)(2,1)S(1)} %copy-done.6, bf16[128,896]{1,0:T(8,128)(2,1)S(1)} %collective-permute-done.refs_1_, bf16[128,896]{1,0:T(8,128)(2,1)S(1)} %collective-permute-done.1.refs_2_, ...), custom_call_target="tpu_custom_call" | custom-call | flops 1644167168 | bytes 9437184 | tf_op jit(solution)/shard_map/block_sums/pallas_call | solution.py:58
  82.7 0.0 collective-permute-done.11
  82.7 0.3 add_convert_fusion.1
  82.9 17.5 %collective-permute-start.12 = (bf16[4,448,256]{2,1,0:T(8,128)(2,1)S(1)}, bf16[4,448,256]{2,1,0:T(8,128)(2,1)S(1)}, u32[]{:S(2)}, u32[]{:S(2)}) collective-permute-start(bf16[4,448,256]{2,1,0:T(8,128)(2,1)S(1)} %add_convert_fusion.1), channel_id=1, source_target_pairs={{0,2},{2,0},{1,3},{3,1},{4,6},{6,4},{5,7},{7,5},{8,10},{10,8},{9,1... | collective-permute-start | bytes 2752520 | tf_op jit(solution)/shard_map/ppermute | solution.py:133
  100.5 0.0 collective-permute-done.10
  100.5 20.3 %collective-permute-done.12 = bf16[4,448,256]{2,1,0:T(8,128)(2,1)S(1)} collective-permute-done((bf16[4,448,256]{2,1,0:T(8,128)(2,1)S(1)}, bf16[4,448,256]{2,1,0:T(8,128)(2,1)S(1)}, u32[]{:S(2)}, u32[]{:S(2)}) %collective-permute-start.12) | collective-permute-done | bytes 917536 | tf_op jit(solution)/shard_map/ppermute | solution.py:133
  120.8 0.4 add_convert_fusion
  121.1 0.0 copy-start.12
  121.1 56.6 %all_to_all.5 = bf16[16,112,256]{2,1,0:T(8,128)(2,1)S(1)} all-to-all(bf16[16,112,256]{2,1,0:T(8,128)(2,1)S(1)} %bitcast.16), channel_id=1, replica_groups=mesh['y'=4,'h'=2,'x'=4,'m'=4,'p'=2,'c'=2] {'x','m'}, dimensions={0} | all-to-all | bytes 1835008 | tf_op jit(solution)/shard_map/all_to_all | solution.py:142
  177.7 0.8 add_convert_fusion.2
  178.5 0.0 all-gather.5.cloned.1.call-update
  178.5 0.0 all-gather.7.cloned.1.call-start
  178.6 0.0 copy-done
  178.6 0.0 copy-done.12
  178.6 0.8 convolution_convert_fusion
  179.5 8.7 %collective-permute-start.14 = (bf16[128,256]{1,0:T(8,128)(2,1)S(1)}, bf16[128,256]{1,0:T(8,128)(2,1)S(1)}, u32[]{:S(2)}, u32[]{:S(2)}) collective-permute-start(bf16[128,256]{1,0:T(8,128)(2,1)S(1)} %convolution_convert_fusion), channel_id=1, source_target_pairs={{0,64},{64,0},{1,65},{65,1},{2,66},{66,2},{3,67},{67,3},{4,68},{68... | collective-permute-start | bytes 196616 | tf_op jit(solution)/shard_map/ppermute | solution.py:129
  188.1 5.3 %collective-permute-done.14 = bf16[128,256]{1,0:T(8,128)(2,1)S(1)} collective-permute-done((bf16[128,256]{1,0:T(8,128)(2,1)S(1)}, bf16[128,256]{1,0:T(8,128)(2,1)S(1)}, u32[]{:S(2)}, u32[]{:S(2)}) %collective-permute-start.14) | collective-permute-done | bytes 65568 | tf_op jit(solution)/shard_map/ppermute | solution.py:129
  193.4 0.7 pad_maximum_fusion
  194.1 0.0 all-gather.7.cloned.1.call-update
  194.1 43.6 %all-gather.5.cloned.1.call-done = bf16[32,1,112,256]{3,2,1,0:T(8,128)(2,1)} async-done(((bf16[4,1,112,256]{3,2,1,0:T(8,128)(2,1)}), bf16[32,1,112,256]{3,2,1,0:T(8,128)(2,1)}) %all-gather.5.cloned.1.call-update) | async-done | bytes 1835024 | tf_op jit(solution)/shard_map/all_gather | solution.py:146
  237.7 8.2 %collective-permute-start.13 = (bf16[4,2,4,112,256]{4,3,2,1,0:T(8,128)(2,1)}, bf16[4,2,4,112,256]{4,3,2,1,0:T(8,128)(2,1)}, u32[]{:S(2)}, u32[]{:S(2)}) collective-permute-start(bf16[4,2,4,112,256]{4,3,2,1,0:T(8,128)(2,1)} %bitcast.14), channel_id=1, source_target_pairs={{0,1},{1,0},{2,3},{3,2},{4,5},{5,4},{6,7},{7,6},{8,9},{9,8},{10,11... | collective-permute-start | bytes 5505032 | tf_op jit(solution)/shard_map/ppermute | solution.py:133
  246.0 0.1 pad_add_fusion.where_ref
  246.0 56.1 %all-gather.7.cloned.1.call-done = bf16[32,128,256]{2,1,0:T(8,128)(2,1)} async-done(((bf16[2,128,256]{2,1,0:T(8,128)(2,1)}), bf16[32,128,256]{2,1,0:T(8,128)(2,1)}) %all-gather.7.cloned.1.call-update) | async-done | bytes 2097168 | tf_op jit(solution)/shard_map/all_gather | solution.py:130
  302.1 0.0 collective-permute-done.13.mate_ref
  302.1 1.6 copy-done.1
  303.7 1.5 copy-done.2
  305.2 4.5 %final_products.1 = (f32[448,256]{1,0:T(8,128)}, f32[448,256]{1,0:T(8,128)}) custom-call(s32[2]{0:T(128)S(1)} %pad_add_fusion.where_ref, bf16[4,2,4,112,256]{4,3,2,1,0:T(8,128)(2,1)S(1)} %bitcast.15, bf16[4,2,4,112,256]{4,3,2,1,0:T(8,128)(2,1)} %collective-permute-done.13.mate_ref, bf16[4,4,2,128,256]{4,3,2,1,0:T(8,128)(2,1)S(1)} %bitcast.13), custom_call_target="tpu_custom_call" | custom-call | flops 1879048192 | bytes 7340032 | tf_op jit(solution)/shard_map/final_products/pallas_call | solution.py:101
  (9 shorter events, 0.0 us)
Async XLA Ops:
  7.2 171.4 %copy-start = (bf16[256,4096]{1,0:T(8,128)(2,1)S(1)}, bf16[256,4096]{1,0:T(8,128)(2,1)}, u32[]{:S(2)}) copy-start(bf16[256,4096]{1,0:T(8,128)(2,1)} %param.5) | copy-start | bytes 6291460
  7.2 230.5 %all-gather.5.cloned.1.call-start = ((), (), s32[]{:S(2)}) async-start(), calls=%async_computation.1 | async-start | bytes 2064384 | tf_op jit(solution)/shard_map/all_gather | solution.py:146
  7.2 17.2 %collective-permute-start = (bf16[128,896]{1,0:T(8,128)(2,1)}, bf16[128,896]{1,0:T(8,128)(2,1)S(1)}, u32[]{:S(2)}, u32[]{:S(2)}) collective-permute-start(bf16[128,896]{1,0:T(8,128)(2,1)} %refs_0_.3), channel_id=1, source_target_pairs={{128,0},{256,128},{384,256},{0,384},{129,1},{257,129},{385,257},{1... | collective-permute-start | bytes 688136 | tf_op jit(solution)/shard_map/ppermute | solution.py:24
  12.8 51.6 %collective-permute-start.7 = (bf16[448,896]{1,0:T(8,128)(2,1)}, bf16[448,896]{1,0:T(8,128)(2,1)S(1)}, u32[]{:S(2)}, u32[]{:S(2)}) collective-permute-start(bf16[448,896]{1,0:T(8,128)(2,1)} %refs_8_.3), channel_id=1, source_target_pairs={{16,0},{32,16},{48,32},{0,48},{17,1},{33,17},{49,33},{1,49},{18,2}... | collective-permute-start | bytes 2408456 | tf_op jit(solution)/shard_map/ppermute | solution.py:24
  17.2 47.2 %collective-permute-start.8 = (bf16[448,896]{1,0:T(8,128)(2,1)}, bf16[448,896]{1,0:T(8,128)(2,1)}, u32[]{:S(2)}, u32[]{:S(2)}) collective-permute-start(bf16[448,896]{1,0:T(8,128)(2,1)} %refs_8_.3), channel_id=1, source_target_pairs={{32,0},{48,16},{0,32},{16,48},{33,1},{49,17},{1,33},{17,49},{34,2}... | collective-permute-start | bytes 2408456 | tf_op jit(solution)/shard_map/ppermute | solution.py:24
  19.7 44.8 %collective-permute-start.9 = (bf16[448,896]{1,0:T(8,128)(2,1)}, bf16[448,896]{1,0:T(8,128)(2,1)}, u32[]{:S(2)}, u32[]{:S(2)}) collective-permute-start(bf16[448,896]{1,0:T(8,128)(2,1)} %refs_8_.3), channel_id=1, source_target_pairs={{48,0},{0,16},{16,32},{32,48},{49,1},{1,17},{17,33},{33,49},{50,2}... | collective-permute-start | bytes 2408456 | tf_op jit(solution)/shard_map/ppermute | solution.py:24
  22.2 17.7 %collective-permute-start.1 = (bf16[128,896]{1,0:T(8,128)(2,1)}, bf16[128,896]{1,0:T(8,128)(2,1)S(1)}, u32[]{:S(2)}, u32[]{:S(2)}) collective-permute-start(bf16[128,896]{1,0:T(8,128)(2,1)} %refs_0_.3), channel_id=1, source_target_pairs={{256,0},{384,128},{0,256},{128,384},{257,1},{385,129},{1,257},{129... | collective-permute-start | bytes 688136 | tf_op jit(solution)/shard_map/ppermute | solution.py:24
  24.5 19.6 %collective-permute-start.3 = (bf16[128,896]{1,0:T(8,128)(2,1)}, bf16[128,896]{1,0:T(8,128)(2,1)}, u32[]{:S(2)}, u32[]{:S(2)}) collective-permute-start(bf16[128,896]{1,0:T(8,128)(2,1)} %refs_0_.3), channel_id=1, source_target_pairs={{0,64},{64,0},{1,65},{65,1},{2,66},{66,2},{3,67},{67,3},{4,68},{68... | collective-permute-start | bytes 688136 | tf_op jit(solution)/shard_map/ppermute | solution.py:121
  39.9 8.6 %collective-permute-start.2 = (bf16[128,896]{1,0:T(8,128)(2,1)}, bf16[128,896]{1,0:T(8,128)(2,1)S(1)}, u32[]{:S(2)}, u32[]{:S(2)}) collective-permute-start(bf16[128,896]{1,0:T(8,128)(2,1)} %refs_0_.3), channel_id=1, source_target_pairs={{384,0},{0,128},{128,256},{256,384},{385,1},{1,129},{129,257},{257... | collective-permute-start | bytes 688136 | tf_op jit(solution)/shard_map/ppermute | solution.py:24
  44.1 8.5 %collective-permute-start.4 = (bf16[128,896]{1,0:T(8,128)(2,1)}, bf16[128,896]{1,0:T(8,128)(2,1)S(1)}, u32[]{:S(2)}, u32[]{:S(2)}) collective-permute-start(bf16[128,896]{1,0:T(8,128)(2,1)} %collective-permute-done.3.refs_4_), channel_id=1, source_target_pairs={{128,0},{256,128},{384,256},{0,384},{129,1},{257,129},{385,257},{1... | collective-permute-start | bytes 688136 | tf_op jit(solution)/shard_map/ppermute | solution.py:24
  48.5 0.7 copy-start.7
  49.2 8.6 %collective-permute-start.5 = (bf16[128,896]{1,0:T(8,128)(2,1)}, bf16[128,896]{1,0:T(8,128)(2,1)}, u32[]{:S(2)}, u32[]{:S(2)}) collective-permute-start(bf16[128,896]{1,0:T(8,128)(2,1)} %collective-permute-done.3.refs_4_), channel_id=1, source_target_pairs={{256,0},{384,128},{0,256},{128,384},{257,1},{385,129},{1,257},{129... | collective-permute-start | bytes 688136 | tf_op jit(solution)/shard_map/ppermute | solution.py:24
  52.5 0.7 copy-start.9
  53.2 11.2 %collective-permute-start.6 = (bf16[128,896]{1,0:T(8,128)(2,1)}, bf16[128,896]{1,0:T(8,128)(2,1)}, u32[]{:S(2)}, u32[]{:S(2)}) collective-permute-start(bf16[128,896]{1,0:T(8,128)(2,1)} %collective-permute-done.3.refs_4_), channel_id=1, source_target_pairs={{384,0},{0,128},{128,256},{256,384},{385,1},{1,129},{129,257},{257... | collective-permute-start | bytes 688136 | tf_op jit(solution)/shard_map/ppermute | solution.py:24
  64.5 1.1 copy-start.3
  65.6 0.9 copy-start.5
  66.6 0.9 copy-start.8
  67.5 0.9 copy-start.10
  68.4 10.3 %copy-start.4 = (bf16[448,896]{1,0:T(8,128)(2,1)S(1)}, bf16[448,896]{1,0:T(8,128)(2,1)}, u32[]{:S(2)}) copy-start(bf16[448,896]{1,0:T(8,128)(2,1)} %refs_8_.3) | copy-start | bytes 2408452
  68.4 10.3 %copy-start.6 = (bf16[128,896]{1,0:T(8,128)(2,1)S(1)}, bf16[128,896]{1,0:T(8,128)(2,1)}, u32[]{:S(2)}) copy-start(bf16[128,896]{1,0:T(8,128)(2,1)} %refs_0_.3) | copy-start | bytes 688132
  68.4 10.3 %copy-start.11 = (bf16[128,896]{1,0:T(8,128)(2,1)S(1)}, bf16[128,896]{1,0:T(8,128)(2,1)}, u32[]{:S(2)}) copy-start(bf16[128,896]{1,0:T(8,128)(2,1)} %copy-done.9) | copy-start | bytes 688132
  72.4 10.3 %collective-permute-start.11 = (bf16[4,448,256]{2,1,0:T(8,128)(2,1)S(1)}, bf16[4,448,256]{2,1,0:T(8,128)(2,1)S(1)}, u32[]{:S(2)}, u32[]{:S(2)}) collective-permute-start(bf16[4,448,256]{2,1,0:T(8,128)(2,1)S(1)} %get-tuple-element.9), channel_id=1, source_target_pairs={{0,1},{1,0},{2,3},{3,2},{4,5},{5,4},{6,7},{7,6},{8,9},{9,8},{10,11... | collective-permute-start | bytes 2752520 | tf_op jit(solution)/shard_map/ppermute | solution.py:133
  76.8 23.7 %collective-permute-start.10 = (bf16[4,448,256]{2,1,0:T(8,128)(2,1)S(1)}, bf16[4,448,256]{2,1,0:T(8,128)(2,1)S(1)}, u32[]{:S(2)}, u32[]{:S(2)}) collective-permute-start(bf16[4,448,256]{2,1,0:T(8,128)(2,1)S(1)} %get-tuple-element.7), channel_id=1, source_target_pairs={{0,1},{1,0},{2,3},{3,2},{4,5},{5,4},{6,7},{7,6},{8,9},{9,8},{10,11... | collective-permute-start | bytes 2752520 | tf_op jit(solution)/shard_map/ppermute | solution.py:133
  82.9 37.8 %collective-permute-start.12 = (bf16[4,448,256]{2,1,0:T(8,128)(2,1)S(1)}, bf16[4,448,256]{2,1,0:T(8,128)(2,1)S(1)}, u32[]{:S(2)}, u32[]{:S(2)}) collective-permute-start(bf16[4,448,256]{2,1,0:T(8,128)(2,1)S(1)} %add_convert_fusion.1), channel_id=1, source_target_pairs={{0,2},{2,0},{1,3},{3,1},{4,6},{6,4},{5,7},{7,5},{8,10},{10,8},{9,1... | collective-permute-start | bytes 2752520 | tf_op jit(solution)/shard_map/ppermute | solution.py:133
  121.1 57.5 %copy-start.12 = (bf16[128,4096]{1,0:T(8,128)(2,1)S(1)}, bf16[128,4096]{1,0:T(8,128)(2,1)}, u32[]{:S(2)}) copy-start(bf16[128,4096]{1,0:T(8,128)(2,1)} %param.4) | copy-start | bytes 3145732
  178.5 123.6 %all-gather.7.cloned.1.call-start = ((), (), s32[]{:S(2)}) async-start(), calls=%async_computation.2 | async-start | bytes 2228224 | tf_op jit(solution)/shard_map/all_gather | solution.py:130
  179.5 14.0 %collective-permute-start.14 = (bf16[128,256]{1,0:T(8,128)(2,1)S(1)}, bf16[128,256]{1,0:T(8,128)(2,1)S(1)}, u32[]{:S(2)}, u32[]{:S(2)}) collective-permute-start(bf16[128,256]{1,0:T(8,128)(2,1)S(1)} %convolution_convert_fusion), channel_id=1, source_target_pairs={{0,64},{64,0},{1,65},{65,1},{2,66},{66,2},{3,67},{67,3},{4,68},{68... | collective-permute-start | bytes 196616 | tf_op jit(solution)/shard_map/ppermute | solution.py:129
  237.7 64.4 %collective-permute-start.13 = (bf16[4,2,4,112,256]{4,3,2,1,0:T(8,128)(2,1)}, bf16[4,2,4,112,256]{4,3,2,1,0:T(8,128)(2,1)}, u32[]{:S(2)}, u32[]{:S(2)}) collective-permute-start(bf16[4,2,4,112,256]{4,3,2,1,0:T(8,128)(2,1)} %bitcast.14), channel_id=1, source_target_pairs={{0,1},{1,0},{2,3},{3,2},{4,5},{5,4},{6,7},{7,6},{8,9},{9,8},{10,11... | collective-permute-start | bytes 5505032 | tf_op jit(solution)/shard_map/ppermute | solution.py:133
  302.1 1.6 copy-start.1
  303.7 1.5 copy-start.2
Sparse Core Ops, SparseCore 0:
  178.7 59.0 all-gather.4
  241.3 60.7 all-gather.6

commit v2 on v1

v2 whole, which is shorter than its diff:
```python
import jax
import jax.numpy as jnp
from jax import lax
from jax.experimental import pallas as pl
from jax.experimental.pallas import tpu as pltpu
from jax.sharding import Mesh, PartitionSpec as P

F32 = jnp.float32
BF16 = jnp.bfloat16
NX, NY, NM = 4, 4, 4
VMEM = pl.BlockSpec(memory_space=pltpu.VMEM)
SMEM = pl.BlockSpec(memory_space=pltpu.SMEM)


def params():
    return pltpu.CompilerParams(vmem_limit_bytes=24 * 1024 * 1024)


def cost(flops, nbytes):
    return pl.CostEstimate(flops=flops, bytes_accessed=nbytes, transcendentals=0)


def from_rel(value, axis, step, size):
    return lax.ppermute(value, axis, [((i + step) % size, i) for i in range(size)])


def block_kernel(where_ref, *refs):
    tokens, basis_ref, out_ref = refs[:NY], refs[NY], refs[NY + 1]
    half = where_ref[1]
    rows = tokens[0].shape[1]
    piece = basis_ref.shape[1] // NM
    for j in range(NX):
        for parity in range(2):
            right = jnp.concatenate([tokens[2 * parity + n][half] for n in range(2)], axis=0)
            sums = lax.dot_general(
                basis_ref[j], right, (((1,), (1,)), ((), ())), preferred_element_type=F32
            ).astype(BF16)
            for m in range(NM):
                out_ref[2 * m + parity, j] = sums[m * piece : (m + 1) * piece]


def block_sums(where, tokens, basis):
    _, rows, depth = tokens[0].shape
    crows = basis.shape[1]
    return pl.pallas_call(
        block_kernel,
        out_shape=jax.ShapeDtypeStruct((2 * NM, NX, crows // NM, 2 * rows), BF16),
        in_specs=[SMEM] + [VMEM] * (NY + 1),
        out_specs=VMEM,
        compiler_params=params(),
        cost_estimate=cost(2 * NX * crows * NY * rows * depth, 9 * 2**20),
        name="block_sums",
    )(where, *tokens, basis)


def final_kernel(where_ref, mine_ref, mate_ref, *refs):
    acts, (grad_ref, scale_ref) = refs[:NX], refs[NX:]
    here, core = where_ref[0], where_ref[1]
    pairs, _, _, piece, width = mine_ref.shape
    rows = acts[0].shape[2]
    first = True
    for side, ref in ((0, mine_ref), (1, mate_ref)):
        half = lax.rem(core + side, 2)
        for j in range(NX):
            home = lax.rem(here + j, NX)
            for parity in range(2):
                g = ref[:, parity, home].reshape(pairs * piece, width)
                a = acts[j][2 * parity : 2 * parity + 2, half].reshape(2 * rows, -1)
                gw, aw = g.astype(F32), a.astype(F32)
                g2, a2 = (gw * gw).astype(BF16), (aw * aw).astype(BF16)
                p1 = jnp.dot(g, a, preferred_element_type=F32)
                p2 = jnp.dot(g2, a2, preferred_element_type=F32)
                if first:
                    grad_ref[...] = p1
                    scale_ref[...] = p2
                    first = False
                else:
                    grad_ref[...] += p1
                    scale_ref[...] += p2
    scale_ref[...] = scale_ref[...] / (2 * NY * NX * rows)


def final(where, mine, mate, acts):
    pairs, _, _, piece, width = mine.shape
    shape = jax.ShapeDtypeStruct((pairs * piece, acts[0].shape[-1]), F32)
    return pl.pallas_call(
        final_kernel,
        out_shape=(shape, shape),
        in_specs=[SMEM] + [VMEM] * (2 + NX),
        out_specs=(VMEM, VMEM),
        compiler_params=params(),
        cost_estimate=cost(4 * 448 * 4096 * 256, 7 * 2**20),
        name="final_products",
    )(where, mine, mate, *acts)


def added(*values):
    total = values[0].astype(F32)
    for v in values[1:]:
        total = total + v.astype(F32)
    return total.astype(BF16)


def body(activations, act_basis, out_grads, grad_basis):
    x, core = lax.axis_index("x"), lax.axis_index("c")
    swap = lambda v, axis: lax.ppermute(v, axis, [(0, 1), (1, 0)])
    basis = lax.all_gather(grad_basis, "x", axis=0, tiled=False)
    halves = jnp.stack([out_grads, swap(out_grads, "h")])
    tokens = [halves] + [from_rel(halves, "y", j, NY) for j in (1, 2, 3)]

    send = block_sums(jnp.stack([x, 1 - core]).astype(jnp.int32), tokens, basis)
    got = swap(send, "c")
    mine = block_sums(jnp.stack([x, core]).astype(jnp.int32), tokens, basis)
    partial = added(mine, got)

    activations, partial = lax.optimization_barrier((activations, partial))
    acts = lax.dot_general(
        activations, act_basis, (((1,), (1,)), ((), ())), preferred_element_type=F32
    ).astype(BF16)
    both = jnp.stack([acts, swap(acts, "h")])
    column = jnp.stack([both] + [from_rel(both, "y", j, NY) for j in (1, 2, 3)])
    all_acts = [column] + [from_rel(column, "x", j, NX) for j in (1, 2, 3)]

    own = lax.psum_scatter(partial, ("m", "p"), scatter_dimension=0, tiled=False)
    own, all_acts = lax.optimization_barrier((own, all_acts))
    own = lax.all_to_all(own, "x", split_axis=0, concat_axis=0, tiled=True)
    mine = lax.all_gather(own, ("m", "p"), axis=0, tiled=False).reshape(NM, 2, *own.shape)
    mate = swap(mine, "c")
    return final(jnp.stack([x, core]).astype(jnp.int32), mine, mate, all_acts)


def solution(mesh):
    fine = Mesh(mesh.devices.reshape(NY, 2, NX, NM, 2, 2), ("y", "h", "x", "m", "p", "c"))
    dp, tensor = ("y", "h", "x"), ("m", "p", "c")
    return jax.shard_map(
        body,
        mesh=fine,
        in_specs=(P(dp, None), P(tensor, None), P(dp, tensor), P(dp, tensor)),
        out_specs=(P(dp, tensor), P(dp, tensor)),
        check_vma=False,
    )
```

time: 317 us -> 252 us (0.79)
  blocking collectives: 56.6 us -> 10 us
  starting transfers between devices: 84 us -> 69.5 us
    all_gather x1, waiting for transfers between devices: 56.1 us -> 5.51 us  [body(): basis = lax.all_gather(grad_basis, 'x', axis=0, tiled=False)]
    all_to_all x1, blocking collectives: 56.6 us -> 10 us  [body(): own = lax.all_to_all(own, 'x', split_axis=0, concat_axis=0, tiled=True)]
    ppermute x9, waiting for transfers between devices: 11 us -> 39.9 us  [from_rel(): lax.ppermute(value, axis, [((i + step) % size, i) for i in range(size)])]
    ppermute x2 -> x0, starting transfers between devices: 24.1 us -> none  [the longest x1 15.4 us: body(): other_half = lax.ppermute(out_grads, 'h', [(0, 1), (1, 0)])]
    all_gather x1, waiting for transfers between devices: 43.6 us -> 64.7 us  [body(): lax.all_gather(own, ('m', 'p'), axis=0, tiled=False)]
    reduce_scatter x0 -> x1, waiting for transfers between devices: none -> 13.4 us  [body(): lax.psum_scatter(partial, ('m', 'p'), scatter_dimension=0, tiled=False)]
    ppermute x4, waiting for transfers between devices: 20.3 us -> 11.3 us  [body(): swap = lambda v, axis: lax.ppermute(v, axis, [(0, 1), (1, 0)])]
    ppermute x4, starting transfers between devices: 32.1 us -> 39.1 us  [body(): swap = lambda v, axis: lax.ppermute(v, axis, [(0, 1), (1, 0)])]
  transfers between devices with their start and end apart: 17 -> 16, of which waited for: 8 -> 15; matrix products, arithmetic and copies ran while one was open for 1% -> 1% of each run, Pallas kernels for 1% -> 1%
where the time goes in v2:
time: 252 us; the launch traced here: 251 us
  waiting for transfers between devices  136 us (54%)
  starting transfers between devices  69.5 us (28%)
  between operations  13.9 us (6%)
  blocking collectives  10 us (4%)
  Pallas kernels  9.93 us (4%)
  local copies, waits for them, and re-layouts  8.25 us (3%)
  other arithmetic  3.01 us (1%)
    all_gather x1, waiting for transfers between devices, body(): lax.all_gather(own, ('m', 'p'), axis=0, tiled=False)  64.7 us
    ppermute x9, waiting for transfers between devices, from_rel(): lax.ppermute(value, axis, [((i + step) % size, i) for i in range(size)])  39.9 us
    ppermute x4, starting transfers between devices, body(): swap = lambda v, axis: lax.ppermute(v, axis, [(0, 1), (1, 0)])  39.1 us
    ppermute x9, starting transfers between devices, from_rel(): lax.ppermute(value, axis, [((i + step) % size, i) for i in range(size)])  30.3 us
    reduce_scatter x1, waiting for transfers between devices, body(): lax.psum_scatter(partial, ('m', 'p'), scatter_dimension=0, tiled=False)  13.4 us
    ppermute x4, waiting for transfers between devices, body(): swap = lambda v, axis: lax.ppermute(v, axis, [(0, 1), (1, 0)])  11.3 us
    all_to_all x1, blocking collectives, body(): own = lax.all_to_all(own, 'x', split_axis=0, concat_axis=0, tiled=True)  10 us
    unnamed x18, local copies, waits for them, and re-layouts  8.25 us
  transfers between devices with their start and end apart: 16, of which 15 were waited for; matrix products, arithmetic and copies ran while one was open for 1% of the time, Pallas kernels for 1%

profile of v2, /device:TPU:1, one launch (start us, length us, event | category | flops | bytes accessed | tf_op | source)
XLA Modules:
  0.0 251.0 jit_solution(551930912475221688)
XLA Ops:
  7.2 0.0 copy-start
  7.2 0.0 all-gather.5.cloned.1.call-start
  7.2 0.7 all-gather.5.cloned.1.call-update
  7.9 0.0 reduce-scatter.2.cloned.1.call-start
  8.0 16.3 %collective-permute-start = (bf16[128,896]{1,0:T(8,128)(2,1)}, bf16[128,896]{1,0:T(8,128)(2,1)S(1)}, u32[]{:S(2)}, u32[]{:S(2)}) collective-permute-start(bf16[128,896]{1,0:T(8,128)(2,1)} %param.6), channel_id=1, source_target_pairs={{0,64},{64,0},{1,65},{65,1},{2,66},{66,2},{3,67},{67,3},{4,68},{68... | collective-permute-start | bytes 688136 | tf_op jit(solution)/shard_map/ppermute | solution.py:106
  24.2 5.3 %collective-permute-done = bf16[128,896]{1,0:T(8,128)(2,1)S(1)} collective-permute-done((bf16[128,896]{1,0:T(8,128)(2,1)}, bf16[128,896]{1,0:T(8,128)(2,1)S(1)}, u32[]{:S(2)}, u32[]{:S(2)}) %collective-permute-start) | collective-permute-done | bytes 229408 | tf_op jit(solution)/shard_map/ppermute | solution.py:106
  29.6 1.0 pad_maximum_fusion.1.refs_0_
  30.6 3.4 %collective-permute-start.3 = (bf16[2,128,896]{2,1,0:T(8,128)(2,1)S(1)}, bf16[2,128,896]{2,1,0:T(8,128)(2,1)S(1)}, u32[]{:S(2)}, u32[]{:S(2)}) collective-permute-start(bf16[2,128,896]{2,1,0:T(8,128)(2,1)S(1)} %pad_maximum_fusion.1.refs_0_), channel_id=1, source_target_pairs={{384,0},{0,128},{128,256},{256,384},{385,1},{1,129},{129,257},{257... | collective-permute-start | bytes 1376264 | tf_op jit(solution)/shard_map/ppermute | solution.py:24
  34.0 4.5 %collective-permute-start.2 = (bf16[2,128,896]{2,1,0:T(8,128)(2,1)S(1)}, bf16[2,128,896]{2,1,0:T(8,128)(2,1)S(1)}, u32[]{:S(2)}, u32[]{:S(2)}) collective-permute-start(bf16[2,128,896]{2,1,0:T(8,128)(2,1)S(1)} %pad_maximum_fusion.1.refs_0_), channel_id=1, source_target_pairs={{256,0},{384,128},{0,256},{128,384},{257,1},{385,129},{1,257},{129... | collective-permute-start | bytes 1376264 | tf_op jit(solution)/shard_map/ppermute | solution.py:24
  38.5 3.0 %collective-permute-start.1 = (bf16[2,128,896]{2,1,0:T(8,128)(2,1)S(1)}, bf16[2,128,896]{2,1,0:T(8,128)(2,1)}, u32[]{:S(2)}, u32[]{:S(2)}) collective-permute-start(bf16[2,128,896]{2,1,0:T(8,128)(2,1)S(1)} %pad_maximum_fusion.1.refs_0_), channel_id=1, source_target_pairs={{128,0},{256,128},{384,256},{0,384},{129,1},{257,129},{385,257},{1... | collective-permute-start | bytes 1376264 | tf_op jit(solution)/shard_map/ppermute | solution.py:24
  41.5 0.1 pad_add_fusion.1.where_ref
  41.6 2.3 collective-permute-done.3.refs_3_
  43.9 11.5 %collective-permute-done.2.refs_2_ = bf16[2,128,896]{2,1,0:T(8,128)(2,1)S(1)} collective-permute-done((bf16[2,128,896]{2,1,0:T(8,128)(2,1)S(1)}, bf16[2,128,896]{2,1,0:T(8,128)(2,1)S(1)}, u32[]{:S(2)}, u32[]{:S(2)}) %collective-permute-start.2) | collective-permute-done | bytes 458784 | tf_op jit(solution)/shard_map/ppermute | solution.py:24
  55.4 2.3 collective-permute-done.1.refs_1_
  57.7 5.5 %all-gather.5.cloned.1.call-done = bf16[1792,896]{1,0:T(8,128)(2,1)} async-done(((bf16[448,896]{1,0:T(8,128)(2,1)}), bf16[1792,896]{1,0:T(8,128)(2,1)}) %all-gather.5.cloned.1.call-update) | async-done | bytes 3211280 | tf_op jit(solution)/shard_map/all_gather | solution.py:107
  63.2 0.0 copy-start.1
  63.2 1.9 copy-done.1
  65.1 0.0 copy-start.2
  65.1 3.3 %block_sums.3 = bf16[8,4,112,256]{3,2,1,0:T(8,128)(2,1)S(1)} custom-call(s32[2]{0:T(128)S(1)} %pad_add_fusion.1.where_ref, bf16[2,128,896]{2,1,0:T(8,128)(2,1)S(1)} %pad_maximum_fusion.1.refs_0_, bf16[2,128,896]{2,1,0:T(8,128)(2,1)} %collective-permute-done.1.refs_1_, bf16[2,128,896]{2,1,0:T(8,128)(2,1)S(1)} %collective-permute-done.2.refs_2_, ...), custom_call_target="tpu_custom_call" | custom-call | flops 1644167168 | bytes 9437184 | tf_op jit(solution)/shard_map/block_sums/pallas_call | solution.py:45
  68.4 2.6 %collective-permute-start.4 = (bf16[8,4,112,256]{3,2,1,0:T(8,128)(2,1)S(1)}, bf16[8,4,112,256]{3,2,1,0:T(8,128)(2,1)S(1)}, u32[]{:S(2)}, u32[]{:S(2)}) collective-permute-start(bf16[8,4,112,256]{3,2,1,0:T(8,128)(2,1)S(1)} %block_sums.3), channel_id=1, source_target_pairs={{0,1},{1,0},{2,3},{3,2},{4,5},{5,4},{6,7},{7,6},{8,9},{9,8},{10,11... | collective-permute-start | bytes 5505032 | tf_op jit(solution)/shard_map/ppermute | solution.py:106
  71.0 0.1 pad_add_fusion.where_ref
  71.1 0.0 copy-done.2
  71.1 3.1 %block_sums.2 = bf16[8,4,112,256]{3,2,1,0:T(8,128)(2,1)S(1)} custom-call(s32[2]{0:T(128)S(1)} %pad_add_fusion.where_ref, bf16[2,128,896]{2,1,0:T(8,128)(2,1)S(1)} %pad_maximum_fusion.1.refs_0_, bf16[2,128,896]{2,1,0:T(8,128)(2,1)} %collective-permute-done.1.refs_1_, bf16[2,128,896]{2,1,0:T(8,128)(2,1)S(1)} %collective-permute-done.2.refs_2_, ...), custom_call_target="tpu_custom_call" | custom-call | flops 1644167168 | bytes 9437184 | tf_op jit(solution)/shard_map/block_sums/pallas_call | solution.py:45
  74.2 0.2 collective-permute-done.4
  74.4 1.8 add_convert_fusion
  76.1 0.0 copy-start.8
  76.2 0.0 reduce-scatter.2.cloned.1.call-update
  76.2 0.0 all-gather.7.cloned.1.call-start
  76.2 0.0 copy-done
  76.2 1.1 copy-done.8
  77.4 0.9 convolution_convert_fusion
  78.3 12.5 %collective-permute-start.5 = (bf16[128,256]{1,0:T(8,128)(2,1)S(1)}, bf16[128,256]{1,0:T(8,128)(2,1)S(1)}, u32[]{:S(2)}, u32[]{:S(2)}) collective-permute-start(bf16[128,256]{1,0:T(8,128)(2,1)S(1)} %convolution_convert_fusion), channel_id=1, source_target_pairs={{0,64},{64,0},{1,65},{65,1},{2,66},{66,2},{3,67},{67,3},{4,68},{68... | collective-permute-start | bytes 196616 | tf_op jit(solution)/shard_map/ppermute | solution.py:106
  90.8 2.1 collective-permute-done.5
  93.0 4.6 %collective-permute-start.7 = (bf16[2,128,256]{2,1,0:T(8,128)(2,1)S(1)}, bf16[2,128,256]{2,1,0:T(8,128)(2,1)S(1)}, u32[]{:S(2)}, u32[]{:S(2)}) collective-permute-start(bf16[2,128,256]{2,1,0:T(8,128)(2,1)S(1)} %get-tuple-element.17), channel_id=1, source_target_pairs={{256,0},{384,128},{0,256},{128,384},{257,1},{385,129},{1,257},{129... | collective-permute-start | bytes 393224 | tf_op jit(solution)/shard_map/ppermute | solution.py:24
  97.6 2.8 %collective-permute-start.6 = (bf16[2,128,256]{2,1,0:T(8,128)(2,1)S(1)}, bf16[2,128,256]{2,1,0:T(8,128)(2,1)S(1)}, u32[]{:S(2)}, u32[]{:S(2)}) collective-permute-start(bf16[2,128,256]{2,1,0:T(8,128)(2,1)S(1)} %get-tuple-element.17), channel_id=1, source_target_pairs={{128,0},{256,128},{384,256},{0,384},{129,1},{257,129},{385,257},{1... | collective-permute-start | bytes 393224 | tf_op jit(solution)/shard_map/ppermute | solution.py:24
  100.4 2.5 collective-permute-start.8
  102.9 0.0 collective-permute-done.7
  102.9 0.4 collective-permute-done.6
  103.3 4.0 %collective-permute-done.8 = bf16[2,128,256]{2,1,0:T(8,128)(2,1)S(1)} collective-permute-done((bf16[2,128,256]{2,1,0:T(8,128)(2,1)S(1)}, bf16[2,128,256]{2,1,0:T(8,128)(2,1)S(1)}, u32[]{:S(2)}, u32[]{:S(2)}) %collective-permute-start.8) | collective-permute-done | bytes 131104 | tf_op jit(solution)/shard_map/ppermute | solution.py:24
  107.3 0.1 pad_maximum_fusion.refs_0_
  107.4 2.3 collective-permute-start.11
  109.7 3.4 %collective-permute-start.10 = (bf16[4,2,128,256]{3,2,1,0:T(8,128)(2,1)S(1)}, bf16[4,2,128,256]{3,2,1,0:T(8,128)(2,1)S(1)}, u32[]{:S(2)}, u32[]{:S(2)}) collective-permute-start(bf16[4,2,128,256]{3,2,1,0:T(8,128)(2,1)S(1)} %pad_maximum_fusion.refs_0_), channel_id=1, source_target_pairs={{32,0},{48,16},{0,32},{16,48},{33,1},{49,17},{1,33},{17,49},{34,2}... | collective-permute-start | bytes 1572872 | tf_op jit(solution)/shard_map/ppermute | solution.py:24
  113.1 3.7 %collective-permute-start.9 = (bf16[4,2,128,256]{3,2,1,0:T(8,128)(2,1)S(1)}, bf16[4,2,128,256]{3,2,1,0:T(8,128)(2,1)S(1)}, u32[]{:S(2)}, u32[]{:S(2)}) collective-permute-start(bf16[4,2,128,256]{3,2,1,0:T(8,128)(2,1)S(1)} %pad_maximum_fusion.refs_0_), channel_id=1, source_target_pairs={{16,0},{32,16},{48,32},{0,48},{17,1},{33,17},{49,33},{1,49},{18,2}... | collective-permute-start | bytes 1572872 | tf_op jit(solution)/shard_map/ppermute | solution.py:24
  116.9 5.2 %collective-permute-done.11.refs_3_ = bf16[4,2,128,256]{3,2,1,0:T(8,128)(2,1)S(1)} collective-permute-done((bf16[4,2,128,256]{3,2,1,0:T(8,128)(2,1)S(1)}, bf16[4,2,128,256]{3,2,1,0:T(8,128)(2,1)S(1)}, u32[]{:S(2)}, u32[]{:S(2)}) %collective-permute-start.11) | collective-permute-done | bytes 524320 | tf_op jit(solution)/shard_map/ppermute | solution.py:24
  122.1 9.9 %collective-permute-done.10.refs_2_ = bf16[4,2,128,256]{3,2,1,0:T(8,128)(2,1)S(1)} collective-permute-done((bf16[4,2,128,256]{3,2,1,0:T(8,128)(2,1)S(1)}, bf16[4,2,128,256]{3,2,1,0:T(8,128)(2,1)S(1)}, u32[]{:S(2)}, u32[]{:S(2)}) %collective-permute-start.10) | collective-permute-done | bytes 524320 | tf_op jit(solution)/shard_map/ppermute | solution.py:24
  131.9 0.0 copy-start.4
  131.9 0.8 copy-done.4
  132.7 4.3 %collective-permute-done.9.refs_1_ = bf16[4,2,128,256]{3,2,1,0:T(8,128)(2,1)S(1)} collective-permute-done((bf16[4,2,128,256]{3,2,1,0:T(8,128)(2,1)S(1)}, bf16[4,2,128,256]{3,2,1,0:T(8,128)(2,1)S(1)}, u32[]{:S(2)}, u32[]{:S(2)}) %collective-permute-start.9) | collective-permute-done | bytes 524320 | tf_op jit(solution)/shard_map/ppermute | solution.py:24
  137.1 0.0 copy-start.6
  137.1 0.8 copy-done.6
  137.9 13.4 %reduce-scatter.2.cloned.1.call-done = bf16[1,4,112,256]{3,2,1,0:T(8,128)(2,1)} async-done(((bf16[8,4,112,256]{3,2,1,0:T(8,128)(2,1)}), bf16[1,4,112,256]{3,2,1,0:T(8,128)(2,1)}) %reduce-scatter.2.cloned.1.call-update) | async-done | bytes 229392 | tf_op jit(solution)/shard_map/reduce_scatter | solution.py:124
  151.3 10.0 %all_to_all.5 = bf16[4,112,256]{2,1,0:T(8,128)(2,1)} all-to-all(bf16[4,112,256]{2,1,0:T(8,128)(2,1)} %bitcast.24), channel_id=1, replica_groups=mesh['y'=4,'h'=2,'x'=4,'m'=4,'p'=2,'c'=2] {'x'}, dimensions={0} | all-to-all | bytes 458752 | tf_op jit(solution)/shard_map/all_to_all | solution.py:126
  161.4 0.0 all-gather.7.cloned.1.call-update
  161.4 64.7 %all-gather.7.cloned.1.call-done = bf16[32,112,256]{2,1,0:T(8,128)(2,1)} async-done(((bf16[4,112,256]{2,1,0:T(8,128)(2,1)}), bf16[32,112,256]{2,1,0:T(8,128)(2,1)}) %all-gather.7.cloned.1.call-update) | async-done | bytes 1835024 | tf_op jit(solution)/shard_map/all_gather | solution.py:127
  226.1 7.7 %collective-permute-start.12 = (bf16[4,2,4,112,256]{4,3,2,1,0:T(8,128)(2,1)}, bf16[4,2,4,112,256]{4,3,2,1,0:T(8,128)(2,1)S(1)}, u32[]{:S(2)}, u32[]{:S(2)}) collective-permute-start(bf16[4,2,4,112,256]{4,3,2,1,0:T(8,128)(2,1)} %bitcast.19), channel_id=1, source_target_pairs={{0,1},{1,0},{2,3},{3,2},{4,5},{5,4},{6,7},{7,6},{8,9},{9,8},{10,11... | collective-permute-start | bytes 5505032 | tf_op jit(solution)/shard_map/ppermute | solution.py:106
  233.8 3.6 %collective-permute-done.12.mate_ref = bf16[4,2,4,112,256]{4,3,2,1,0:T(8,128)(2,1)S(1)} collective-permute-done((bf16[4,2,4,112,256]{4,3,2,1,0:T(8,128)(2,1)}, bf16[4,2,4,112,256]{4,3,2,1,0:T(8,128)(2,1)S(1)}, u32[]{:S(2)}, u32[]{:S(2)}) %collective-permute-start.12) | collective-permute-done | bytes 1835040 | tf_op jit(solution)/shard_map/ppermute | solution.py:106
  237.4 0.0 copy-start.3
  237.4 1.5 copy-done.3
  238.9 0.0 copy-start.5
  238.9 1.0 copy-done.5
  239.9 0.0 copy-start.7
  239.9 1.0 copy-done.7
  241.0 3.5 %final_products.1 = (f32[448,256]{1,0:T(8,128)}, f32[448,256]{1,0:T(8,128)}) custom-call(s32[2]{0:T(128)S(1)} %pad_add_fusion.where_ref, bf16[4,2,4,112,256]{4,3,2,1,0:T(8,128)(2,1)S(1)} %bitcast.20, bf16[4,2,4,112,256]{4,3,2,1,0:T(8,128)(2,1)S(1)} %collective-permute-done.12.mate_ref, bf16[4,2,128,256]{3,2,1,0:T(8,128)(2,1)S(1)} %pad_maximum_fusion.refs_0_, ...), custom_call_target="tpu_custom_call" | custom-call | flops 1879048192 | bytes 7340032 | tf_op jit(solution)/shard_map/final_products/pallas_call | solution.py:86
  (1 shorter events, 0.0 us)
Async XLA Ops:
  7.2 69.1 %copy-start = (bf16[256,4096]{1,0:T(8,128)(2,1)S(1)}, bf16[256,4096]{1,0:T(8,128)(2,1)}, u32[]{:S(2)}) copy-start(bf16[256,4096]{1,0:T(8,128)(2,1)} %param.5) | copy-start | bytes 6291460
  7.2 56.0 %all-gather.5.cloned.1.call-start = ((), (), s32[]{:S(2)}) async-start(), calls=%async_computation.3 | async-start | bytes 4014080 | tf_op jit(solution)/shard_map/all_gather | solution.py:107
  7.9 143.4 %reduce-scatter.2.cloned.1.call-start = ((), (), s32[]{:S(2)}) async-start(), calls=%async_computation.2 | async-start | bytes 2064384 | tf_op jit(solution)/shard_map/reduce_scatter | solution.py:124
  8.0 21.6 %collective-permute-start = (bf16[128,896]{1,0:T(8,128)(2,1)}, bf16[128,896]{1,0:T(8,128)(2,1)S(1)}, u32[]{:S(2)}, u32[]{:S(2)}) collective-permute-start(bf16[128,896]{1,0:T(8,128)(2,1)} %param.6), channel_id=1, source_target_pairs={{0,64},{64,0},{1,65},{65,1},{2,66},{66,2},{3,67},{67,3},{4,68},{68... | collective-permute-start | bytes 688136 | tf_op jit(solution)/shard_map/ppermute | solution.py:106
  30.6 13.4 %collective-permute-start.3 = (bf16[2,128,896]{2,1,0:T(8,128)(2,1)S(1)}, bf16[2,128,896]{2,1,0:T(8,128)(2,1)S(1)}, u32[]{:S(2)}, u32[]{:S(2)}) collective-permute-start(bf16[2,128,896]{2,1,0:T(8,128)(2,1)S(1)} %pad_maximum_fusion.1.refs_0_), channel_id=1, source_target_pairs={{384,0},{0,128},{128,256},{256,384},{385,1},{1,129},{129,257},{257... | collective-permute-start | bytes 1376264 | tf_op jit(solution)/shard_map/ppermute | solution.py:24
  34.0 21.4 %collective-permute-start.2 = (bf16[2,128,896]{2,1,0:T(8,128)(2,1)S(1)}, bf16[2,128,896]{2,1,0:T(8,128)(2,1)S(1)}, u32[]{:S(2)}, u32[]{:S(2)}) collective-permute-start(bf16[2,128,896]{2,1,0:T(8,128)(2,1)S(1)} %pad_maximum_fusion.1.refs_0_), channel_id=1, source_target_pairs={{256,0},{384,128},{0,256},{128,384},{257,1},{385,129},{1,257},{129... | collective-permute-start | bytes 1376264 | tf_op jit(solution)/shard_map/ppermute | solution.py:24
  38.5 19.2 %collective-permute-start.1 = (bf16[2,128,896]{2,1,0:T(8,128)(2,1)S(1)}, bf16[2,128,896]{2,1,0:T(8,128)(2,1)}, u32[]{:S(2)}, u32[]{:S(2)}) collective-permute-start(bf16[2,128,896]{2,1,0:T(8,128)(2,1)S(1)} %pad_maximum_fusion.1.refs_0_), channel_id=1, source_target_pairs={{128,0},{256,128},{384,256},{0,384},{129,1},{257,129},{385,257},{1... | collective-permute-start | bytes 1376264 | tf_op jit(solution)/shard_map/ppermute | solution.py:24
  63.2 1.9 copy-start.1
  65.1 6.0 %copy-start.2 = (bf16[1792,896]{1,0:T(8,128)(2,1)S(1)}, bf16[1792,896]{1,0:T(8,128)(2,1)}, u32[]{:S(2)}) copy-start(bf16[1792,896]{1,0:T(8,128)(2,1)} %all-gather.5.cloned.1.call-done) | copy-start | bytes 9633796
  68.4 6.0 %collective-permute-start.4 = (bf16[8,4,112,256]{3,2,1,0:T(8,128)(2,1)S(1)}, bf16[8,4,112,256]{3,2,1,0:T(8,128)(2,1)S(1)}, u32[]{:S(2)}, u32[]{:S(2)}) collective-permute-start(bf16[8,4,112,256]{3,2,1,0:T(8,128)(2,1)S(1)} %block_sums.3), channel_id=1, source_target_pairs={{0,1},{1,0},{2,3},{3,2},{4,5},{5,4},{6,7},{7,6},{8,9},{9,8},{10,11... | collective-permute-start | bytes 5505032 | tf_op jit(solution)/shard_map/ppermute | solution.py:106
  76.1 1.2 copy-start.8
  76.2 149.9 %all-gather.7.cloned.1.call-start = ((), (), s32[]{:S(2)}) async-start(), calls=%async_computation.4 | async-start | bytes 2064384 | tf_op jit(solution)/shard_map/all_gather | solution.py:127
  78.3 14.7 %collective-permute-start.5 = (bf16[128,256]{1,0:T(8,128)(2,1)S(1)}, bf16[128,256]{1,0:T(8,128)(2,1)S(1)}, u32[]{:S(2)}, u32[]{:S(2)}) collective-permute-start(bf16[128,256]{1,0:T(8,128)(2,1)S(1)} %convolution_convert_fusion), channel_id=1, source_target_pairs={{0,64},{64,0},{1,65},{65,1},{2,66},{66,2},{3,67},{67,3},{4,68},{68... | collective-permute-start | bytes 196616 | tf_op jit(solution)/shard_map/ppermute | solution.py:106
  93.0 9.9 %collective-permute-start.7 = (bf16[2,128,256]{2,1,0:T(8,128)(2,1)S(1)}, bf16[2,128,256]{2,1,0:T(8,128)(2,1)S(1)}, u32[]{:S(2)}, u32[]{:S(2)}) collective-permute-start(bf16[2,128,256]{2,1,0:T(8,128)(2,1)S(1)} %get-tuple-element.17), channel_id=1, source_target_pairs={{256,0},{384,128},{0,256},{128,384},{257,1},{385,129},{1,257},{129... | collective-permute-start | bytes 393224 | tf_op jit(solution)/shard_map/ppermute | solution.py:24
  97.6 5.7 %collective-permute-start.6 = (bf16[2,128,256]{2,1,0:T(8,128)(2,1)S(1)}, bf16[2,128,256]{2,1,0:T(8,128)(2,1)S(1)}, u32[]{:S(2)}, u32[]{:S(2)}) collective-permute-start(bf16[2,128,256]{2,1,0:T(8,128)(2,1)S(1)} %get-tuple-element.17), channel_id=1, source_target_pairs={{128,0},{256,128},{384,256},{0,384},{129,1},{257,129},{385,257},{1... | collective-permute-start | bytes 393224 | tf_op jit(solution)/shard_map/ppermute | solution.py:24
  100.4 6.9 %collective-permute-start.8 = (bf16[2,128,256]{2,1,0:T(8,128)(2,1)S(1)}, bf16[2,128,256]{2,1,0:T(8,128)(2,1)S(1)}, u32[]{:S(2)}, u32[]{:S(2)}) collective-permute-start(bf16[2,128,256]{2,1,0:T(8,128)(2,1)S(1)} %get-tuple-element.17), channel_id=1, source_target_pairs={{384,0},{0,128},{128,256},{256,384},{385,1},{1,129},{129,257},{257... | collective-permute-start | bytes 393224 | tf_op jit(solution)/shard_map/ppermute | solution.py:24
  107.4 14.7 %collective-permute-start.11 = (bf16[4,2,128,256]{3,2,1,0:T(8,128)(2,1)S(1)}, bf16[4,2,128,256]{3,2,1,0:T(8,128)(2,1)S(1)}, u32[]{:S(2)}, u32[]{:S(2)}) collective-permute-start(bf16[4,2,128,256]{3,2,1,0:T(8,128)(2,1)S(1)} %pad_maximum_fusion.refs_0_), channel_id=1, source_target_pairs={{48,0},{0,16},{16,32},{32,48},{49,1},{1,17},{17,33},{33,49},{50,2}... | collective-permute-start | bytes 1572872 | tf_op jit(solution)/shard_map/ppermute | solution.py:24
  109.7 22.2 %collective-permute-start.10 = (bf16[4,2,128,256]{3,2,1,0:T(8,128)(2,1)S(1)}, bf16[4,2,128,256]{3,2,1,0:T(8,128)(2,1)S(1)}, u32[]{:S(2)}, u32[]{:S(2)}) collective-permute-start(bf16[4,2,128,256]{3,2,1,0:T(8,128)(2,1)S(1)} %pad_maximum_fusion.refs_0_), channel_id=1, source_target_pairs={{32,0},{48,16},{0,32},{16,48},{33,1},{49,17},{1,33},{17,49},{34,2}... | collective-permute-start | bytes 1572872 | tf_op jit(solution)/shard_map/ppermute | solution.py:24
  113.1 23.9 %collective-permute-start.9 = (bf16[4,2,128,256]{3,2,1,0:T(8,128)(2,1)S(1)}, bf16[4,2,128,256]{3,2,1,0:T(8,128)(2,1)S(1)}, u32[]{:S(2)}, u32[]{:S(2)}) collective-permute-start(bf16[4,2,128,256]{3,2,1,0:T(8,128)(2,1)S(1)} %pad_maximum_fusion.refs_0_), channel_id=1, source_target_pairs={{16,0},{32,16},{48,32},{0,48},{17,1},{33,17},{49,33},{1,49},{18,2}... | collective-permute-start | bytes 1572872 | tf_op jit(solution)/shard_map/ppermute | solution.py:24
  131.9 0.8 copy-start.4
  137.1 0.8 copy-start.6
  226.1 11.3 %collective-permute-start.12 = (bf16[4,2,4,112,256]{4,3,2,1,0:T(8,128)(2,1)}, bf16[4,2,4,112,256]{4,3,2,1,0:T(8,128)(2,1)S(1)}, u32[]{:S(2)}, u32[]{:S(2)}) collective-permute-start(bf16[4,2,4,112,256]{4,3,2,1,0:T(8,128)(2,1)} %bitcast.19), channel_id=1, source_target_pairs={{0,1},{1,0},{2,3},{3,2},{4,5},{5,4},{6,7},{7,6},{8,9},{9,8},{10,11... | collective-permute-start | bytes 5505032 | tf_op jit(solution)/shard_map/ppermute | solution.py:106
  237.4 1.5 copy-start.3
  238.9 1.0 copy-start.5
  239.9 1.0 copy-start.7
Sparse Core Ops, SparseCore 0:
  10.1 53.0 all-gather.4
  76.3 74.9 reduce-scatter.1
  161.5 64.5 all-gather.6

commit v3 on v2

v3 whole, which is shorter than its diff:
```python
import functools

import jax
import jax.numpy as jnp
from jax import lax
from jax.experimental import pallas as pl
from jax.experimental.pallas import tpu as pltpu
from jax.sharding import Mesh, PartitionSpec as P

F32 = jnp.float32
BF16 = jnp.bfloat16
NX, NY, NM = 4, 4, 4
VMEM = pl.BlockSpec(memory_space=pltpu.VMEM)
SMEM = pl.BlockSpec(memory_space=pltpu.SMEM)


def params():
    return pltpu.CompilerParams(vmem_limit_bytes=24 * 1024 * 1024)


def cost(flops, nbytes):
    return pl.CostEstimate(flops=flops, bytes_accessed=nbytes, transcendentals=0)


def from_rel(value, axis, step, size):
    return lax.ppermute(value, axis, [((i + step) % size, i) for i in range(size)])


def block_kernel(where_ref, *refs):
    tokens, basis_ref, out_ref = refs[:NY], refs[NY], refs[NY + 1]
    half = where_ref[1]
    rows = tokens[0].shape[1]
    piece = basis_ref.shape[1] // NM
    for j in range(NX):
        for parity in range(2):
            right = jnp.concatenate([tokens[2 * parity + n][half] for n in range(2)], axis=0)
            sums = lax.dot_general(
                basis_ref[j], right, (((1,), (1,)), ((), ())), preferred_element_type=F32
            ).astype(BF16)
            for m in range(NM):
                out_ref[2 * m + parity, j] = sums[m * piece : (m + 1) * piece]


def block_sums(where, tokens, basis):
    _, rows, depth = tokens[0].shape
    crows = basis.shape[1]
    return pl.pallas_call(
        block_kernel,
        out_shape=jax.ShapeDtypeStruct((2 * NM, NX, crows // NM, 2 * rows), BF16),
        in_specs=[SMEM] + [VMEM] * (NY + 1),
        out_specs=VMEM,
        compiler_params=params(),
        cost_estimate=cost(2 * NX * crows * NY * rows * depth, 9 * 2**20),
        name="block_sums",
    )(where, *tokens, basis)


def add_products(out1, out2, first, pieces, acts, cols):
    for j in range(NX):
        g, a = pieces(j), acts(j)[:, cols]
        gw, aw = g.astype(F32), a.astype(F32)
        g2, a2 = (gw * gw).astype(BF16), (aw * aw).astype(BF16)
        p1 = jnp.dot(g, a, preferred_element_type=F32)
        p2 = jnp.dot(g2, a2, preferred_element_type=F32)
        if first and j == 0:
            out1[...] = p1
            out2[...] = p2
        else:
            out1[...] += p1
            out2[...] += p2


def pieces_of(ref):
    pairs, _, piece, width = ref.shape
    return lambda j: ref[:, j].reshape(pairs * piece, width)


def acts_of(refs, here, half):
    rows, cols = refs[0].shape[2:]

    def at(j):
        return refs[j][:, half].reshape(2 * rows, cols)

    return at


def near_kernel(where_ref, mine_ref, *refs):
    acts, (p1_ref, p2_ref) = refs[:NX], refs[NX:]
    here, core = where_ref[0], where_ref[1]
    side = pieces_of(mine_ref)
    add_products(
        p1_ref, p2_ref, True, lambda j: side(lax.rem(here + j, NX)), acts_of(acts, here, core), slice(None)
    )


def far_kernel(keep, where_ref, mate_ref, p1_ref, p2_ref, *refs):
    acts, outs = refs[:NX], refs[NX:]
    acc1, acc2 = outs[-2:]
    here, core = where_ref[0], where_ref[1]
    half = acc1.shape[1]
    cols = slice(0, half) if keep else slice(half, 2 * half)
    acc1[...] = p1_ref[:, cols]
    acc2[...] = p2_ref[:, cols]
    side = pieces_of(mate_ref)
    add_products(
        acc1, acc2, False, lambda j: side(lax.rem(here + j, NX)), acts_of(acts, here, 1 - core), cols
    )
    total = 2 * NY * NX * acts[0].shape[2]
    if keep:
        acc2[...] = acc2[...] / total
    else:
        outs[0][0] = acc1[...].astype(BF16)
        outs[0][1] = (acc2[...] / total).astype(BF16)


def near_products(where, mine, acts):
    pairs, _, piece, width = mine.shape
    shape = jax.ShapeDtypeStruct((pairs * piece, acts[0].shape[-1]), F32)
    return pl.pallas_call(
        near_kernel,
        out_shape=(shape, shape),
        in_specs=[SMEM] + [VMEM] * (1 + NX),
        out_specs=(VMEM, VMEM),
        compiler_params=params(),
        cost_estimate=cost(4 * 448 * 1024 * 512, 5 * 2**20),
        name="near_products",
    )(where, mine, *acts)


def far_products(keep, where, mate, p1, p2, acts):
    crows, cols = p1.shape
    shape = jax.ShapeDtypeStruct((crows, cols // 2), F32)
    return pl.pallas_call(
        functools.partial(far_kernel, keep),
        out_shape=(shape, shape) if keep else jax.ShapeDtypeStruct((2, crows, cols // 2), BF16),
        in_specs=[SMEM] + [VMEM] * (3 + NX),
        out_specs=(VMEM, VMEM) if keep else VMEM,
        scratch_shapes=[] if keep else [pltpu.VMEM((crows, cols // 2), F32)] * 2,
        compiler_params=params(),
        cost_estimate=cost(2 * 448 * 1024 * 512, 5 * 2**20),
        name="far_products",
    )(where, mate, p1, p2, *acts)


def added(*values):
    total = values[0].astype(F32)
    for v in values[1:]:
        total = total + v.astype(F32)
    return total.astype(BF16)


def own_columns(value, parity):
    rows = [((i + 2) % NY * 2 + 1, i * 2 + 1) for i in range(NY)]
    first = jnp.where(parity == 0, value, lax.ppermute(value, ("y", "p"), rows))
    rows = [((i + 1 + 2 * p) % NY * 2 + p, i * 2 + p) for i in range(NY) for p in range(2)]
    return jnp.stack([first, lax.ppermute(value, ("y", "p"), rows)])


def body(activations, act_basis, out_grads, grad_basis):
    x, core, parity = (lax.axis_index(a) for a in ("x", "c", "p"))
    swap = lambda v, axis: lax.ppermute(v, axis, [(0, 1), (1, 0)])
    pack = lambda *v: jnp.stack(v).astype(jnp.int32)
    basis = lax.all_gather(grad_basis, "x", axis=0, tiled=False)
    halves = jnp.stack([out_grads, swap(out_grads, "h")])
    tokens = [halves] + [from_rel(halves, "y", j, NY) for j in (1, 2, 3)]

    acts = lax.dot_general(
        activations, act_basis, (((1,), (1,)), ((), ())), preferred_element_type=F32
    ).astype(BF16)
    acts = jnp.stack([acts, swap(acts, "h")])
    *tokens, acts = lax.optimization_barrier((*tokens, acts))

    send = block_sums(pack(x, 1 - core), tokens, basis)
    got = swap(send, "c")
    mine = block_sums(pack(x, core), tokens, basis)
    partial = added(mine, got)

    acts, partial = lax.optimization_barrier((acts, partial))
    acts = own_columns(jnp.concatenate([acts, swap(acts, "p")], axis=-1), parity)
    all_acts = [acts] + [from_rel(acts, "x", j, NX) for j in (1, 2, 3)]

    own = lax.psum_scatter(partial, ("m", "p"), scatter_dimension=0, tiled=False)
    own, all_acts = lax.optimization_barrier((own, all_acts))
    own = lax.all_to_all(own, "x", split_axis=0, concat_axis=0, tiled=True)
    mine = lax.all_gather(own, "m", axis=0, tiled=False)
    mate = swap(mine, "c")
    where = pack(x, core)
    p1, p2 = near_products(where, mine, all_acts)
    away = swap(far_products(False, where, mate, p1, p2, all_acts), "p")
    grad, scale = far_products(True, where, mate, p1, p2, all_acts)
    return grad + away[0].astype(F32), scale + away[1].astype(F32)


def solution(mesh):
    fine = Mesh(mesh.devices.reshape(NY, 2, NX, NM, 2, 2), ("y", "h", "x", "m", "p", "c"))
    dp, tensor = ("y", "h", "x"), ("m", "p", "c")
    return jax.shard_map(
        body,
        mesh=fine,
        in_specs=(P(dp, None), P(tensor, None), P(dp, tensor), P(dp, tensor)),
        out_specs=(P(dp, tensor), P(dp, tensor)),
        check_vma=False,
    )
```

time: 252 us -> 230 us (0.913)
  waiting for transfers between devices: 136 us -> 68.6 us
  blocking collectives: 10 us -> 36.9 us
  starting transfers between devices: 69.5 us -> 86.1 us
  local copies, waits for them, and re-layouts: 8.25 us -> 5.63 us
    all_gather x1 -> x0, waiting for transfers between devices: 64.7 us -> none  [body(): lax.all_gather(own, ('m', 'p'), axis=0, tiled=False)]
    all_gather x0 -> x1, blocking collectives: none -> 27.6 us  [body(): mine = lax.all_gather(own, 'm', axis=0, tiled=False)]
    ppermute x4 -> x6, starting transfers between devices: 39.1 us -> 62 us  [body(): swap = lambda v, axis: lax.ppermute(v, axis, [(0, 1), (1, 0)])]
    ppermute x9 -> x6, waiting for transfers between devices: 39.9 us -> 18.3 us  [from_rel(): lax.ppermute(value, axis, [((i + step) % size, i) for i in range(size)])]
    ppermute x4 -> x6, waiting for transfers between devices: 11.3 us -> 20.6 us  [body(): swap = lambda v, axis: lax.ppermute(v, axis, [(0, 1), (1, 0)])]
    ppermute x9 -> x6, starting transfers between devices: 30.3 us -> 21.4 us  [from_rel(): lax.ppermute(value, axis, [((i + step) % size, i) for i in range(size)])]
    ppermute x0 -> x2, waiting for transfers between devices: none -> 6.85 us  [the longest x1 6.85 us: own_columns(): return jnp.stack([first, lax.ppermute(value, ('y', 'p'), rows)])]
    reduce_scatter x1, waiting for transfers between devices: 13.4 us -> 17.8 us  [body(): lax.psum_scatter(partial, ('m', 'p'), scatter_dimension=0, tiled=False)]
  transfers between devices with their start and end apart: 16 -> 16, of which waited for: 15 -> 11; matrix products, arithmetic and copies ran while one was open for 1% -> 2% of each run, Pallas kernels for 1% -> 3%
where the time goes in v3:
time: 230 us; the launch traced here: 229 us
  starting transfers between devices  86.1 us (37%)
  waiting for transfers between devices  68.6 us (30%)
  blocking collectives  36.9 us (16%)
  between operations  14.3 us (6%)
  Pallas kernels  10.5 us (5%)
  local copies, waits for them, and re-layouts  5.63 us (2%)
  other arithmetic  5.43 us (2%)
    ppermute x6, starting transfers between devices, body(): swap = lambda v, axis: lax.ppermute(v, axis, [(0, 1), (1, 0)])  62 us
    all_gather x1, blocking collectives, body(): mine = lax.all_gather(own, 'm', axis=0, tiled=False)  27.6 us
    ppermute x6, starting transfers between devices, from_rel(): lax.ppermute(value, axis, [((i + step) % size, i) for i in range(size)])  21.4 us
    ppermute x6, waiting for transfers between devices, body(): swap = lambda v, axis: lax.ppermute(v, axis, [(0, 1), (1, 0)])  20.6 us
    ppermute x6, waiting for transfers between devices, from_rel(): lax.ppermute(value, axis, [((i + step) % size, i) for i in range(size)])  18.3 us
    reduce_scatter x1, waiting for transfers between devices, body(): lax.psum_scatter(partial, ('m', 'p'), scatter_dimension=0, tiled=False)  17.8 us
    all_to_all x1, blocking collectives, body(): own = lax.all_to_all(own, 'x', split_axis=0, concat_axis=0, tiled=True)  9.21 us
    ppermute x1, waiting for transfers between devices, own_columns(): return jnp.stack([first, lax.ppermute(value, ('y', 'p'), rows)])  6.85 us
  transfers between devices with their start and end apart: 16, of which 11 were waited for; matrix products, arithmetic and copies ran while one was open for 2% of the time, Pallas kernels for 3%

profile of v3, /device:TPU:1, one launch (start us, length us, event | category | flops | bytes accessed | tf_op | source)
XLA Modules:
  0.0 229.5 jit_solution(4220253903757945148)
XLA Ops:
  7.2 0.0 copy-start
  7.2 0.0 all-gather.4.cloned.1.call-start
  7.2 0.7 all-gather.4.cloned.1.call-update
  7.9 0.0 reduce-scatter.2.cloned.1.call-start
  8.0 16.3 %collective-permute-start = (bf16[128,896]{1,0:T(8,128)(2,1)}, bf16[128,896]{1,0:T(8,128)(2,1)S(1)}, u32[]{:S(2)}, u32[]{:S(2)}) collective-permute-start(bf16[128,896]{1,0:T(8,128)(2,1)} %param.6), channel_id=1, source_target_pairs={{0,64},{64,0},{1,65},{65,1},{2,66},{66,2},{3,67},{67,3},{4,68},{68... | collective-permute-start | bytes 688136 | tf_op jit(solution)/shard_map/ppermute | solution.py:161
  24.2 5.3 %collective-permute-done = bf16[128,896]{1,0:T(8,128)(2,1)S(1)} collective-permute-done((bf16[128,896]{1,0:T(8,128)(2,1)}, bf16[128,896]{1,0:T(8,128)(2,1)S(1)}, u32[]{:S(2)}, u32[]{:S(2)}) %collective-permute-start) | collective-permute-done | bytes 229408 | tf_op jit(solution)/shard_map/ppermute | solution.py:161
  29.6 1.0 pad_maximum_fusion.1.refs_0_
  30.6 3.4 %collective-permute-start.3 = (bf16[2,128,896]{2,1,0:T(8,128)(2,1)S(1)}, bf16[2,128,896]{2,1,0:T(8,128)(2,1)S(1)}, u32[]{:S(2)}, u32[]{:S(2)}) collective-permute-start(bf16[2,128,896]{2,1,0:T(8,128)(2,1)S(1)} %pad_maximum_fusion.1.refs_0_), channel_id=1, source_target_pairs={{384,0},{0,128},{128,256},{256,384},{385,1},{1,129},{129,257},{257... | collective-permute-start | bytes 1376264 | tf_op jit(solution)/shard_map/ppermute | solution.py:26
  34.0 4.5 %collective-permute-start.2 = (bf16[2,128,896]{2,1,0:T(8,128)(2,1)S(1)}, bf16[2,128,896]{2,1,0:T(8,128)(2,1)S(1)}, u32[]{:S(2)}, u32[]{:S(2)}) collective-permute-start(bf16[2,128,896]{2,1,0:T(8,128)(2,1)S(1)} %pad_maximum_fusion.1.refs_0_), channel_id=1, source_target_pairs={{256,0},{384,128},{0,256},{128,384},{257,1},{385,129},{1,257},{129... | collective-permute-start | bytes 1376264 | tf_op jit(solution)/shard_map/ppermute | solution.py:26
  38.5 3.0 %collective-permute-start.1 = (bf16[2,128,896]{2,1,0:T(8,128)(2,1)S(1)}, bf16[2,128,896]{2,1,0:T(8,128)(2,1)}, u32[]{:S(2)}, u32[]{:S(2)}) collective-permute-start(bf16[2,128,896]{2,1,0:T(8,128)(2,1)S(1)} %pad_maximum_fusion.1.refs_0_), channel_id=1, source_target_pairs={{128,0},{256,128},{384,256},{0,384},{129,1},{257,129},{385,257},{1... | collective-permute-start | bytes 1376264 | tf_op jit(solution)/shard_map/ppermute | solution.py:26
  41.5 0.0 copy-done
  41.5 2.1 convolution_convert_fusion
  43.6 11.8 %collective-permute-start.4 = (bf16[128,256]{1,0:T(8,128)(2,1)S(1)}, bf16[128,256]{1,0:T(8,128)(2,1)}, u32[]{:S(2)}, u32[]{:S(2)}) collective-permute-start(bf16[128,256]{1,0:T(8,128)(2,1)S(1)} %convolution_convert_fusion), channel_id=1, source_target_pairs={{0,64},{64,0},{1,65},{65,1},{2,66},{66,2},{3,67},{67,3},{4,68},{68... | collective-permute-start | bytes 196616 | tf_op jit(solution)/shard_map/ppermute | solution.py:161
  55.4 0.1 pad_add_fusion.1.where_ref
  55.5 1.9 collective-permute-done.4
  57.4 1.5 pad_maximum_fusion.2
  58.9 0.0 collective-permute-done.3.refs_3_
  58.9 0.0 collective-permute-done.2.refs_2_
  58.9 0.0 collective-permute-done.1.refs_1_
  58.9 4.3 %all-gather.4.cloned.1.call-done = bf16[1792,896]{1,0:T(8,128)(2,1)} async-done(((bf16[448,896]{1,0:T(8,128)(2,1)}), bf16[1792,896]{1,0:T(8,128)(2,1)}) %all-gather.4.cloned.1.call-update) | async-done | bytes 3211280 | tf_op jit(solution)/shard_map/all_gather | solution.py:163
  63.2 0.0 copy-start.1
  63.2 1.9 copy-done.1
  65.1 0.0 copy-start.2
  65.1 3.3 %block_sums.3 = bf16[8,4,112,256]{3,2,1,0:T(8,128)(2,1)S(1)} custom-call(s32[2]{0:T(128)S(1)} %pad_add_fusion.1.where_ref, bf16[2,128,896]{2,1,0:T(8,128)(2,1)S(1)} %pad_maximum_fusion.1.refs_0_, bf16[2,128,896]{2,1,0:T(8,128)(2,1)} %collective-permute-done.1.refs_1_, bf16[2,128,896]{2,1,0:T(8,128)(2,1)S(1)} %collective-permute-done.2.refs_2_, ...), custom_call_target="tpu_custom_call" | custom-call | flops 1644167168 | bytes 9437184 | tf_op jit(solution)/shard_map/block_sums/pallas_call | solution.py:47
  68.4 2.6 %collective-permute-start.5 = (bf16[8,4,112,256]{3,2,1,0:T(8,128)(2,1)S(1)}, bf16[8,4,112,256]{3,2,1,0:T(8,128)(2,1)S(1)}, u32[]{:S(2)}, u32[]{:S(2)}) collective-permute-start(bf16[8,4,112,256]{3,2,1,0:T(8,128)(2,1)S(1)} %block_sums.3), channel_id=1, source_target_pairs={{0,1},{1,0},{2,3},{3,2},{4,5},{5,4},{6,7},{7,6},{8,9},{9,8},{10,11... | collective-permute-start | bytes 5505032 | tf_op jit(solution)/shard_map/ppermute | solution.py:161
  71.0 0.1 pad_add_fusion.where_ref
  71.1 0.0 copy-done.2
  71.1 3.1 %block_sums.2 = bf16[8,4,112,256]{3,2,1,0:T(8,128)(2,1)S(1)} custom-call(s32[2]{0:T(128)S(1)} %pad_add_fusion.where_ref, bf16[2,128,896]{2,1,0:T(8,128)(2,1)S(1)} %pad_maximum_fusion.1.refs_0_, bf16[2,128,896]{2,1,0:T(8,128)(2,1)} %collective-permute-done.1.refs_1_, bf16[2,128,896]{2,1,0:T(8,128)(2,1)S(1)} %collective-permute-done.2.refs_2_, ...), custom_call_target="tpu_custom_call" | custom-call | flops 1644167168 | bytes 9437184 | tf_op jit(solution)/shard_map/block_sums/pallas_call | solution.py:47
  74.2 0.0 copy-start.8
  74.2 0.2 collective-permute-done.5
  74.4 1.7 add_convert_fusion
  76.1 0.0 reduce-scatter.2.cloned.1.call-update
  76.1 0.0 copy-done.8
  76.1 16.1 %collective-permute-start.6 = (bf16[2,128,256]{2,1,0:T(8,128)(2,1)S(1)}, bf16[2,128,256]{2,1,0:T(8,128)(2,1)S(1)}, u32[]{:S(2)}, u32[]{:S(2)}) collective-permute-start(bf16[2,128,256]{2,1,0:T(8,128)(2,1)S(1)} %copy-done.8), channel_id=1, source_target_pairs={{0,2},{2,0},{1,3},{3,1},{4,6},{6,4},{5,7},{7,5},{8,10},{10,8},{9,1... | collective-permute-start | bytes 393224 | tf_op jit(solution)/shard_map/ppermute | solution.py:161
  92.2 3.5 %collective-permute-done.6 = bf16[2,128,256]{2,1,0:T(8,128)(2,1)S(1)} collective-permute-done((bf16[2,128,256]{2,1,0:T(8,128)(2,1)S(1)}, bf16[2,128,256]{2,1,0:T(8,128)(2,1)S(1)}, u32[]{:S(2)}, u32[]{:S(2)}) %collective-permute-start.6) | collective-permute-done | bytes 131104 | tf_op jit(solution)/shard_map/ppermute | solution.py:161
  95.8 0.7 collective-permute-start.7
  96.4 1.9 collective-permute-start.8
  98.4 0.0 collective-permute-done.7
  98.4 6.8 %collective-permute-done.8 = bf16[2,128,512]{2,1,0:T(8,128)(2,1)S(1)} collective-permute-done((bf16[2,128,512]{2,1,0:T(8,128)(2,1)S(1)}, bf16[2,128,512]{2,1,0:T(8,128)(2,1)S(1)}, u32[]{:S(2)}, u32[]{:S(2)}) %collective-permute-start.8) | collective-permute-done | bytes 262176 | tf_op jit(solution)/shard_map/ppermute | solution.py:156
  105.3 0.1 pad_maximum_fusion.refs_0_
  105.3 3.1 %collective-permute-start.11 = (bf16[2,2,128,512]{3,2,1,0:T(8,128)(2,1)S(1)}, bf16[2,2,128,512]{3,2,1,0:T(8,128)(2,1)S(1)}, u32[]{:S(2)}, u32[]{:S(2)}) collective-permute-start(bf16[2,2,128,512]{3,2,1,0:T(8,128)(2,1)S(1)} %pad_maximum_fusion.refs_0_), channel_id=1, source_target_pairs={{48,0},{0,16},{16,32},{32,48},{49,1},{1,17},{17,33},{33,49},{50,2}... | collective-permute-start | bytes 1572872 | tf_op jit(solution)/shard_map/ppermute | solution.py:26
  108.5 4.4 %collective-permute-start.10 = (bf16[2,2,128,512]{3,2,1,0:T(8,128)(2,1)S(1)}, bf16[2,2,128,512]{3,2,1,0:T(8,128)(2,1)S(1)}, u32[]{:S(2)}, u32[]{:S(2)}) collective-permute-start(bf16[2,2,128,512]{3,2,1,0:T(8,128)(2,1)S(1)} %pad_maximum_fusion.refs_0_), channel_id=1, source_target_pairs={{32,0},{48,16},{0,32},{16,48},{33,1},{49,17},{1,33},{17,49},{34,2}... | collective-permute-start | bytes 1572872 | tf_op jit(solution)/shard_map/ppermute | solution.py:26
  112.8 3.1 %collective-permute-start.9 = (bf16[2,2,128,512]{3,2,1,0:T(8,128)(2,1)S(1)}, bf16[2,2,128,512]{3,2,1,0:T(8,128)(2,1)S(1)}, u32[]{:S(2)}, u32[]{:S(2)}) collective-permute-start(bf16[2,2,128,512]{3,2,1,0:T(8,128)(2,1)S(1)} %pad_maximum_fusion.refs_0_), channel_id=1, source_target_pairs={{16,0},{32,16},{48,32},{0,48},{17,1},{33,17},{49,33},{1,49},{18,2}... | collective-permute-start | bytes 1572872 | tf_op jit(solution)/shard_map/ppermute | solution.py:26
  115.9 4.3 %collective-permute-done.11.refs_3_ = bf16[2,2,128,512]{3,2,1,0:T(8,128)(2,1)S(1)} collective-permute-done((bf16[2,2,128,512]{3,2,1,0:T(8,128)(2,1)S(1)}, bf16[2,2,128,512]{3,2,1,0:T(8,128)(2,1)S(1)}, u32[]{:S(2)}, u32[]{:S(2)}) %collective-permute-start.11) | collective-permute-done | bytes 524320 | tf_op jit(solution)/shard_map/ppermute | solution.py:26
  120.2 12.2 %collective-permute-done.10.refs_2_ = bf16[2,2,128,512]{3,2,1,0:T(8,128)(2,1)S(1)} collective-permute-done((bf16[2,2,128,512]{3,2,1,0:T(8,128)(2,1)S(1)}, bf16[2,2,128,512]{3,2,1,0:T(8,128)(2,1)S(1)}, u32[]{:S(2)}, u32[]{:S(2)}) %collective-permute-start.10) | collective-permute-done | bytes 524320 | tf_op jit(solution)/shard_map/ppermute | solution.py:26
  132.4 0.0 copy-start.3
  132.4 0.8 copy-done.3
  133.2 1.8 collective-permute-done.9.refs_1_
  135.0 0.8 copy-done.6
  135.8 17.8 %reduce-scatter.2.cloned.1.call-done = bf16[1,4,112,256]{3,2,1,0:T(8,128)(2,1)} async-done(((bf16[8,4,112,256]{3,2,1,0:T(8,128)(2,1)}), bf16[1,4,112,256]{3,2,1,0:T(8,128)(2,1)}) %reduce-scatter.2.cloned.1.call-update) | async-done | bytes 229392 | tf_op jit(solution)/shard_map/reduce_scatter | solution.py:182
  153.6 9.2 %all_to_all.5 = bf16[4,112,256]{2,1,0:T(8,128)(2,1)S(1)} all-to-all(bf16[4,112,256]{2,1,0:T(8,128)(2,1)} %bitcast.33), channel_id=1, replica_groups=mesh['y'=4,'h'=2,'x'=4,'m'=4,'p'=2,'c'=2] {'x'}, dimensions={0} | all-to-all | bytes 458752 | tf_op jit(solution)/shard_map/all_to_all | solution.py:184
  162.8 27.6 %all-gather.1 = bf16[16,112,256]{2,1,0:T(8,128)(2,1)S(1)} all-gather(bf16[4,112,256]{2,1,0:T(8,128)(2,1)S(1)} %all_to_all.5), channel_id=3, replica_groups=mesh['y'=4,'h'=2,'x'=4,'m'=4,'p'=2,'c'=2] {'m'}, dimensions={0}, use_global_device_ids=true | all-gather | bytes 1146880 | tf_op jit(solution)/shard_map/all_gather | solution.py:185
  190.5 11.2 %collective-permute-start.12 = (bf16[4,4,112,256]{3,2,1,0:T(8,128)(2,1)S(1)}, bf16[4,4,112,256]{3,2,1,0:T(8,128)(2,1)S(1)}, u32[]{:S(2)}, u32[]{:S(2)}) collective-permute-start(bf16[4,4,112,256]{3,2,1,0:T(8,128)(2,1)S(1)} %bitcast.27), channel_id=1, source_target_pairs={{0,1},{1,0},{2,3},{3,2},{4,5},{5,4},{6,7},{7,6},{8,9},{9,8},{10,11... | collective-permute-start | bytes 2752520 | tf_op jit(solution)/shard_map/ppermute | solution.py:161
  201.7 0.0 copy-start.4
  201.7 1.0 copy-done.4
  202.8 1.0 copy-done.7
  203.8 1.7 near_products.1
  205.5 0.0 collective-permute-done.12.mate_ref
  205.5 0.0 copy-done.5
  205.5 1.2 far_products.3
  206.7 4.0 %collective-permute-start.13 = (bf16[2,448,256]{2,1,0:T(8,128)(2,1)S(1)}, bf16[2,448,256]{2,1,0:T(8,128)(2,1)S(1)}, u32[]{:S(2)}, u32[]{:S(2)}) collective-permute-start(bf16[2,448,256]{2,1,0:T(8,128)(2,1)S(1)} %far_products.3), channel_id=1, source_target_pairs={{0,2},{2,0},{1,3},{3,1},{4,6},{6,4},{5,7},{7,5},{8,10},{10,8},{9,1... | collective-permute-start | bytes 1376264 | tf_op jit(solution)/shard_map/ppermute | solution.py:161
  210.7 1.2 far_products.2
  212.0 9.7 %collective-permute-done.13 = bf16[2,448,256]{2,1,0:T(8,128)(2,1)S(1)} collective-permute-done((bf16[2,448,256]{2,1,0:T(8,128)(2,1)S(1)}, bf16[2,448,256]{2,1,0:T(8,128)(2,1)S(1)}, u32[]{:S(2)}, u32[]{:S(2)}) %collective-permute-start.13) | collective-permute-done | bytes 458784 | tf_op jit(solution)/shard_map/ppermute | solution.py:161
  221.6 1.0 convert_add_fusion
  (6 shorter events, 0.1 us)
Async XLA Ops:
  7.2 34.3 %copy-start = (bf16[256,4096]{1,0:T(8,128)(2,1)S(1)}, bf16[256,4096]{1,0:T(8,128)(2,1)}, u32[]{:S(2)}) copy-start(bf16[256,4096]{1,0:T(8,128)(2,1)} %param.5) | copy-start | bytes 6291460
  7.2 56.0 %all-gather.4.cloned.1.call-start = ((), (), s32[]{:S(2)}) async-start(), calls=%async_computation.3 | async-start | bytes 4014080 | tf_op jit(solution)/shard_map/all_gather | solution.py:163
  7.9 145.7 %reduce-scatter.2.cloned.1.call-start = ((), (), s32[]{:S(2)}) async-start(), calls=%async_computation.2 | async-start | bytes 2064384 | tf_op jit(solution)/shard_map/reduce_scatter | solution.py:182
  8.0 21.6 %collective-permute-start = (bf16[128,896]{1,0:T(8,128)(2,1)}, bf16[128,896]{1,0:T(8,128)(2,1)S(1)}, u32[]{:S(2)}, u32[]{:S(2)}) collective-permute-start(bf16[128,896]{1,0:T(8,128)(2,1)} %param.6), channel_id=1, source_target_pairs={{0,64},{64,0},{1,65},{65,1},{2,66},{66,2},{3,67},{67,3},{4,68},{68... | collective-permute-start | bytes 688136 | tf_op jit(solution)/shard_map/ppermute | solution.py:161
  30.6 28.4 %collective-permute-start.3 = (bf16[2,128,896]{2,1,0:T(8,128)(2,1)S(1)}, bf16[2,128,896]{2,1,0:T(8,128)(2,1)S(1)}, u32[]{:S(2)}, u32[]{:S(2)}) collective-permute-start(bf16[2,128,896]{2,1,0:T(8,128)(2,1)S(1)} %pad_maximum_fusion.1.refs_0_), channel_id=1, source_target_pairs={{384,0},{0,128},{128,256},{256,384},{385,1},{1,129},{129,257},{257... | collective-permute-start | bytes 1376264 | tf_op jit(solution)/shard_map/ppermute | solution.py:26
  34.0 25.0 %collective-permute-start.2 = (bf16[2,128,896]{2,1,0:T(8,128)(2,1)S(1)}, bf16[2,128,896]{2,1,0:T(8,128)(2,1)S(1)}, u32[]{:S(2)}, u32[]{:S(2)}) collective-permute-start(bf16[2,128,896]{2,1,0:T(8,128)(2,1)S(1)} %pad_maximum_fusion.1.refs_0_), channel_id=1, source_target_pairs={{256,0},{384,128},{0,256},{128,384},{257,1},{385,129},{1,257},{129... | collective-permute-start | bytes 1376264 | tf_op jit(solution)/shard_map/ppermute | solution.py:26
  38.5 20.4 %collective-permute-start.1 = (bf16[2,128,896]{2,1,0:T(8,128)(2,1)S(1)}, bf16[2,128,896]{2,1,0:T(8,128)(2,1)}, u32[]{:S(2)}, u32[]{:S(2)}) collective-permute-start(bf16[2,128,896]{2,1,0:T(8,128)(2,1)S(1)} %pad_maximum_fusion.1.refs_0_), channel_id=1, source_target_pairs={{128,0},{256,128},{384,256},{0,384},{129,1},{257,129},{385,257},{1... | collective-permute-start | bytes 1376264 | tf_op jit(solution)/shard_map/ppermute | solution.py:26
  43.6 13.8 %collective-permute-start.4 = (bf16[128,256]{1,0:T(8,128)(2,1)S(1)}, bf16[128,256]{1,0:T(8,128)(2,1)}, u32[]{:S(2)}, u32[]{:S(2)}) collective-permute-start(bf16[128,256]{1,0:T(8,128)(2,1)S(1)} %convolution_convert_fusion), channel_id=1, source_target_pairs={{0,64},{64,0},{1,65},{65,1},{2,66},{66,2},{3,67},{67,3},{4,68},{68... | collective-permute-start | bytes 196616 | tf_op jit(solution)/shard_map/ppermute | solution.py:161
  63.2 1.9 copy-start.1
  65.1 6.0 %copy-start.2 = (bf16[1792,896]{1,0:T(8,128)(2,1)S(1)}, bf16[1792,896]{1,0:T(8,128)(2,1)}, u32[]{:S(2)}) copy-start(bf16[1792,896]{1,0:T(8,128)(2,1)} %all-gather.4.cloned.1.call-done) | copy-start | bytes 9633796
  68.4 6.0 %collective-permute-start.5 = (bf16[8,4,112,256]{3,2,1,0:T(8,128)(2,1)S(1)}, bf16[8,4,112,256]{3,2,1,0:T(8,128)(2,1)S(1)}, u32[]{:S(2)}, u32[]{:S(2)}) collective-permute-start(bf16[8,4,112,256]{3,2,1,0:T(8,128)(2,1)S(1)} %block_sums.3), channel_id=1, source_target_pairs={{0,1},{1,0},{2,3},{3,2},{4,5},{5,4},{6,7},{7,6},{8,9},{9,8},{10,11... | collective-permute-start | bytes 5505032 | tf_op jit(solution)/shard_map/ppermute | solution.py:161
  74.2 1.9 copy-start.8
  76.1 19.6 %collective-permute-start.6 = (bf16[2,128,256]{2,1,0:T(8,128)(2,1)S(1)}, bf16[2,128,256]{2,1,0:T(8,128)(2,1)S(1)}, u32[]{:S(2)}, u32[]{:S(2)}) collective-permute-start(bf16[2,128,256]{2,1,0:T(8,128)(2,1)S(1)} %copy-done.8), channel_id=1, source_target_pairs={{0,2},{2,0},{1,3},{3,1},{4,6},{6,4},{5,7},{7,5},{8,10},{10,8},{9,1... | collective-permute-start | bytes 393224 | tf_op jit(solution)/shard_map/ppermute | solution.py:161
  95.8 2.6 %collective-permute-start.7 = (bf16[2,128,512]{2,1,0:T(8,128)(2,1)S(1)}, bf16[2,128,512]{2,1,0:T(8,128)(2,1)S(1)}, u32[]{:S(2)}, u32[]{:S(2)}) collective-permute-start(bf16[2,128,512]{2,1,0:T(8,128)(2,1)S(1)} %constant_dynamic-update-slice_fusion), channel_id=1, source_target_pairs={{258,2},{386,130},{2,258},{130,386},{259,3},{387,131},{3,259},{131... | collective-permute-start | bytes 786440 | tf_op jit(solution)/shard_map/ppermute | solution.py:154
  96.4 8.8 %collective-permute-start.8 = (bf16[2,128,512]{2,1,0:T(8,128)(2,1)S(1)}, bf16[2,128,512]{2,1,0:T(8,128)(2,1)S(1)}, u32[]{:S(2)}, u32[]{:S(2)}) collective-permute-start(bf16[2,128,512]{2,1,0:T(8,128)(2,1)S(1)} %constant_dynamic-update-slice_fusion), channel_id=1, source_target_pairs={{128,0},{386,2},{256,128},{2,130},{384,256},{130,258},{0,384},{258... | collective-permute-start | bytes 786440 | tf_op jit(solution)/shard_map/ppermute | solution.py:156
  105.3 14.8 %collective-permute-start.11 = (bf16[2,2,128,512]{3,2,1,0:T(8,128)(2,1)S(1)}, bf16[2,2,128,512]{3,2,1,0:T(8,128)(2,1)S(1)}, u32[]{:S(2)}, u32[]{:S(2)}) collective-permute-start(bf16[2,2,128,512]{3,2,1,0:T(8,128)(2,1)S(1)} %pad_maximum_fusion.refs_0_), channel_id=1, source_target_pairs={{48,0},{0,16},{16,32},{32,48},{49,1},{1,17},{17,33},{33,49},{50,2}... | collective-permute-start | bytes 1572872 | tf_op jit(solution)/shard_map/ppermute | solution.py:26
  108.5 23.9 %collective-permute-start.10 = (bf16[2,2,128,512]{3,2,1,0:T(8,128)(2,1)S(1)}, bf16[2,2,128,512]{3,2,1,0:T(8,128)(2,1)S(1)}, u32[]{:S(2)}, u32[]{:S(2)}) collective-permute-start(bf16[2,2,128,512]{3,2,1,0:T(8,128)(2,1)S(1)} %pad_maximum_fusion.refs_0_), channel_id=1, source_target_pairs={{32,0},{48,16},{0,32},{16,48},{33,1},{49,17},{1,33},{17,49},{34,2}... | collective-permute-start | bytes 1572872 | tf_op jit(solution)/shard_map/ppermute | solution.py:26
  112.8 22.2 %collective-permute-start.9 = (bf16[2,2,128,512]{3,2,1,0:T(8,128)(2,1)S(1)}, bf16[2,2,128,512]{3,2,1,0:T(8,128)(2,1)S(1)}, u32[]{:S(2)}, u32[]{:S(2)}) collective-permute-start(bf16[2,2,128,512]{3,2,1,0:T(8,128)(2,1)S(1)} %pad_maximum_fusion.refs_0_), channel_id=1, source_target_pairs={{16,0},{32,16},{48,32},{0,48},{17,1},{33,17},{49,33},{1,49},{18,2}... | collective-permute-start | bytes 1572872 | tf_op jit(solution)/shard_map/ppermute | solution.py:26
  132.4 0.8 copy-start.3
  135.0 0.8 copy-start.6
  162.8 42.6 %copy-start.5 = (bf16[2,2,128,512]{3,2,1,0:T(8,128)(2,1)S(1)}, bf16[2,2,128,512]{3,2,1,0:T(8,128)(2,1)}, u32[]{:S(2)}) copy-start(bf16[2,2,128,512]{3,2,1,0:T(8,128)(2,1)} %copy-done.3) | copy-start | bytes 1572868
  190.5 15.0 %collective-permute-start.12 = (bf16[4,4,112,256]{3,2,1,0:T(8,128)(2,1)S(1)}, bf16[4,4,112,256]{3,2,1,0:T(8,128)(2,1)S(1)}, u32[]{:S(2)}, u32[]{:S(2)}) collective-permute-start(bf16[4,4,112,256]{3,2,1,0:T(8,128)(2,1)S(1)} %bitcast.27), channel_id=1, source_target_pairs={{0,1},{1,0},{2,3},{3,2},{4,5},{5,4},{6,7},{7,6},{8,9},{9,8},{10,11... | collective-permute-start | bytes 2752520 | tf_op jit(solution)/shard_map/ppermute | solution.py:161
  201.7 1.0 copy-start.4
  202.8 1.0 copy-start.7
  206.7 14.9 %collective-permute-start.13 = (bf16[2,448,256]{2,1,0:T(8,128)(2,1)S(1)}, bf16[2,448,256]{2,1,0:T(8,128)(2,1)S(1)}, u32[]{:S(2)}, u32[]{:S(2)}) collective-permute-start(bf16[2,448,256]{2,1,0:T(8,128)(2,1)S(1)} %far_products.3), channel_id=1, source_target_pairs={{0,2},{2,0},{1,3},{3,1},{4,6},{6,4},{5,7},{7,5},{8,10},{10,8},{9,1... | collective-permute-start | bytes 1376264 | tf_op jit(solution)/shard_map/ppermute | solution.py:161
Sparse Core Ops, SparseCore 0:
  10.1 53.0 all-gather.3
  76.2 77.3 reduce-scatter.1

commit v4 on v3

--- a/solution.py
+++ b/solution.py
@@ -11,6 +11,7 @@
 BF16 = jnp.bfloat16
 NX, NY, NM = 4, 4, 4
 VMEM = pl.BlockSpec(memory_space=pltpu.VMEM)
+ANY = pl.BlockSpec(memory_space=pl.ANY)
 SMEM = pl.BlockSpec(memory_space=pltpu.SMEM)
 
 
@@ -26,33 +27,39 @@
     return lax.ppermute(value, axis, [((i + step) % size, i) for i in range(size)])
 
 
-def block_kernel(where_ref, *refs):
-    tokens, basis_ref, out_ref = refs[:NY], refs[NY], refs[NY + 1]
-    half = where_ref[1]
+def block_kernel(rel, where_ref, *refs):
+    tokens, basis = refs[:2], refs[2 : 2 + NX]
+    out_ref, held_ref = refs[3 + NX :]
+    here, y, half, parity = (where_ref[i] for i in range(4))
     rows = tokens[0].shape[1]
-    piece = basis_ref.shape[1] // NM
+    for side in range(2):
+
+        @pl.when(half == side)
+        def _():
+            for n in range(2):
+                source = lax.rem(y + 2 * (parity + rel) + n, NY)
+                held_ref[pl.ds(n * rows, rows)] = tokens[side][source]
+
     for j in range(NX):
-        for parity in range(2):
-            right = jnp.concatenate([tokens[2 * parity + n][half] for n in range(2)], axis=0)
-            sums = lax.dot_general(
-                basis_ref[j], right, (((1,), (1,)), ((), ())), preferred_element_type=F32
-            ).astype(BF16)
-            for m in range(NM):
-                out_ref[2 * m + parity, j] = sums[m * piece : (m + 1) * piece]
-
-
-def block_sums(where, tokens, basis):
+        home = lax.rem(here + j, NX)
+        out_ref[home] = lax.dot_general(
+            basis[j][...], held_ref[...], (((1,), (1,)), ((), ())), preferred_element_type=F32
+        ).astype(BF16)
+
+
+def block_sums(rel, where, tokens, basis, turn):
     _, rows, depth = tokens[0].shape
-    crows = basis.shape[1]
+    crows = basis[0].shape[0]
     return pl.pallas_call(
-        block_kernel,
-        out_shape=jax.ShapeDtypeStruct((2 * NM, NX, crows // NM, 2 * rows), BF16),
-        in_specs=[SMEM] + [VMEM] * (NY + 1),
+        functools.partial(block_kernel, rel),
+        out_shape=jax.ShapeDtypeStruct((NX, crows, 2 * rows), BF16),
+        in_specs=[SMEM] + [VMEM] * (2 + NX) + [ANY],
         out_specs=VMEM,
+        scratch_shapes=[pltpu.VMEM((2 * rows, depth), BF16)],
         compiler_params=params(),
-        cost_estimate=cost(2 * NX * crows * NY * rows * depth, 9 * 2**20),
+        cost_estimate=cost(2 * NX * crows * 2 * rows * depth, 6 * 2**20),
         name="block_sums",
-    )(where, *tokens, basis)
+    )(where, *tokens, *basis, turn)
 
 
 def add_products(out1, out2, first, pieces, acts, cols):
@@ -157,32 +164,42 @@
 
 
 def body(activations, act_basis, out_grads, grad_basis):
-    x, core, parity = (lax.axis_index(a) for a in ("x", "c", "p"))
+    x, y, core, parity = (lax.axis_index(a) for a in ("x", "y", "c", "p"))
     swap = lambda v, axis: lax.ppermute(v, axis, [(0, 1), (1, 0)])
     pack = lambda *v: jnp.stack(v).astype(jnp.int32)
-    basis = lax.all_gather(grad_basis, "x", axis=0, tiled=False)
-    halves = jnp.stack([out_grads, swap(out_grads, "h")])
-    tokens = [halves] + [from_rel(halves, "y", j, NY) for j in (1, 2, 3)]
-
+    gather = lambda v, axis: lax.all_gather(v, axis, axis=0, tiled=False)
     acts = lax.dot_general(
         activations, act_basis, (((1,), (1,)), ((), ())), preferred_element_type=F32
     ).astype(BF16)
-    acts = jnp.stack([acts, swap(acts, "h")])
+    depth = out_grads.shape[1]
+    payload = jnp.concatenate([out_grads, acts], axis=1)
+    crossed = swap(payload, "h")
+    turn, grad_basis, out_grads = lax.optimization_barrier(
+        (swap(payload[:16, :128], "c"), grad_basis, out_grads)
+    )
+    basis = [grad_basis] + [from_rel(grad_basis, "x", j, NX) for j in (1, 2, 3)]
+    tokens = [gather(out_grads, "y"), gather(crossed[:, :depth], "y")]
+    acts = jnp.stack([acts, crossed[:, depth:]])
+    acts = jnp.concatenate([acts, swap(acts, "p")], axis=-1)
     *tokens, acts = lax.optimization_barrier((*tokens, acts))
 
-    send = block_sums(pack(x, 1 - core), tokens, basis)
-    got = swap(send, "c")
-    mine = block_sums(pack(x, core), tokens, basis)
-    partial = added(mine, got)
-
-    acts, partial = lax.optimization_barrier((acts, partial))
-    acts = own_columns(jnp.concatenate([acts, swap(acts, "p")], axis=-1), parity)
+    here, there = pack(x, y, core, parity), pack(x, y, 1 - core, parity)
+    got = swap(block_sums(1, there, tokens, basis, turn), "c")
+    other = added(block_sums(1, here, tokens, basis, turn), got)
+    other, acts, *tokens = lax.optimization_barrier((other, acts, *tokens))
+    pair = swap(other, "p")
+    got = swap(block_sums(0, there, tokens, basis, turn), "c")
+    acts = own_columns(acts, parity)
+    partial = added(block_sums(0, here, tokens, basis, turn), got, pair)
+    partial, acts = lax.optimization_barrier((partial, acts))
     all_acts = [acts] + [from_rel(acts, "x", j, NX) for j in (1, 2, 3)]
-
-    own = lax.psum_scatter(partial, ("m", "p"), scatter_dimension=0, tiled=False)
+    crows, width = partial.shape[1:]
+    spread = lax.all_to_all(
+        partial.reshape(NX * NM, crows // NM, width), ("x", "m"), split_axis=0, concat_axis=0, tiled=True
+    ).reshape(NX, NM, crows // NM, width)
+    own = added(*[spread[:, j] for j in range(NM)])
     own, all_acts = lax.optimization_barrier((own, all_acts))
-    own = lax.all_to_all(own, "x", split_axis=0, concat_axis=0, tiled=True)
-    mine = lax.all_gather(own, "m", axis=0, tiled=False)
+    mine = gather(own, "m")
     mate = swap(mine, "c")
     where = pack(x, core)
     p1, p2 = near_products(where, mine, all_acts)

time: 230 us -> 220 us (0.957)
  blocking collectives: 36.9 us -> 61.5 us
  waiting for transfers between devices: 68.6 us -> 52.5 us
  starting transfers between devices: 86.1 us -> 70.6 us
  between operations: 14.3 us -> 1.02 us
  Pallas kernels: 10.5 us -> 16.7 us
    all_to_all x0 -> x1, waiting for transfers between devices: none -> 37.2 us  [body(): lax.all_to_all(partial.reshape(NX * NM, crows // NM, width), ('x', 'm'),...]
    all_gather x1 -> x3, blocking collectives: 27.6 us -> 61.5 us  [body(): gather = lambda v, axis: lax.all_gather(v, axis, axis=0, tiled=False)]
    ppermute x6 -> x8, starting transfers between devices: 62 us -> 37.1 us  [body(): swap = lambda v, axis: lax.ppermute(v, axis, [(0, 1), (1, 0)])]
    reduce_scatter x1 -> x0, waiting for transfers between devices: 17.8 us -> none  [body(): lax.psum_scatter(partial, ('m', 'p'), scatter_dimension=0, tiled=False)]
    ppermute x6, waiting for transfers between devices: 18.3 us -> 1.01 us  [from_rel(): lax.ppermute(value, axis, [((i + step) % size, i) for i in range(size)])]
    all_to_all x1 -> x0, blocking collectives: 9.21 us -> none  [body(): own = lax.all_to_all(own, 'x', split_axis=0, concat_axis=0, tiled=True)]
    all_to_all x0 -> x1, starting transfers between devices: none -> 9.18 us  [body(): lax.all_to_all(partial.reshape(NX * NM, crows // NM, width), ('x', 'm'),...]
    ppermute x1, waiting for transfers between devices: 6.85 us -> 0.01 us  [own_columns(): return jnp.stack([first, lax.ppermute(value, ('y', 'p'), rows)])]
  transfers between devices with their start and end apart: 16 -> 17, of which waited for: 11 -> 4; matrix products, arithmetic and copies ran while one was open for 2% -> 3% of each run, Pallas kernels for 3% -> 6%
where the time goes in v4:
time: 220 us; the launch traced here: 219 us
  starting transfers between devices  70.6 us (32%)
  blocking collectives  61.5 us (28%)
  waiting for transfers between devices  52.5 us (24%)
  Pallas kernels  16.7 us (8%)
  other arithmetic  7.44 us (3%)
  local copies, waits for them, and re-layouts  7.26 us (3%)
    all_gather x3, blocking collectives, body(): gather = lambda v, axis: lax.all_gather(v, axis, axis=0, tiled=False)  61.5 us
    all_to_all x1, waiting for transfers between devices, body(): lax.all_to_all(partial.reshape(NX * NM, crows // NM, width), ('x', 'm'),...  37.2 us
    ppermute x8, starting transfers between devices, body(): swap = lambda v, axis: lax.ppermute(v, axis, [(0, 1), (1, 0)])  37.1 us
    ppermute x6, starting transfers between devices, from_rel(): lax.ppermute(value, axis, [((i + step) % size, i) for i in range(size)])  18.7 us
    ppermute x8, waiting for transfers between devices, body(): swap = lambda v, axis: lax.ppermute(v, axis, [(0, 1), (1, 0)])  14.3 us
    pallas_call x4, Pallas kernels, block_sums(): pl.pallas_call(functools.partial(block_kernel, rel), out_shape=jax.ShapeD...  10.6 us
    all_to_all x1, starting transfers between devices, body(): lax.all_to_all(partial.reshape(NX * NM, crows // NM, width), ('x', 'm'),...  9.18 us
    ppermute x1, starting transfers between devices, own_columns(): return jnp.stack([first, lax.ppermute(value, ('y', 'p'), rows)])  4.91 us
  transfers between devices with their start and end apart: 17, of which 4 were waited for; matrix products, arithmetic and copies ran while one was open for 3% of the time, Pallas kernels for 6%

profile of v4, /device:TPU:1, one launch (start us, length us, event | category | flops | bytes accessed | tf_op | source)
XLA Modules:
  0.0 219.1 jit_solution(4692172568700962451)
XLA Ops:
  0.6 0.0 copy-start
  0.6 0.0 copy-start.9
  0.7 0.8 slice.27
  1.5 8.8 %collective-permute-start = (bf16[16,128]{1,0:T(8,128)(2,1)S(1)}, bf16[16,128]{1,0:T(8,128)(2,1)S(1)}, u32[]{:S(2)}, u32[]{:S(2)}) collective-permute-start(bf16[16,128]{1,0:T(8,128)(2,1)S(1)} %slice.27), channel_id=1, source_target_pairs={{0,1},{1,0},{2,3},{3,2},{4,5},{5,4},{6,7},{7,6},{8,9},{9,8},{10,11... | collective-permute-start | bytes 12296 | tf_op jit(solution)/shard_map/ppermute | solution.py:168
  10.3 2.1 convolution_convert_fusion
  12.4 0.7 pad_maximum_fusion.1
  13.1 10.1 %collective-permute-start.1 = (bf16[128,1152]{1,0:T(8,128)(2,1)}, bf16[128,1152]{1,0:T(8,128)(2,1)}, u32[]{:S(2)}, u32[]{:S(2)}) collective-permute-start(bf16[128,1152]{1,0:T(8,128)(2,1)} %pad_maximum_fusion.1), channel_id=1, source_target_pairs={{0,64},{64,0},{1,65},{65,1},{2,66},{66,2},{3,67},{67,3},{4,68},{68... | collective-permute-start | bytes 884744 | tf_op jit(solution)/shard_map/ppermute | solution.py:168
  23.2 0.1 add_add_fusion.1.where_ref
  23.3 0.0 collective-permute-done.refs_6_
  23.3 4.4 %collective-permute-start.3 = (bf16[448,896]{1,0:T(8,128)(2,1)}, bf16[448,896]{1,0:T(8,128)(2,1)S(1)}, u32[]{:S(2)}, u32[]{:S(2)}) collective-permute-start(bf16[448,896]{1,0:T(8,128)(2,1)} %refs_2_.3), channel_id=1, source_target_pairs={{16,0},{32,16},{48,32},{0,48},{17,1},{33,17},{49,33},{1,49},{18,2}... | collective-permute-start | bytes 2408456 | tf_op jit(solution)/shard_map/ppermute | solution.py:27
  27.7 2.4 %collective-permute-start.4 = (bf16[448,896]{1,0:T(8,128)(2,1)}, bf16[448,896]{1,0:T(8,128)(2,1)S(1)}, u32[]{:S(2)}, u32[]{:S(2)}) collective-permute-start(bf16[448,896]{1,0:T(8,128)(2,1)} %refs_2_.3), channel_id=1, source_target_pairs={{32,0},{48,16},{0,32},{16,48},{33,1},{49,17},{1,33},{17,49},{34,2}... | collective-permute-start | bytes 2408456 | tf_op jit(solution)/shard_map/ppermute | solution.py:27
  30.1 2.5 %collective-permute-start.5 = (bf16[448,896]{1,0:T(8,128)(2,1)}, bf16[448,896]{1,0:T(8,128)(2,1)S(1)}, u32[]{:S(2)}, u32[]{:S(2)}) collective-permute-start(bf16[448,896]{1,0:T(8,128)(2,1)} %refs_2_.3), channel_id=1, source_target_pairs={{48,0},{0,16},{16,32},{32,48},{49,1},{1,17},{17,33},{33,49},{50,2}... | collective-permute-start | bytes 2408456 | tf_op jit(solution)/shard_map/ppermute | solution.py:27
  32.6 13.5 %all-gather = bf16[512,896]{1,0:T(8,128)(2,1)S(1)} all-gather(bf16[128,896]{1,0:T(8,128)(2,1)S(1)} %copy-done.9), channel_id=2, replica_groups=mesh['y'=4,'h'=2,'x'=4,'m'=4,'p'=2,'c'=2] {'y'}, dimensions={0}, use_global_device_ids=true | all-gather | bytes 1146880 | tf_op jit(solution)/shard_map/all_gather | solution.py:170
  46.1 0.0 collective-permute-done.1
  46.1 0.8 slice_bitcast_fusion.2
  47.0 5.8 %collective-permute-start.2 = (bf16[2,128,256]{2,1,0:T(8,128)(2,1)S(1)}, bf16[2,128,256]{2,1,0:T(8,128)(2,1)S(1)}, u32[]{:S(2)}, u32[]{:S(2)}) collective-permute-start(bf16[2,128,256]{2,1,0:T(8,128)(2,1)S(1)} %pad_maximum_fusion.3), channel_id=1, source_target_pairs={{0,2},{2,0},{1,3},{3,1},{4,6},{6,4},{5,7},{7,5},{8,10},{10,8},{9,1... | collective-permute-start | bytes 393224 | tf_op jit(solution)/shard_map/ppermute | solution.py:168
  52.7 1.0 slice.36
  53.7 13.5 %all-gather.1 = bf16[512,896]{1,0:T(8,128)(2,1)S(1)} all-gather(bf16[128,896]{1,0:T(8,128)(2,1)S(1)} %slice.36), channel_id=3, replica_groups=mesh['y'=4,'h'=2,'x'=4,'m'=4,'p'=2,'c'=2] {'y'}, dimensions={0}, use_global_device_ids=true | all-gather | bytes 1146880 | tf_op jit(solution)/shard_map/all_gather | solution.py:170
  67.2 0.0 collective-permute-done.2
  67.2 0.0 collective-permute-done.3.refs_3_
  67.3 0.0 collective-permute-done.4.refs_4_
  67.3 0.0 copy-start.5
  67.3 1.0 collective-permute-done.5.refs_5_
  68.3 2.6 %block_sums.5 = bf16[4,448,256]{2,1,0:T(8,128)(2,1)S(1)} custom-call(s32[4]{0:T(128)S(1)} %add_add_fusion.1.where_ref, bf16[4,128,896]{2,1,0:T(8,128)(2,1)S(1)} %bitcast.30, bf16[4,128,896]{2,1,0:T(8,128)(2,1)S(1)} %bitcast.34, bf16[448,896]{1,0:T(8,128)(2,1)} %refs_2_.3, bf16[448,896]{1,0:T(8,128)(2,1)S(1)} %collective-permute-done.3.refs_3_, ...), custom_call_target="tpu_custom_call" | custom-call | flops 822083584 | bytes 6291456 | tf_op jit(solution)/shard_map/block_sums/pallas_call | solution.py:53
  70.9 3.2 %collective-permute-start.6 = (bf16[4,448,256]{2,1,0:T(8,128)(2,1)S(1)}, bf16[4,448,256]{2,1,0:T(8,128)(2,1)S(1)}, u32[]{:S(2)}, u32[]{:S(2)}) collective-permute-start(bf16[4,448,256]{2,1,0:T(8,128)(2,1)S(1)} %block_sums.5), channel_id=1, source_target_pairs={{0,1},{1,0},{2,3},{3,2},{4,5},{5,4},{6,7},{7,6},{8,9},{9,8},{10,11... | collective-permute-start | bytes 2752520 | tf_op jit(solution)/shard_map/ppermute | solution.py:168
  74.1 0.1 add_add_fusion.where_ref
  74.2 2.4 %block_sums.4 = bf16[4,448,256]{2,1,0:T(8,128)(2,1)S(1)} custom-call(s32[4]{0:T(128)S(1)} %add_add_fusion.where_ref, bf16[4,128,896]{2,1,0:T(8,128)(2,1)S(1)} %bitcast.31, bf16[4,128,896]{2,1,0:T(8,128)(2,1)S(1)} %bitcast.35, bf16[448,896]{1,0:T(8,128)(2,1)} %refs_2_.3, bf16[448,896]{1,0:T(8,128)(2,1)S(1)} %collective-permute-done.3.refs_3_, ...), custom_call_target="tpu_custom_call" | custom-call | flops 822083584 | bytes 6291456 | tf_op jit(solution)/shard_map/block_sums/pallas_call | solution.py:53
  76.6 0.0 collective-permute-done.6
  76.6 1.2 add_convert_fusion.1
  77.8 1.9 collective-permute-start.8
  79.8 3.3 %block_sums.7 = bf16[4,448,256]{2,1,0:T(8,128)(2,1)} custom-call(s32[4]{0:T(128)S(1)} %add_add_fusion.1.where_ref, bf16[4,128,896]{2,1,0:T(8,128)(2,1)S(1)} %bitcast.32, bf16[4,128,896]{2,1,0:T(8,128)(2,1)S(1)} %bitcast.36, bf16[448,896]{1,0:T(8,128)(2,1)} %refs_2_.3, bf16[448,896]{1,0:T(8,128)(2,1)S(1)} %collective-permute-done.3.refs_3_, ...), custom_call_target="tpu_custom_call" | custom-call | flops 822083584 | bytes 6291456 | tf_op jit(solution)/shard_map/block_sums/pallas_call | solution.py:53
  83.0 2.2 collective-permute-start.7
  85.2 0.7 collective-permute-start.9
  85.9 4.9 %collective-permute-start.10 = (bf16[2,128,512]{2,1,0:T(8,128)(2,1)S(1)}, bf16[2,128,512]{2,1,0:T(8,128)(2,1)S(1)}, u32[]{:S(2)}, u32[]{:S(2)}) collective-permute-start(bf16[2,128,512]{2,1,0:T(8,128)(2,1)S(1)} %pad_maximum_fusion.2), channel_id=1, source_target_pairs={{128,0},{386,2},{256,128},{2,130},{384,256},{130,258},{0,384},{258... | collective-permute-start | bytes 786440 | tf_op jit(solution)/shard_map/ppermute | solution.py:163
  90.8 1.2 copy-done.2
  92.0 1.1 copy-done.4
  93.1 1.1 copy-done.6
  94.3 1.1 copy-done.8
  95.4 2.3 %block_sums.6 = bf16[4,448,256]{2,1,0:T(8,128)(2,1)S(1)} custom-call(s32[4]{0:T(128)S(1)} %add_add_fusion.where_ref, bf16[4,128,896]{2,1,0:T(8,128)(2,1)S(1)} %bitcast.33, bf16[4,128,896]{2,1,0:T(8,128)(2,1)S(1)} %bitcast.37, bf16[448,896]{1,0:T(8,128)(2,1)} %refs_2_.3, bf16[448,896]{1,0:T(8,128)(2,1)S(1)} %copy-done.4, bf16[448,896]{1,0:T(8,128)(2,1)S(1)} %copy-done.6, ...), custom_call_target="tpu_custom_call" | custom-call | flops 822083584 | bytes 6291456 | tf_op jit(solution)/shard_map/block_sums/pallas_call | solution.py:53
  97.8 0.0 collective-permute-done.9
  97.8 0.0 collective-permute-done.10
  97.8 0.1 pad_maximum_fusion.refs_0_
  97.9 4.1 %collective-permute-done.8 = bf16[4,448,256]{2,1,0:T(8,128)(2,1)} collective-permute-done((bf16[4,448,256]{2,1,0:T(8,128)(2,1)}, bf16[4,448,256]{2,1,0:T(8,128)(2,1)}, u32[]{:S(2)}, u32[]{:S(2)}) %collective-permute-start.8) | collective-permute-done | bytes 917536 | tf_op jit(solution)/shard_map/ppermute | solution.py:168
  102.0 0.0 collective-permute-done.7
  102.0 2.7 %add_convert_fusion = bf16[4,448,256]{2,1,0:T(8,128)(2,1)} fusion(bf16[4,448,256]{2,1,0:T(8,128)(2,1)} %collective-permute-done.8, bf16[4,448,256]{2,1,0:T(8,128)(2,1)} %collective-permute-done.7, bf16[4,448,256]{2,1,0:T(8,128)(2,1)S(1)} %block_sums.6), kind=kLoop, calls=%fused_computation | loop fusion | flops 2752512 | bytes 3670016 | tf_op jit(solution)/shard_map/convert_element_type | solution.py:156
  104.7 9.2 %all-to-all-start = ((bf16[16,112,256]{2,1,0:T(8,128)(2,1)}), bf16[16,112,256]{2,1,0:T(8,128)(2,1)}, u32[]{:S(2)}, u32[]{:S(2)}) async-start(bf16[16,112,256]{2,1,0:T(8,128)(2,1)} %bitcast.11), calls=%async_computation | async-start | bytes 1835008 | tf_op jit(solution)/shard_map/all_to_all | solution.py:197
  113.9 4.4 %collective-permute-start.11 = (bf16[2,2,128,512]{3,2,1,0:T(8,128)(2,1)S(1)}, bf16[2,2,128,512]{3,2,1,0:T(8,128)(2,1)S(1)}, u32[]{:S(2)}, u32[]{:S(2)}) collective-permute-start(bf16[2,2,128,512]{3,2,1,0:T(8,128)(2,1)S(1)} %pad_maximum_fusion.refs_0_), channel_id=1, source_target_pairs={{16,0},{32,16},{48,32},{0,48},{17,1},{33,17},{49,33},{1,49},{18,2}... | collective-permute-start | bytes 1572872 | tf_op jit(solution)/shard_map/ppermute | solution.py:27
  118.4 2.5 %collective-permute-start.12 = (bf16[2,2,128,512]{3,2,1,0:T(8,128)(2,1)S(1)}, bf16[2,2,128,512]{3,2,1,0:T(8,128)(2,1)}, u32[]{:S(2)}, u32[]{:S(2)}) collective-permute-start(bf16[2,2,128,512]{3,2,1,0:T(8,128)(2,1)S(1)} %pad_maximum_fusion.refs_0_), channel_id=1, source_target_pairs={{32,0},{48,16},{0,32},{16,48},{33,1},{49,17},{1,33},{17,49},{34,2}... | collective-permute-start | bytes 1572872 | tf_op jit(solution)/shard_map/ppermute | solution.py:27
  120.8 2.5 %collective-permute-start.13 = (bf16[2,2,128,512]{3,2,1,0:T(8,128)(2,1)S(1)}, bf16[2,2,128,512]{3,2,1,0:T(8,128)(2,1)}, u32[]{:S(2)}, u32[]{:S(2)}) collective-permute-start(bf16[2,2,128,512]{3,2,1,0:T(8,128)(2,1)S(1)} %pad_maximum_fusion.refs_0_), channel_id=1, source_target_pairs={{48,0},{0,16},{16,32},{32,48},{49,1},{1,17},{17,33},{33,49},{50,2}... | collective-permute-start | bytes 1572872 | tf_op jit(solution)/shard_map/ppermute | solution.py:27
  123.3 37.2 %all-to-all-done = bf16[16,112,256]{2,1,0:T(8,128)(2,1)} async-done(((bf16[16,112,256]{2,1,0:T(8,128)(2,1)}), bf16[16,112,256]{2,1,0:T(8,128)(2,1)}, u32[]{:S(2)}, u32[]{:S(2)}) %all-to-all-start) | async-done | bytes 917536 | tf_op jit(solution)/shard_map/all_to_all | solution.py:197
  160.5 1.4 fusion
  161.9 0.0 collective-permute-done.11.refs_1_
  161.9 0.0 collective-permute-done.12.refs_2_
  161.9 0.0 collective-permute-done.13.refs_3_
  162.0 34.5 %all-gather.2 = bf16[16,112,256]{2,1,0:T(8,128)(2,1)S(1)} all-gather(bf16[4,112,256]{2,1,0:T(8,128)(2,1)S(1)} %fusion), channel_id=4, replica_groups=mesh['y'=4,'h'=2,'x'=4,'m'=4,'p'=2,'c'=2] {'m'}, dimensions={0}, use_global_device_ids=true | all-gather | bytes 1146880 | tf_op jit(solution)/shard_map/all_gather | solution.py:170
  196.4 3.3 %collective-permute-start.14 = (bf16[4,4,112,256]{3,2,1,0:T(8,128)(2,1)S(1)}, bf16[4,4,112,256]{3,2,1,0:T(8,128)(2,1)S(1)}, u32[]{:S(2)}, u32[]{:S(2)}) collective-permute-start(bf16[4,4,112,256]{3,2,1,0:T(8,128)(2,1)S(1)} %bitcast.38), channel_id=1, source_target_pairs={{0,1},{1,0},{2,3},{3,2},{4,5},{5,4},{6,7},{7,6},{8,9},{9,8},{10,11... | collective-permute-start | bytes 2752520 | tf_op jit(solution)/shard_map/ppermute | solution.py:168
  199.7 0.1 pad_add_fusion.where_ref
  199.8 2.3 %near_products.1 = (f32[448,512]{1,0:T(8,128)S(1)}, f32[448,512]{1,0:T(8,128)S(1)}) custom-call(s32[2]{0:T(128)S(1)} %pad_add_fusion.where_ref, bf16[4,4,112,256]{3,2,1,0:T(8,128)(2,1)S(1)} %bitcast.39, bf16[2,2,128,512]{3,2,1,0:T(8,128)(2,1)S(1)} %pad_maximum_fusion.refs_0_, bf16[2,2,128,512]{3,2,1,0:T(8,128)(2,1)S(1)} %collective-permute-done.11.refs_1_, ...), custom_call_target="tpu_custom_call" | custom-call | flops 939524096 | bytes 5242880 | tf_op jit(solution)/shard_map/near_products/pallas_call | solution.py:126
  202.2 0.0 collective-permute-done.14.mate_ref
  202.2 1.9 far_products.3
  204.0 1.9 collective-permute-start.15
  206.0 1.9 far_products.2
  207.9 10.2 %collective-permute-done.15 = bf16[2,448,256]{2,1,0:T(8,128)(2,1)S(1)} collective-permute-done((bf16[2,448,256]{2,1,0:T(8,128)(2,1)S(1)}, bf16[2,448,256]{2,1,0:T(8,128)(2,1)S(1)}, u32[]{:S(2)}, u32[]{:S(2)}) %collective-permute-start.15) | collective-permute-done | bytes 458784 | tf_op jit(solution)/shard_map/ppermute | solution.py:168
  218.1 1.0 convert_add_fusion
  (16 shorter events, 0.1 us)
Async XLA Ops:
  0.6 9.7 %copy-start = (bf16[256,4096]{1,0:T(8,128)(2,1)S(1)}, bf16[256,4096]{1,0:T(8,128)(2,1)}, u32[]{:S(2)}) copy-start(bf16[256,4096]{1,0:T(8,128)(2,1)} %param.5) | copy-start | bytes 6291460
  0.6 11.7 %copy-start.9 = (bf16[128,896]{1,0:T(8,128)(2,1)S(1)}, bf16[128,896]{1,0:T(8,128)(2,1)}, u32[]{:S(2)}) copy-start(bf16[128,896]{1,0:T(8,128)(2,1)} %param.6) | copy-start | bytes 688132
  1.5 21.8 %collective-permute-start = (bf16[16,128]{1,0:T(8,128)(2,1)S(1)}, bf16[16,128]{1,0:T(8,128)(2,1)S(1)}, u32[]{:S(2)}, u32[]{:S(2)}) collective-permute-start(bf16[16,128]{1,0:T(8,128)(2,1)S(1)} %slice.27), channel_id=1, source_target_pairs={{0,1},{1,0},{2,3},{3,2},{4,5},{5,4},{6,7},{7,6},{8,9},{9,8},{10,11... | collective-permute-start | bytes 12296 | tf_op jit(solution)/shard_map/ppermute | solution.py:168
  13.1 33.0 %collective-permute-start.1 = (bf16[128,1152]{1,0:T(8,128)(2,1)}, bf16[128,1152]{1,0:T(8,128)(2,1)}, u32[]{:S(2)}, u32[]{:S(2)}) collective-permute-start(bf16[128,1152]{1,0:T(8,128)(2,1)} %pad_maximum_fusion.1), channel_id=1, source_target_pairs={{0,64},{64,0},{1,65},{65,1},{2,66},{66,2},{3,67},{67,3},{4,68},{68... | collective-permute-start | bytes 884744 | tf_op jit(solution)/shard_map/ppermute | solution.py:168
  23.3 44.0 %collective-permute-start.3 = (bf16[448,896]{1,0:T(8,128)(2,1)}, bf16[448,896]{1,0:T(8,128)(2,1)S(1)}, u32[]{:S(2)}, u32[]{:S(2)}) collective-permute-start(bf16[448,896]{1,0:T(8,128)(2,1)} %refs_2_.3), channel_id=1, source_target_pairs={{16,0},{32,16},{48,32},{0,48},{17,1},{33,17},{49,33},{1,49},{18,2}... | collective-permute-start | bytes 2408456 | tf_op jit(solution)/shard_map/ppermute | solution.py:27
  27.7 39.6 %collective-permute-start.4 = (bf16[448,896]{1,0:T(8,128)(2,1)}, bf16[448,896]{1,0:T(8,128)(2,1)S(1)}, u32[]{:S(2)}, u32[]{:S(2)}) collective-permute-start(bf16[448,896]{1,0:T(8,128)(2,1)} %refs_2_.3), channel_id=1, source_target_pairs={{32,0},{48,16},{0,32},{16,48},{33,1},{49,17},{1,33},{17,49},{34,2}... | collective-permute-start | bytes 2408456 | tf_op jit(solution)/shard_map/ppermute | solution.py:27
  30.1 38.2 %collective-permute-start.5 = (bf16[448,896]{1,0:T(8,128)(2,1)}, bf16[448,896]{1,0:T(8,128)(2,1)S(1)}, u32[]{:S(2)}, u32[]{:S(2)}) collective-permute-start(bf16[448,896]{1,0:T(8,128)(2,1)} %refs_2_.3), channel_id=1, source_target_pairs={{48,0},{0,16},{16,32},{32,48},{49,1},{1,17},{17,33},{33,49},{50,2}... | collective-permute-start | bytes 2408456 | tf_op jit(solution)/shard_map/ppermute | solution.py:27
  47.0 20.3 %collective-permute-start.2 = (bf16[2,128,256]{2,1,0:T(8,128)(2,1)S(1)}, bf16[2,128,256]{2,1,0:T(8,128)(2,1)S(1)}, u32[]{:S(2)}, u32[]{:S(2)}) collective-permute-start(bf16[2,128,256]{2,1,0:T(8,128)(2,1)S(1)} %pad_maximum_fusion.3), channel_id=1, source_target_pairs={{0,2},{2,0},{1,3},{3,1},{4,6},{6,4},{5,7},{7,5},{8,10},{10,8},{9,1... | collective-permute-start | bytes 393224 | tf_op jit(solution)/shard_map/ppermute | solution.py:168
  67.2 12.5 %copy-start.1 = (bf16[512,896]{1,0:T(8,128)(2,1)}, bf16[512,896]{1,0:T(8,128)(2,1)S(1)}, u32[]{:S(2)}) copy-start(bf16[512,896]{1,0:T(8,128)(2,1)S(1)} %all-gather.1) | copy-start | bytes 2752516
  67.2 12.5 %copy-start.3 = (bf16[448,896]{1,0:T(8,128)(2,1)}, bf16[448,896]{1,0:T(8,128)(2,1)S(1)}, u32[]{:S(2)}) copy-start(bf16[448,896]{1,0:T(8,128)(2,1)S(1)} %collective-permute-done.3.refs_3_) | copy-start | bytes 2408452
  67.3 12.5 %copy-start.5 = (bf16[448,896]{1,0:T(8,128)(2,1)}, bf16[448,896]{1,0:T(8,128)(2,1)S(1)}, u32[]{:S(2)}) copy-start(bf16[448,896]{1,0:T(8,128)(2,1)S(1)} %collective-permute-done.4.refs_4_) | copy-start | bytes 2408452
  68.3 11.5 %copy-start.7 = (bf16[448,896]{1,0:T(8,128)(2,1)}, bf16[448,896]{1,0:T(8,128)(2,1)S(1)}, u32[]{:S(2)}) copy-start(bf16[448,896]{1,0:T(8,128)(2,1)S(1)} %collective-permute-done.5.refs_5_) | copy-start | bytes 2408452
  70.9 5.7 %collective-permute-start.6 = (bf16[4,448,256]{2,1,0:T(8,128)(2,1)S(1)}, bf16[4,448,256]{2,1,0:T(8,128)(2,1)S(1)}, u32[]{:S(2)}, u32[]{:S(2)}) collective-permute-start(bf16[4,448,256]{2,1,0:T(8,128)(2,1)S(1)} %block_sums.5), channel_id=1, source_target_pairs={{0,1},{1,0},{2,3},{3,2},{4,5},{5,4},{6,7},{7,6},{8,9},{9,8},{10,11... | collective-permute-start | bytes 2752520 | tf_op jit(solution)/shard_map/ppermute | solution.py:168
  77.8 24.2 %collective-permute-start.8 = (bf16[4,448,256]{2,1,0:T(8,128)(2,1)}, bf16[4,448,256]{2,1,0:T(8,128)(2,1)}, u32[]{:S(2)}, u32[]{:S(2)}) collective-permute-start(bf16[4,448,256]{2,1,0:T(8,128)(2,1)} %add_convert_fusion.1), channel_id=1, source_target_pairs={{0,2},{2,0},{1,3},{3,1},{4,6},{6,4},{5,7},{7,5},{8,10},{10,8},{9,1... | collective-permute-start | bytes 2752520 | tf_op jit(solution)/shard_map/ppermute | solution.py:168
  83.0 18.9 %collective-permute-start.7 = (bf16[4,448,256]{2,1,0:T(8,128)(2,1)}, bf16[4,448,256]{2,1,0:T(8,128)(2,1)}, u32[]{:S(2)}, u32[]{:S(2)}) collective-permute-start(bf16[4,448,256]{2,1,0:T(8,128)(2,1)} %block_sums.7), channel_id=1, source_target_pairs={{0,1},{1,0},{2,3},{3,2},{4,5},{5,4},{6,7},{7,6},{8,9},{9,8},{10,11... | collective-permute-start | bytes 2752520 | tf_op jit(solution)/shard_map/ppermute | solution.py:168
  85.2 12.6 %collective-permute-start.9 = (bf16[2,128,512]{2,1,0:T(8,128)(2,1)S(1)}, bf16[2,128,512]{2,1,0:T(8,128)(2,1)S(1)}, u32[]{:S(2)}, u32[]{:S(2)}) collective-permute-start(bf16[2,128,512]{2,1,0:T(8,128)(2,1)S(1)} %pad_maximum_fusion.2), channel_id=1, source_target_pairs={{258,2},{386,130},{2,258},{130,386},{259,3},{387,131},{3,259},{131... | collective-permute-start | bytes 786440 | tf_op jit(solution)/shard_map/ppermute | solution.py:161
  85.9 11.9 %collective-permute-start.10 = (bf16[2,128,512]{2,1,0:T(8,128)(2,1)S(1)}, bf16[2,128,512]{2,1,0:T(8,128)(2,1)S(1)}, u32[]{:S(2)}, u32[]{:S(2)}) collective-permute-start(bf16[2,128,512]{2,1,0:T(8,128)(2,1)S(1)} %pad_maximum_fusion.2), channel_id=1, source_target_pairs={{128,0},{386,2},{256,128},{2,130},{384,256},{130,258},{0,384},{258... | collective-permute-start | bytes 786440 | tf_op jit(solution)/shard_map/ppermute | solution.py:163
  90.8 1.2 copy-start.2
  92.0 1.1 copy-start.4
  93.1 1.1 copy-start.6
  94.3 1.1 copy-start.8
  104.7 55.8 %all-to-all-start = ((bf16[16,112,256]{2,1,0:T(8,128)(2,1)}), bf16[16,112,256]{2,1,0:T(8,128)(2,1)}, u32[]{:S(2)}, u32[]{:S(2)}) async-start(bf16[16,112,256]{2,1,0:T(8,128)(2,1)} %bitcast.11), calls=%async_computation | async-start | bytes 1835008 | tf_op jit(solution)/shard_map/all_to_all | solution.py:197
  113.9 48.0 %collective-permute-start.11 = (bf16[2,2,128,512]{3,2,1,0:T(8,128)(2,1)S(1)}, bf16[2,2,128,512]{3,2,1,0:T(8,128)(2,1)S(1)}, u32[]{:S(2)}, u32[]{:S(2)}) collective-permute-start(bf16[2,2,128,512]{3,2,1,0:T(8,128)(2,1)S(1)} %pad_maximum_fusion.refs_0_), channel_id=1, source_target_pairs={{16,0},{32,16},{48,32},{0,48},{17,1},{33,17},{49,33},{1,49},{18,2}... | collective-permute-start | bytes 1572872 | tf_op jit(solution)/shard_map/ppermute | solution.py:27
  118.4 43.6 %collective-permute-start.12 = (bf16[2,2,128,512]{3,2,1,0:T(8,128)(2,1)S(1)}, bf16[2,2,128,512]{3,2,1,0:T(8,128)(2,1)}, u32[]{:S(2)}, u32[]{:S(2)}) collective-permute-start(bf16[2,2,128,512]{3,2,1,0:T(8,128)(2,1)S(1)} %pad_maximum_fusion.refs_0_), channel_id=1, source_target_pairs={{32,0},{48,16},{0,32},{16,48},{33,1},{49,17},{1,33},{17,49},{34,2}... | collective-permute-start | bytes 1572872 | tf_op jit(solution)/shard_map/ppermute | solution.py:27
  120.8 41.1 %collective-permute-start.13 = (bf16[2,2,128,512]{3,2,1,0:T(8,128)(2,1)S(1)}, bf16[2,2,128,512]{3,2,1,0:T(8,128)(2,1)}, u32[]{:S(2)}, u32[]{:S(2)}) collective-permute-start(bf16[2,2,128,512]{3,2,1,0:T(8,128)(2,1)S(1)} %pad_maximum_fusion.refs_0_), channel_id=1, source_target_pairs={{48,0},{0,16},{16,32},{32,48},{49,1},{1,17},{17,33},{33,49},{50,2}... | collective-permute-start | bytes 1572872 | tf_op jit(solution)/shard_map/ppermute | solution.py:27
  196.4 5.7 %collective-permute-start.14 = (bf16[4,4,112,256]{3,2,1,0:T(8,128)(2,1)S(1)}, bf16[4,4,112,256]{3,2,1,0:T(8,128)(2,1)S(1)}, u32[]{:S(2)}, u32[]{:S(2)}) collective-permute-start(bf16[4,4,112,256]{3,2,1,0:T(8,128)(2,1)S(1)} %bitcast.38), channel_id=1, source_target_pairs={{0,1},{1,0},{2,3},{3,2},{4,5},{5,4},{6,7},{7,6},{8,9},{9,8},{10,11... | collective-permute-start | bytes 2752520 | tf_op jit(solution)/shard_map/ppermute | solution.py:168
  204.0 14.0 %collective-permute-start.15 = (bf16[2,448,256]{2,1,0:T(8,128)(2,1)S(1)}, bf16[2,448,256]{2,1,0:T(8,128)(2,1)S(1)}, u32[]{:S(2)}, u32[]{:S(2)}) collective-permute-start(bf16[2,448,256]{2,1,0:T(8,128)(2,1)S(1)} %far_products.3), channel_id=1, source_target_pairs={{0,2},{2,0},{1,3},{3,1},{4,6},{6,4},{5,7},{7,5},{8,10},{10,8},{9,1... | collective-permute-start | bytes 1376264 | tf_op jit(solution)/shard_map/ppermute | solution.py:168

commit v5 on v4

--- a/solution.py
+++ b/solution.py
@@ -37,7 +37,7 @@
         @pl.when(half == side)
         def _():
             for n in range(2):
-                source = lax.rem(y + 2 * (parity + rel) + n, NY)
+                source = lax.rem(y + lax.rem(parity + rel, 2) + 2 * n, NY)
                 held_ref[pl.ds(n * rows, rows)] = tokens[side][source]
 
     for j in range(NX):
@@ -82,26 +82,21 @@
     return lambda j: ref[:, j].reshape(pairs * piece, width)
 
 
-def acts_of(refs, here, half):
-    rows, cols = refs[0].shape[2:]
-
-    def at(j):
-        return refs[j][:, half].reshape(2 * rows, cols)
-
-    return at
+def acts_of(refs, half):
+    return lambda j: jnp.concatenate([r[j, half] for r in refs], axis=0)
 
 
 def near_kernel(where_ref, mine_ref, *refs):
-    acts, (p1_ref, p2_ref) = refs[:NX], refs[NX:]
+    acts, (p1_ref, p2_ref) = refs[:2], refs[2:]
     here, core = where_ref[0], where_ref[1]
     side = pieces_of(mine_ref)
     add_products(
-        p1_ref, p2_ref, True, lambda j: side(lax.rem(here + j, NX)), acts_of(acts, here, core), slice(None)
+        p1_ref, p2_ref, True, lambda j: side(lax.rem(here + j, NX)), acts_of(acts, core), slice(None)
     )
 
 
 def far_kernel(keep, where_ref, mate_ref, p1_ref, p2_ref, *refs):
-    acts, outs = refs[:NX], refs[NX:]
+    acts, outs = refs[:2], refs[2:]
     acc1, acc2 = outs[-2:]
     here, core = where_ref[0], where_ref[1]
     half = acc1.shape[1]
@@ -110,7 +105,7 @@
     acc2[...] = p2_ref[:, cols]
     side = pieces_of(mate_ref)
     add_products(
-        acc1, acc2, False, lambda j: side(lax.rem(here + j, NX)), acts_of(acts, here, 1 - core), cols
+        acc1, acc2, False, lambda j: side(lax.rem(here + j, NX)), acts_of(acts, 1 - core), cols
     )
     total = 2 * NY * NX * acts[0].shape[2]
     if keep:
@@ -126,7 +121,7 @@
     return pl.pallas_call(
         near_kernel,
         out_shape=(shape, shape),
-        in_specs=[SMEM] + [VMEM] * (1 + NX),
+        in_specs=[SMEM] + [VMEM] * 3,
         out_specs=(VMEM, VMEM),
         compiler_params=params(),
         cost_estimate=cost(4 * 448 * 1024 * 512, 5 * 2**20),
@@ -140,7 +135,7 @@
     return pl.pallas_call(
         functools.partial(far_kernel, keep),
         out_shape=(shape, shape) if keep else jax.ShapeDtypeStruct((2, crows, cols // 2), BF16),
-        in_specs=[SMEM] + [VMEM] * (3 + NX),
+        in_specs=[SMEM] + [VMEM] * 5,
         out_specs=(VMEM, VMEM) if keep else VMEM,
         scratch_shapes=[] if keep else [pltpu.VMEM((crows, cols // 2), F32)] * 2,
         compiler_params=params(),
@@ -157,10 +152,10 @@
 
 
 def own_columns(value, parity):
-    rows = [((i + 2) % NY * 2 + 1, i * 2 + 1) for i in range(NY)]
+    rows = [((i + 1) % NY * 2 + 1, i * 2 + 1) for i in range(NY)]
     first = jnp.where(parity == 0, value, lax.ppermute(value, ("y", "p"), rows))
-    rows = [((i + 1 + 2 * p) % NY * 2 + p, i * 2 + p) for i in range(NY) for p in range(2)]
-    return jnp.stack([first, lax.ppermute(value, ("y", "p"), rows)])
+    rows = [((i + 2 + p) % NY * 2 + p, i * 2 + p) for i in range(NY) for p in range(2)]
+    return [first, lax.ppermute(value, ("y", "p"), rows)]
 
 
 def body(activations, act_basis, out_grads, grad_basis):
@@ -175,7 +170,7 @@
     payload = jnp.concatenate([out_grads, acts], axis=1)
     crossed = swap(payload, "h")
     turn, grad_basis, out_grads = lax.optimization_barrier(
-        (swap(payload[:16, :128], "c"), grad_basis, out_grads)
+        (swap(acts[:16, :128], "c"), grad_basis, out_grads)
     )
     basis = [grad_basis] + [from_rel(grad_basis, "x", j, NX) for j in (1, 2, 3)]
     tokens = [gather(out_grads, "y"), gather(crossed[:, :depth], "y")]
@@ -189,10 +184,10 @@
     other, acts, *tokens = lax.optimization_barrier((other, acts, *tokens))
     pair = swap(other, "p")
     got = swap(block_sums(0, there, tokens, basis, turn), "c")
-    acts = own_columns(acts, parity)
+    acts = jnp.stack([acts] + [from_rel(acts, "x", j, NX) for j in (1, 2, 3)])
     partial = added(block_sums(0, here, tokens, basis, turn), got, pair)
     partial, acts = lax.optimization_barrier((partial, acts))
-    all_acts = [acts] + [from_rel(acts, "x", j, NX) for j in (1, 2, 3)]
+    all_acts = own_columns(acts, parity)
     crows, width = partial.shape[1:]
     spread = lax.all_to_all(
         partial.reshape(NX * NM, crows // NM, width), ("x", "m"), split_axis=0, concat_axis=0, tiled=True

time: 220 us -> 219 us (level)
  waiting for transfers between devices: 52.5 us -> 61.7 us
  blocking collectives: 61.5 us -> 54.5 us
  starting transfers between devices: 70.6 us -> 76.3 us
  local copies, waits for them, and re-layouts: 7.26 us -> 1.62 us
  Pallas kernels: 16.7 us -> 13.1 us
    ppermute x6, waiting for transfers between devices: 1.01 us -> 11.3 us  [from_rel(): lax.ppermute(value, axis, [((i + step) % size, i) for i in range(size)])]
    ppermute x8, starting transfers between devices: 37.1 us -> 44.9 us  [body(): swap = lambda v, axis: lax.ppermute(v, axis, [(0, 1), (1, 0)])]
    all_gather x3, blocking collectives: 61.5 us -> 54.5 us  [body(): gather = lambda v, axis: lax.all_gather(v, axis, axis=0, tiled=False)]
    ppermute x8, waiting for transfers between devices: 14.3 us -> 9.21 us  [body(): swap = lambda v, axis: lax.ppermute(v, axis, [(0, 1), (1, 0)])]
    all_to_all x1, waiting for transfers between devices: 37.2 us -> 41.2 us  [body(): lax.all_to_all(partial.reshape(NX * NM, crows // NM, width), ('x', 'm'),...]
    pallas_call x4, Pallas kernels: 10.6 us -> 7.02 us  [block_sums(): pl.pallas_call(functools.partial(block_kernel, rel), out_shape=jax.ShapeD...]
    unnamed x20 -> x6, local copies, waits for them, and re-layouts: 4.62 us -> 1.59 us
    convert_element_type x2, other arithmetic: 3.93 us -> 1.56 us  [added(): return total.astype(BF16)]
  transfers between devices with their start and end apart: 17 -> 17, of which waited for: 4 -> 6; matrix products, arithmetic and copies ran while one was open for 3% -> 2% of each run, Pallas kernels for 6% -> 4%
where the time goes in v5:
time: 219 us; the launch traced here: 218 us
  starting transfers between devices  76.3 us (35%)
  waiting for transfers between devices  61.7 us (28%)
  blocking collectives  54.5 us (25%)
  Pallas kernels  13.1 us (6%)
  other arithmetic  7.49 us (3%)
    all_gather x3, blocking collectives, body(): gather = lambda v, axis: lax.all_gather(v, axis, axis=0, tiled=False)  54.5 us
    ppermute x8, starting transfers between devices, body(): swap = lambda v, axis: lax.ppermute(v, axis, [(0, 1), (1, 0)])  44.9 us
    all_to_all x1, waiting for transfers between devices, body(): lax.all_to_all(partial.reshape(NX * NM, crows // NM, width), ('x', 'm'),...  41.2 us
    ppermute x6, starting transfers between devices, from_rel(): lax.ppermute(value, axis, [((i + step) % size, i) for i in range(size)])  17.8 us
    ppermute x6, waiting for transfers between devices, from_rel(): lax.ppermute(value, axis, [((i + step) % size, i) for i in range(size)])  11.3 us
    ppermute x8, waiting for transfers between devices, body(): swap = lambda v, axis: lax.ppermute(v, axis, [(0, 1), (1, 0)])  9.21 us
    all_to_all x1, starting transfers between devices, body(): lax.all_to_all(partial.reshape(NX * NM, crows // NM, width), ('x', 'm'),...  8.52 us
    pallas_call x4, Pallas kernels, block_sums(): pl.pallas_call(functools.partial(block_kernel, rel), out_shape=jax.ShapeD...  7.02 us
  transfers between devices with their start and end apart: 17, of which 6 were waited for; matrix products, arithmetic and copies ran while one was open for 2% of the time, Pallas kernels for 4%

profile of v5, /device:TPU:1, one launch (start us, length us, event | category | flops | bytes accessed | tf_op | source)
XLA Modules:
  0.0 217.8 jit_solution(17859271829215307907)
XLA Ops:
  0.6 0.0 copy-start
  0.6 0.0 copy-start.2
  0.7 1.6 copy-done
  2.2 0.0 copy-start.1
  2.2 2.1 convolution_convert_fusion
  4.4 8.8 %collective-permute-start = (bf16[16,128]{1,0:T(8,128)(2,1)S(1)}, bf16[16,128]{1,0:T(8,128)(2,1)S(1)}, u32[]{:S(2)}, u32[]{:S(2)}) collective-permute-start(bf16[16,128]{1,0:T(8,128)(2,1)S(1)} %slice.36), channel_id=1, source_target_pairs={{0,1},{1,0},{2,3},{3,2},{4,5},{5,4},{6,7},{7,6},{8,9},{9,8},{10,11... | collective-permute-start | bytes 12296 | tf_op jit(solution)/shard_map/ppermute | solution.py:163
  13.2 0.0 copy-done.2
  13.2 0.7 pad_maximum_fusion.1
  13.9 10.1 %collective-permute-start.1 = (bf16[128,1152]{1,0:T(8,128)(2,1)}, bf16[128,1152]{1,0:T(8,128)(2,1)S(1)}, u32[]{:S(2)}, u32[]{:S(2)}) collective-permute-start(bf16[128,1152]{1,0:T(8,128)(2,1)} %pad_maximum_fusion.1), channel_id=1, source_target_pairs={{0,64},{64,0},{1,65},{65,1},{2,66},{66,2},{3,67},{67,3},{4,68},{68... | collective-permute-start | bytes 884744 | tf_op jit(solution)/shard_map/ppermute | solution.py:163
  24.0 0.1 add_add_fusion.1.where_ref
  24.1 0.0 collective-permute-done.refs_6_
  24.1 0.0 copy-done.1
  24.1 4.4 %collective-permute-start.3 = (bf16[448,896]{1,0:T(8,128)(2,1)S(1)}, bf16[448,896]{1,0:T(8,128)(2,1)S(1)}, u32[]{:S(2)}, u32[]{:S(2)}) collective-permute-start(bf16[448,896]{1,0:T(8,128)(2,1)S(1)} %copy-done.1), channel_id=1, source_target_pairs={{16,0},{32,16},{48,32},{0,48},{17,1},{33,17},{49,33},{1,49},{18,2}... | collective-permute-start | bytes 2408456 | tf_op jit(solution)/shard_map/ppermute | solution.py:27
  28.5 2.4 %collective-permute-start.4 = (bf16[448,896]{1,0:T(8,128)(2,1)S(1)}, bf16[448,896]{1,0:T(8,128)(2,1)S(1)}, u32[]{:S(2)}, u32[]{:S(2)}) collective-permute-start(bf16[448,896]{1,0:T(8,128)(2,1)S(1)} %copy-done.1), channel_id=1, source_target_pairs={{32,0},{48,16},{0,32},{16,48},{33,1},{49,17},{1,33},{17,49},{34,2}... | collective-permute-start | bytes 2408456 | tf_op jit(solution)/shard_map/ppermute | solution.py:27
  30.9 2.5 %collective-permute-start.5 = (bf16[448,896]{1,0:T(8,128)(2,1)S(1)}, bf16[448,896]{1,0:T(8,128)(2,1)S(1)}, u32[]{:S(2)}, u32[]{:S(2)}) collective-permute-start(bf16[448,896]{1,0:T(8,128)(2,1)S(1)} %copy-done.1), channel_id=1, source_target_pairs={{48,0},{0,16},{16,32},{32,48},{49,1},{1,17},{17,33},{33,49},{50,2}... | collective-permute-start | bytes 2408456 | tf_op jit(solution)/shard_map/ppermute | solution.py:27
  33.4 13.5 %all-gather = bf16[512,896]{1,0:T(8,128)(2,1)S(1)} all-gather(bf16[128,896]{1,0:T(8,128)(2,1)S(1)} %copy-done.2), channel_id=2, replica_groups=mesh['y'=4,'h'=2,'x'=4,'m'=4,'p'=2,'c'=2] {'y'}, dimensions={0}, use_global_device_ids=true | all-gather | bytes 1146880 | tf_op jit(solution)/shard_map/all_gather | solution.py:165
  46.9 0.0 collective-permute-done.1
  46.9 5.7 %collective-permute-start.2 = (bf16[2,128,256]{2,1,0:T(8,128)(2,1)S(1)}, bf16[2,128,256]{2,1,0:T(8,128)(2,1)S(1)}, u32[]{:S(2)}, u32[]{:S(2)}) collective-permute-start(bf16[2,128,256]{2,1,0:T(8,128)(2,1)S(1)} %pad_maximum_fusion.3), channel_id=1, source_target_pairs={{0,2},{2,0},{1,3},{3,1},{4,6},{6,4},{5,7},{7,5},{8,10},{10,8},{9,1... | collective-permute-start | bytes 393224 | tf_op jit(solution)/shard_map/ppermute | solution.py:163
  52.6 13.5 %all-gather.1 = bf16[512,896]{1,0:T(8,128)(2,1)S(1)} all-gather(bf16[128,896]{1,0:T(8,128)(2,1)S(1)} %slice.37), channel_id=3, replica_groups=mesh['y'=4,'h'=2,'x'=4,'m'=4,'p'=2,'c'=2] {'y'}, dimensions={0}, use_global_device_ids=true | all-gather | bytes 1146880 | tf_op jit(solution)/shard_map/all_gather | solution.py:165
  66.2 0.0 collective-permute-done.2
  66.2 0.0 collective-permute-done.3.refs_3_
  66.2 0.0 collective-permute-done.4.refs_4_
  66.2 2.7 %collective-permute-done.5.refs_5_ = bf16[448,896]{1,0:T(8,128)(2,1)S(1)} collective-permute-done((bf16[448,896]{1,0:T(8,128)(2,1)S(1)}, bf16[448,896]{1,0:T(8,128)(2,1)S(1)}, u32[]{:S(2)}, u32[]{:S(2)}) %collective-permute-start.5) | collective-permute-done | bytes 802848 | tf_op jit(solution)/shard_map/ppermute | solution.py:27
  68.9 1.8 block_sums.5
  70.6 2.4 %collective-permute-start.6 = (bf16[4,448,256]{2,1,0:T(8,128)(2,1)S(1)}, bf16[4,448,256]{2,1,0:T(8,128)(2,1)S(1)}, u32[]{:S(2)}, u32[]{:S(2)}) collective-permute-start(bf16[4,448,256]{2,1,0:T(8,128)(2,1)S(1)} %block_sums.5), channel_id=1, source_target_pairs={{0,1},{1,0},{2,3},{3,2},{4,5},{5,4},{6,7},{7,6},{8,9},{9,8},{10,11... | collective-permute-start | bytes 2752520 | tf_op jit(solution)/shard_map/ppermute | solution.py:163
  73.1 0.1 add_add_fusion.where_ref
  73.1 1.8 block_sums.4
  74.9 0.2 collective-permute-done.6
  75.1 0.3 add_convert_fusion.1
  75.4 2.6 %collective-permute-start.8 = (bf16[4,448,256]{2,1,0:T(8,128)(2,1)S(1)}, bf16[4,448,256]{2,1,0:T(8,128)(2,1)S(1)}, u32[]{:S(2)}, u32[]{:S(2)}) collective-permute-start(bf16[4,448,256]{2,1,0:T(8,128)(2,1)S(1)} %add_convert_fusion.1), channel_id=1, source_target_pairs={{0,2},{2,0},{1,3},{3,1},{4,6},{6,4},{5,7},{7,5},{8,10},{10,8},{9,1... | collective-permute-start | bytes 2752520 | tf_op jit(solution)/shard_map/ppermute | solution.py:163
  78.1 1.8 block_sums.7
  79.8 2.6 %collective-permute-start.7 = (bf16[4,448,256]{2,1,0:T(8,128)(2,1)S(1)}, bf16[4,448,256]{2,1,0:T(8,128)(2,1)S(1)}, u32[]{:S(2)}, u32[]{:S(2)}) collective-permute-start(bf16[4,448,256]{2,1,0:T(8,128)(2,1)S(1)} %block_sums.7), channel_id=1, source_target_pairs={{0,1},{1,0},{2,3},{3,2},{4,5},{5,4},{6,7},{7,6},{8,9},{9,8},{10,11... | collective-permute-start | bytes 2752520 | tf_op jit(solution)/shard_map/ppermute | solution.py:163
  82.4 1.9 collective-permute-start.11
  84.3 3.4 %collective-permute-start.10 = (bf16[2,128,512]{2,1,0:T(8,128)(2,1)S(1)}, bf16[2,128,512]{2,1,0:T(8,128)(2,1)S(1)}, u32[]{:S(2)}, u32[]{:S(2)}) collective-permute-start(bf16[2,128,512]{2,1,0:T(8,128)(2,1)S(1)} %pad_maximum_fusion.2), channel_id=1, source_target_pairs={{32,0},{48,16},{0,32},{16,48},{33,1},{49,17},{1,33},{17,49},{34,2}... | collective-permute-start | bytes 786440 | tf_op jit(solution)/shard_map/ppermute | solution.py:27
  87.7 3.1 %collective-permute-start.9 = (bf16[2,128,512]{2,1,0:T(8,128)(2,1)S(1)}, bf16[2,128,512]{2,1,0:T(8,128)(2,1)S(1)}, u32[]{:S(2)}, u32[]{:S(2)}) collective-permute-start(bf16[2,128,512]{2,1,0:T(8,128)(2,1)S(1)} %pad_maximum_fusion.2), channel_id=1, source_target_pairs={{16,0},{32,16},{48,32},{0,48},{17,1},{33,17},{49,33},{1,49},{18,2}... | collective-permute-start | bytes 786440 | tf_op jit(solution)/shard_map/ppermute | solution.py:27
  90.9 1.8 block_sums.6
  92.6 6.4 %collective-permute-done.11 = bf16[2,128,512]{2,1,0:T(8,128)(2,1)S(1)} collective-permute-done((bf16[2,128,512]{2,1,0:T(8,128)(2,1)S(1)}, bf16[2,128,512]{2,1,0:T(8,128)(2,1)S(1)}, u32[]{:S(2)}, u32[]{:S(2)}) %collective-permute-start.11) | collective-permute-done | bytes 262176 | tf_op jit(solution)/shard_map/ppermute | solution.py:27
  99.0 0.0 collective-permute-done.10
  99.0 2.2 %collective-permute-done.9 = bf16[2,128,512]{2,1,0:T(8,128)(2,1)S(1)} collective-permute-done((bf16[2,128,512]{2,1,0:T(8,128)(2,1)S(1)}, bf16[2,128,512]{2,1,0:T(8,128)(2,1)S(1)}, u32[]{:S(2)}, u32[]{:S(2)}) %collective-permute-start.9) | collective-permute-done | bytes 262176 | tf_op jit(solution)/shard_map/ppermute | solution.py:27
  101.3 1.1 pad_maximum_fusion
  102.4 0.0 collective-permute-done.8
  102.4 0.0 collective-permute-done.7
  102.4 1.3 add_convert_fusion
  103.7 8.5 %all-to-all-start = ((bf16[16,112,256]{2,1,0:T(8,128)(2,1)}), bf16[16,112,256]{2,1,0:T(8,128)(2,1)}, u32[]{:S(2)}, u32[]{:S(2)}) async-start(bf16[16,112,256]{2,1,0:T(8,128)(2,1)} %bitcast.13), calls=%async_computation | async-start | bytes 1835008 | tf_op jit(solution)/shard_map/all_to_all | solution.py:192
  112.2 1.6 collective-permute-start.12
  113.9 3.4 %collective-permute-start.13 = (bf16[4,2,128,512]{3,2,1,0:T(8,128)(2,1)}, bf16[4,2,128,512]{3,2,1,0:T(8,128)(2,1)}, u32[]{:S(2)}, u32[]{:S(2)}) collective-permute-start(bf16[4,2,128,512]{3,2,1,0:T(8,128)(2,1)} %pad_maximum_fusion), channel_id=1, source_target_pairs={{256,0},{386,2},{384,128},{2,130},{0,256},{130,258},{128,384},{258... | collective-permute-start | bytes 3145736 | tf_op jit(solution)/shard_map/ppermute | solution.py:158
  117.3 0.0 collective-permute-done.12
  117.3 1.4 broadcast_select_fusion.refs_0_
  118.7 41.2 %all-to-all-done = bf16[16,112,256]{2,1,0:T(8,128)(2,1)} async-done(((bf16[16,112,256]{2,1,0:T(8,128)(2,1)}), bf16[16,112,256]{2,1,0:T(8,128)(2,1)}, u32[]{:S(2)}, u32[]{:S(2)}) %all-to-all-start) | async-done | bytes 917536 | tf_op jit(solution)/shard_map/all_to_all | solution.py:192
  159.9 1.4 fusion
  161.3 0.0 collective-permute-done.13.refs_1_
  161.3 27.5 %all-gather.2 = bf16[16,112,256]{2,1,0:T(8,128)(2,1)S(1)} all-gather(bf16[4,112,256]{2,1,0:T(8,128)(2,1)S(1)} %fusion), channel_id=4, replica_groups=mesh['y'=4,'h'=2,'x'=4,'m'=4,'p'=2,'c'=2] {'m'}, dimensions={0}, use_global_device_ids=true | all-gather | bytes 1146880 | tf_op jit(solution)/shard_map/all_gather | solution.py:165
  188.8 4.6 %collective-permute-start.14 = (bf16[4,4,112,256]{3,2,1,0:T(8,128)(2,1)S(1)}, bf16[4,4,112,256]{3,2,1,0:T(8,128)(2,1)S(1)}, u32[]{:S(2)}, u32[]{:S(2)}) collective-permute-start(bf16[4,4,112,256]{3,2,1,0:T(8,128)(2,1)S(1)} %bitcast.39), channel_id=1, source_target_pairs={{0,1},{1,0},{2,3},{3,2},{4,5},{5,4},{6,7},{7,6},{8,9},{9,8},{10,11... | collective-permute-start | bytes 2752520 | tf_op jit(solution)/shard_map/ppermute | solution.py:163
  193.4 0.1 pad_add_fusion.where_ref
  193.5 2.3 %near_products.1 = (f32[448,512]{1,0:T(8,128)S(1)}, f32[448,512]{1,0:T(8,128)S(1)}) custom-call(s32[2]{0:T(128)S(1)} %pad_add_fusion.where_ref, bf16[4,4,112,256]{3,2,1,0:T(8,128)(2,1)S(1)} %bitcast.40, bf16[4,2,128,512]{3,2,1,0:T(8,128)(2,1)S(1)} %broadcast_select_fusion.refs_0_, bf16[4,2,128,512]{3,2,1,0:T(8,128)(2,1)} %collective-permute-done.13.refs_1_), custom_call_target="tpu_custom_call" | custom-call | flops 939524096 | bytes 5242880 | tf_op jit(solution)/shard_map/near_products/pallas_call | solution.py:121
  195.8 0.0 collective-permute-done.14.mate_ref
  195.8 1.9 far_products.3
  197.7 8.2 %collective-permute-start.15 = (bf16[2,448,256]{2,1,0:T(8,128)(2,1)S(1)}, bf16[2,448,256]{2,1,0:T(8,128)(2,1)S(1)}, u32[]{:S(2)}, u32[]{:S(2)}) collective-permute-start(bf16[2,448,256]{2,1,0:T(8,128)(2,1)S(1)} %far_products.3), channel_id=1, source_target_pairs={{0,2},{2,0},{1,3},{3,1},{4,6},{6,4},{5,7},{7,5},{8,10},{10,8},{9,1... | collective-permute-start | bytes 1376264 | tf_op jit(solution)/shard_map/ppermute | solution.py:163
  206.0 1.9 far_products.2
  207.9 9.0 %collective-permute-done.15 = bf16[2,448,256]{2,1,0:T(8,128)(2,1)S(1)} collective-permute-done((bf16[2,448,256]{2,1,0:T(8,128)(2,1)S(1)}, bf16[2,448,256]{2,1,0:T(8,128)(2,1)S(1)}, u32[]{:S(2)}, u32[]{:S(2)}) %collective-permute-start.15) | collective-permute-done | bytes 458784 | tf_op jit(solution)/shard_map/ppermute | solution.py:163
  216.8 1.0 convert_add_fusion
  (5 shorter events, 0.1 us)
Async XLA Ops:
  0.6 1.6 copy-start
  0.6 12.5 %copy-start.2 = (bf16[128,896]{1,0:T(8,128)(2,1)S(1)}, bf16[128,896]{1,0:T(8,128)(2,1)}, u32[]{:S(2)}) copy-start(bf16[128,896]{1,0:T(8,128)(2,1)} %param.6) | copy-start | bytes 688132
  2.2 21.9 %copy-start.1 = (bf16[448,896]{1,0:T(8,128)(2,1)S(1)}, bf16[448,896]{1,0:T(8,128)(2,1)}, u32[]{:S(2)}) copy-start(bf16[448,896]{1,0:T(8,128)(2,1)} %refs_2_.3) | copy-start | bytes 2408452
  4.4 19.7 %collective-permute-start = (bf16[16,128]{1,0:T(8,128)(2,1)S(1)}, bf16[16,128]{1,0:T(8,128)(2,1)S(1)}, u32[]{:S(2)}, u32[]{:S(2)}) collective-permute-start(bf16[16,128]{1,0:T(8,128)(2,1)S(1)} %slice.36), channel_id=1, source_target_pairs={{0,1},{1,0},{2,3},{3,2},{4,5},{5,4},{6,7},{7,6},{8,9},{9,8},{10,11... | collective-permute-start | bytes 12296 | tf_op jit(solution)/shard_map/ppermute | solution.py:163
  13.9 33.0 %collective-permute-start.1 = (bf16[128,1152]{1,0:T(8,128)(2,1)}, bf16[128,1152]{1,0:T(8,128)(2,1)S(1)}, u32[]{:S(2)}, u32[]{:S(2)}) collective-permute-start(bf16[128,1152]{1,0:T(8,128)(2,1)} %pad_maximum_fusion.1), channel_id=1, source_target_pairs={{0,64},{64,0},{1,65},{65,1},{2,66},{66,2},{3,67},{67,3},{4,68},{68... | collective-permute-start | bytes 884744 | tf_op jit(solution)/shard_map/ppermute | solution.py:163
  24.1 42.1 %collective-permute-start.3 = (bf16[448,896]{1,0:T(8,128)(2,1)S(1)}, bf16[448,896]{1,0:T(8,128)(2,1)S(1)}, u32[]{:S(2)}, u32[]{:S(2)}) collective-permute-start(bf16[448,896]{1,0:T(8,128)(2,1)S(1)} %copy-done.1), channel_id=1, source_target_pairs={{16,0},{32,16},{48,32},{0,48},{17,1},{33,17},{49,33},{1,49},{18,2}... | collective-permute-start | bytes 2408456 | tf_op jit(solution)/shard_map/ppermute | solution.py:27
  28.5 37.7 %collective-permute-start.4 = (bf16[448,896]{1,0:T(8,128)(2,1)S(1)}, bf16[448,896]{1,0:T(8,128)(2,1)S(1)}, u32[]{:S(2)}, u32[]{:S(2)}) collective-permute-start(bf16[448,896]{1,0:T(8,128)(2,1)S(1)} %copy-done.1), channel_id=1, source_target_pairs={{32,0},{48,16},{0,32},{16,48},{33,1},{49,17},{1,33},{17,49},{34,2}... | collective-permute-start | bytes 2408456 | tf_op jit(solution)/shard_map/ppermute | solution.py:27
  30.9 38.0 %collective-permute-start.5 = (bf16[448,896]{1,0:T(8,128)(2,1)S(1)}, bf16[448,896]{1,0:T(8,128)(2,1)S(1)}, u32[]{:S(2)}, u32[]{:S(2)}) collective-permute-start(bf16[448,896]{1,0:T(8,128)(2,1)S(1)} %copy-done.1), channel_id=1, source_target_pairs={{48,0},{0,16},{16,32},{32,48},{49,1},{1,17},{17,33},{33,49},{50,2}... | collective-permute-start | bytes 2408456 | tf_op jit(solution)/shard_map/ppermute | solution.py:27
  46.9 19.2 %collective-permute-start.2 = (bf16[2,128,256]{2,1,0:T(8,128)(2,1)S(1)}, bf16[2,128,256]{2,1,0:T(8,128)(2,1)S(1)}, u32[]{:S(2)}, u32[]{:S(2)}) collective-permute-start(bf16[2,128,256]{2,1,0:T(8,128)(2,1)S(1)} %pad_maximum_fusion.3), channel_id=1, source_target_pairs={{0,2},{2,0},{1,3},{3,1},{4,6},{6,4},{5,7},{7,5},{8,10},{10,8},{9,1... | collective-permute-start | bytes 393224 | tf_op jit(solution)/shard_map/ppermute | solution.py:163
  70.6 4.5 %collective-permute-start.6 = (bf16[4,448,256]{2,1,0:T(8,128)(2,1)S(1)}, bf16[4,448,256]{2,1,0:T(8,128)(2,1)S(1)}, u32[]{:S(2)}, u32[]{:S(2)}) collective-permute-start(bf16[4,448,256]{2,1,0:T(8,128)(2,1)S(1)} %block_sums.5), channel_id=1, source_target_pairs={{0,1},{1,0},{2,3},{3,2},{4,5},{5,4},{6,7},{7,6},{8,9},{9,8},{10,11... | collective-permute-start | bytes 2752520 | tf_op jit(solution)/shard_map/ppermute | solution.py:163
  75.4 27.0 %collective-permute-start.8 = (bf16[4,448,256]{2,1,0:T(8,128)(2,1)S(1)}, bf16[4,448,256]{2,1,0:T(8,128)(2,1)S(1)}, u32[]{:S(2)}, u32[]{:S(2)}) collective-permute-start(bf16[4,448,256]{2,1,0:T(8,128)(2,1)S(1)} %add_convert_fusion.1), channel_id=1, source_target_pairs={{0,2},{2,0},{1,3},{3,1},{4,6},{6,4},{5,7},{7,5},{8,10},{10,8},{9,1... | collective-permute-start | bytes 2752520 | tf_op jit(solution)/shard_map/ppermute | solution.py:163
  79.8 22.6 %collective-permute-start.7 = (bf16[4,448,256]{2,1,0:T(8,128)(2,1)S(1)}, bf16[4,448,256]{2,1,0:T(8,128)(2,1)S(1)}, u32[]{:S(2)}, u32[]{:S(2)}) collective-permute-start(bf16[4,448,256]{2,1,0:T(8,128)(2,1)S(1)} %block_sums.7), channel_id=1, source_target_pairs={{0,1},{1,0},{2,3},{3,2},{4,5},{5,4},{6,7},{7,6},{8,9},{9,8},{10,11... | collective-permute-start | bytes 2752520 | tf_op jit(solution)/shard_map/ppermute | solution.py:163
  82.4 16.6 %collective-permute-start.11 = (bf16[2,128,512]{2,1,0:T(8,128)(2,1)S(1)}, bf16[2,128,512]{2,1,0:T(8,128)(2,1)S(1)}, u32[]{:S(2)}, u32[]{:S(2)}) collective-permute-start(bf16[2,128,512]{2,1,0:T(8,128)(2,1)S(1)} %pad_maximum_fusion.2), channel_id=1, source_target_pairs={{48,0},{0,16},{16,32},{32,48},{49,1},{1,17},{17,33},{33,49},{50,2}... | collective-permute-start | bytes 786440 | tf_op jit(solution)/shard_map/ppermute | solution.py:27
  84.3 14.7 %collective-permute-start.10 = (bf16[2,128,512]{2,1,0:T(8,128)(2,1)S(1)}, bf16[2,128,512]{2,1,0:T(8,128)(2,1)S(1)}, u32[]{:S(2)}, u32[]{:S(2)}) collective-permute-start(bf16[2,128,512]{2,1,0:T(8,128)(2,1)S(1)} %pad_maximum_fusion.2), channel_id=1, source_target_pairs={{32,0},{48,16},{0,32},{16,48},{33,1},{49,17},{1,33},{17,49},{34,2}... | collective-permute-start | bytes 786440 | tf_op jit(solution)/shard_map/ppermute | solution.py:27
  87.7 13.5 %collective-permute-start.9 = (bf16[2,128,512]{2,1,0:T(8,128)(2,1)S(1)}, bf16[2,128,512]{2,1,0:T(8,128)(2,1)S(1)}, u32[]{:S(2)}, u32[]{:S(2)}) collective-permute-start(bf16[2,128,512]{2,1,0:T(8,128)(2,1)S(1)} %pad_maximum_fusion.2), channel_id=1, source_target_pairs={{16,0},{32,16},{48,32},{0,48},{17,1},{33,17},{49,33},{1,49},{18,2}... | collective-permute-start | bytes 786440 | tf_op jit(solution)/shard_map/ppermute | solution.py:27
  103.7 56.2 %all-to-all-start = ((bf16[16,112,256]{2,1,0:T(8,128)(2,1)}), bf16[16,112,256]{2,1,0:T(8,128)(2,1)}, u32[]{:S(2)}, u32[]{:S(2)}) async-start(bf16[16,112,256]{2,1,0:T(8,128)(2,1)} %bitcast.13), calls=%async_computation | async-start | bytes 1835008 | tf_op jit(solution)/shard_map/all_to_all | solution.py:192
  112.2 5.1 %collective-permute-start.12 = (bf16[4,2,128,512]{3,2,1,0:T(8,128)(2,1)}, bf16[4,2,128,512]{3,2,1,0:T(8,128)(2,1)}, u32[]{:S(2)}, u32[]{:S(2)}) collective-permute-start(bf16[4,2,128,512]{3,2,1,0:T(8,128)(2,1)} %pad_maximum_fusion), channel_id=1, source_target_pairs={{130,2},{258,130},{386,258},{2,386},{131,3},{259,131},{387,259},{3... | collective-permute-start | bytes 3145736 | tf_op jit(solution)/shard_map/ppermute | solution.py:156
  113.9 47.4 %collective-permute-start.13 = (bf16[4,2,128,512]{3,2,1,0:T(8,128)(2,1)}, bf16[4,2,128,512]{3,2,1,0:T(8,128)(2,1)}, u32[]{:S(2)}, u32[]{:S(2)}) collective-permute-start(bf16[4,2,128,512]{3,2,1,0:T(8,128)(2,1)} %pad_maximum_fusion), channel_id=1, source_target_pairs={{256,0},{386,2},{384,128},{2,130},{0,256},{130,258},{128,384},{258... | collective-permute-start | bytes 3145736 | tf_op jit(solution)/shard_map/ppermute | solution.py:158
  188.8 7.0 %collective-permute-start.14 = (bf16[4,4,112,256]{3,2,1,0:T(8,128)(2,1)S(1)}, bf16[4,4,112,256]{3,2,1,0:T(8,128)(2,1)S(1)}, u32[]{:S(2)}, u32[]{:S(2)}) collective-permute-start(bf16[4,4,112,256]{3,2,1,0:T(8,128)(2,1)S(1)} %bitcast.39), channel_id=1, source_target_pairs={{0,1},{1,0},{2,3},{3,2},{4,5},{5,4},{6,7},{7,6},{8,9},{9,8},{10,11... | collective-permute-start | bytes 2752520 | tf_op jit(solution)/shard_map/ppermute | solution.py:163
  197.7 19.1 %collective-permute-start.15 = (bf16[2,448,256]{2,1,0:T(8,128)(2,1)S(1)}, bf16[2,448,256]{2,1,0:T(8,128)(2,1)S(1)}, u32[]{:S(2)}, u32[]{:S(2)}) collective-permute-start(bf16[2,448,256]{2,1,0:T(8,128)(2,1)S(1)} %far_products.3), channel_id=1, source_target_pairs={{0,2},{2,0},{1,3},{3,1},{4,6},{6,4},{5,7},{7,5},{8,10},{10,8},{9,1... | collective-permute-start | bytes 1376264 | tf_op jit(solution)/shard_map/ppermute | solution.py:163

commit v6 on v5

--- a/solution.py
+++ b/solution.py
@@ -42,9 +42,12 @@
 
     for j in range(NX):
         home = lax.rem(here + j, NX)
-        out_ref[home] = lax.dot_general(
+        sums = lax.dot_general(
             basis[j][...], held_ref[...], (((1,), (1,)), ((), ())), preferred_element_type=F32
         ).astype(BF16)
+        piece = sums.shape[0] // NM
+        for m in range(NM):
+            out_ref[m, home] = sums[m * piece : (m + 1) * piece]
 
 
 def block_sums(rel, where, tokens, basis, turn):
@@ -52,7 +55,7 @@
     crows = basis[0].shape[0]
     return pl.pallas_call(
         functools.partial(block_kernel, rel),
-        out_shape=jax.ShapeDtypeStruct((NX, crows, 2 * rows), BF16),
+        out_shape=jax.ShapeDtypeStruct((NM, NX, crows // NM, 2 * rows), BF16),
         in_specs=[SMEM] + [VMEM] * (2 + NX) + [ANY],
         out_specs=VMEM,
         scratch_shapes=[pltpu.VMEM((2 * rows, depth), BF16)],
@@ -188,11 +191,11 @@
     partial = added(block_sums(0, here, tokens, basis, turn), got, pair)
     partial, acts = lax.optimization_barrier((partial, acts))
     all_acts = own_columns(acts, parity)
-    crows, width = partial.shape[1:]
+    piece, width = partial.shape[2:]
     spread = lax.all_to_all(
-        partial.reshape(NX * NM, crows // NM, width), ("x", "m"), split_axis=0, concat_axis=0, tiled=True
-    ).reshape(NX, NM, crows // NM, width)
-    own = added(*[spread[:, j] for j in range(NM)])
+        partial.reshape(NM * NX, piece, width), ("m", "x"), split_axis=0, concat_axis=0, tiled=True
+    ).reshape(NM, NX, piece, width)
+    own = added(*[spread[j] for j in range(NM)])
     own, all_acts = lax.optimization_barrier((own, all_acts))
     mine = gather(own, "m")
     mate = swap(mine, "c")

time: 219 us -> 218 us (level)
  blocking collectives: 54.5 us -> 61.8 us
  starting transfers between devices: 76.3 us -> 70.9 us
  waiting for transfers between devices: 61.7 us -> 58 us
    all_gather x3, blocking collectives: 54.5 us -> 61.8 us  [body(): gather = lambda v, axis: lax.all_gather(v, axis, axis=0, tiled=False)]
    ppermute x8, starting transfers between devices: 44.9 us -> 39.5 us  [body(): swap = lambda v, axis: lax.ppermute(v, axis, [(0, 1), (1, 0)])]
    all_to_all x1, waiting for transfers between devices: 41.2 us -> 37.5 us  [body(): lax.all_to_all(partial.reshape(NM * NX, piece, width), ('m', 'x'), split_...]
where the time goes in v6:
time: 218 us; the launch traced here: 216 us
  starting transfers between devices  70.9 us (33%)
  blocking collectives  61.8 us (28%)
  waiting for transfers between devices  58 us (27%)
  Pallas kernels  13.2 us (6%)
  other arithmetic  7.41 us (3%)
    all_gather x3, blocking collectives, body(): gather = lambda v, axis: lax.all_gather(v, axis, axis=0, tiled=False)  61.8 us
    ppermute x8, starting transfers between devices, body(): swap = lambda v, axis: lax.ppermute(v, axis, [(0, 1), (1, 0)])  39.5 us
    all_to_all x1, waiting for transfers between devices, body(): lax.all_to_all(partial.reshape(NM * NX, piece, width), ('m', 'x'), split_...  37.5 us
    ppermute x6, starting transfers between devices, from_rel(): lax.ppermute(value, axis, [((i + step) % size, i) for i in range(size)])  17.8 us
    ppermute x6, waiting for transfers between devices, from_rel(): lax.ppermute(value, axis, [((i + step) % size, i) for i in range(size)])  11.3 us
    ppermute x8, waiting for transfers between devices, body(): swap = lambda v, axis: lax.ppermute(v, axis, [(0, 1), (1, 0)])  9.21 us
    all_to_all x1, starting transfers between devices, body(): lax.all_to_all(partial.reshape(NM * NX, piece, width), ('m', 'x'), split_...  8.53 us
    pallas_call x4, Pallas kernels, block_sums(): pl.pallas_call(functools.partial(block_kernel, rel), out_shape=jax.ShapeD...  7.05 us
  transfers between devices with their start and end apart: 17, of which 6 were waited for; matrix products, arithmetic and copies ran while one was open for 2% of the time, Pallas kernels for 4%

profile of v6, /device:TPU:1, one launch (start us, length us, event | category | flops | bytes accessed | tf_op | source)
XLA Modules:
  0.0 216.0 jit_solution(300859001238169417)
XLA Ops:
  0.6 0.0 copy-start
  0.6 0.0 copy-start.2
  0.7 1.6 copy-done
  2.2 0.0 copy-start.1
  2.2 2.1 convolution_convert_fusion
  4.4 8.8 %collective-permute-start = (bf16[16,128]{1,0:T(8,128)(2,1)S(1)}, bf16[16,128]{1,0:T(8,128)(2,1)S(1)}, u32[]{:S(2)}, u32[]{:S(2)}) collective-permute-start(bf16[16,128]{1,0:T(8,128)(2,1)S(1)} %slice.40), channel_id=1, source_target_pairs={{0,1},{1,0},{2,3},{3,2},{4,5},{5,4},{6,7},{7,6},{8,9},{9,8},{10,11... | collective-permute-start | bytes 12296 | tf_op jit(solution)/shard_map/ppermute | solution.py:166
  13.2 0.0 copy-done.2
  13.2 0.7 pad_maximum_fusion.1
  13.9 10.1 %collective-permute-start.1 = (bf16[128,1152]{1,0:T(8,128)(2,1)}, bf16[128,1152]{1,0:T(8,128)(2,1)S(1)}, u32[]{:S(2)}, u32[]{:S(2)}) collective-permute-start(bf16[128,1152]{1,0:T(8,128)(2,1)} %pad_maximum_fusion.1), channel_id=1, source_target_pairs={{0,64},{64,0},{1,65},{65,1},{2,66},{66,2},{3,67},{67,3},{4,68},{68... | collective-permute-start | bytes 884744 | tf_op jit(solution)/shard_map/ppermute | solution.py:166
  24.0 0.1 add_add_fusion.1.where_ref
  24.1 0.0 collective-permute-done.refs_6_
  24.1 0.0 copy-done.1
  24.1 4.4 %collective-permute-start.3 = (bf16[448,896]{1,0:T(8,128)(2,1)S(1)}, bf16[448,896]{1,0:T(8,128)(2,1)S(1)}, u32[]{:S(2)}, u32[]{:S(2)}) collective-permute-start(bf16[448,896]{1,0:T(8,128)(2,1)S(1)} %copy-done.1), channel_id=1, source_target_pairs={{16,0},{32,16},{48,32},{0,48},{17,1},{33,17},{49,33},{1,49},{18,2}... | collective-permute-start | bytes 2408456 | tf_op jit(solution)/shard_map/ppermute | solution.py:27
  28.5 2.4 %collective-permute-start.4 = (bf16[448,896]{1,0:T(8,128)(2,1)S(1)}, bf16[448,896]{1,0:T(8,128)(2,1)S(1)}, u32[]{:S(2)}, u32[]{:S(2)}) collective-permute-start(bf16[448,896]{1,0:T(8,128)(2,1)S(1)} %copy-done.1), channel_id=1, source_target_pairs={{32,0},{48,16},{0,32},{16,48},{33,1},{49,17},{1,33},{17,49},{34,2}... | collective-permute-start | bytes 2408456 | tf_op jit(solution)/shard_map/ppermute | solution.py:27
  30.9 2.5 %collective-permute-start.5 = (bf16[448,896]{1,0:T(8,128)(2,1)S(1)}, bf16[448,896]{1,0:T(8,128)(2,1)S(1)}, u32[]{:S(2)}, u32[]{:S(2)}) collective-permute-start(bf16[448,896]{1,0:T(8,128)(2,1)S(1)} %copy-done.1), channel_id=1, source_target_pairs={{48,0},{0,16},{16,32},{32,48},{49,1},{1,17},{17,33},{33,49},{50,2}... | collective-permute-start | bytes 2408456 | tf_op jit(solution)/shard_map/ppermute | solution.py:27
  33.4 13.5 %all-gather = bf16[512,896]{1,0:T(8,128)(2,1)S(1)} all-gather(bf16[128,896]{1,0:T(8,128)(2,1)S(1)} %copy-done.2), channel_id=2, replica_groups=mesh['y'=4,'h'=2,'x'=4,'m'=4,'p'=2,'c'=2] {'y'}, dimensions={0}, use_global_device_ids=true | all-gather | bytes 1146880 | tf_op jit(solution)/shard_map/all_gather | solution.py:168
  46.9 0.0 collective-permute-done.1
  46.9 5.7 %collective-permute-start.2 = (bf16[2,128,256]{2,1,0:T(8,128)(2,1)S(1)}, bf16[2,128,256]{2,1,0:T(8,128)(2,1)S(1)}, u32[]{:S(2)}, u32[]{:S(2)}) collective-permute-start(bf16[2,128,256]{2,1,0:T(8,128)(2,1)S(1)} %pad_maximum_fusion.3), channel_id=1, source_target_pairs={{0,2},{2,0},{1,3},{3,1},{4,6},{6,4},{5,7},{7,5},{8,10},{10,8},{9,1... | collective-permute-start | bytes 393224 | tf_op jit(solution)/shard_map/ppermute | solution.py:166
  52.6 13.5 %all-gather.1 = bf16[512,896]{1,0:T(8,128)(2,1)S(1)} all-gather(bf16[128,896]{1,0:T(8,128)(2,1)S(1)} %slice.41), channel_id=3, replica_groups=mesh['y'=4,'h'=2,'x'=4,'m'=4,'p'=2,'c'=2] {'y'}, dimensions={0}, use_global_device_ids=true | all-gather | bytes 1146880 | tf_op jit(solution)/shard_map/all_gather | solution.py:168
  66.2 0.0 collective-permute-done.2
  66.2 0.0 collective-permute-done.3.refs_3_
  66.2 0.0 collective-permute-done.4.refs_4_
  66.2 2.7 %collective-permute-done.5.refs_5_ = bf16[448,896]{1,0:T(8,128)(2,1)S(1)} collective-permute-done((bf16[448,896]{1,0:T(8,128)(2,1)S(1)}, bf16[448,896]{1,0:T(8,128)(2,1)S(1)}, u32[]{:S(2)}, u32[]{:S(2)}) %collective-permute-start.5) | collective-permute-done | bytes 802848 | tf_op jit(solution)/shard_map/ppermute | solution.py:27
  68.9 1.8 block_sums.5
  70.7 2.4 %collective-permute-start.6 = (bf16[4,4,112,256]{3,2,1,0:T(8,128)(2,1)S(1)}, bf16[4,4,112,256]{3,2,1,0:T(8,128)(2,1)S(1)}, u32[]{:S(2)}, u32[]{:S(2)}) collective-permute-start(bf16[4,4,112,256]{3,2,1,0:T(8,128)(2,1)S(1)} %block_sums.5), channel_id=1, source_target_pairs={{0,1},{1,0},{2,3},{3,2},{4,5},{5,4},{6,7},{7,6},{8,9},{9,8},{10,11... | collective-permute-start | bytes 2752520 | tf_op jit(solution)/shard_map/ppermute | solution.py:166
  73.1 0.1 add_add_fusion.where_ref
  73.1 1.8 block_sums.4
  74.9 0.2 collective-permute-done.6
  75.1 0.2 add_convert_fusion.1
  75.4 2.6 %collective-permute-start.8 = (bf16[4,4,112,256]{3,2,1,0:T(8,128)(2,1)S(1)}, bf16[4,4,112,256]{3,2,1,0:T(8,128)(2,1)S(1)}, u32[]{:S(2)}, u32[]{:S(2)}) collective-permute-start(bf16[4,4,112,256]{3,2,1,0:T(8,128)(2,1)S(1)} %add_convert_fusion.1), channel_id=1, source_target_pairs={{0,2},{2,0},{1,3},{3,1},{4,6},{6,4},{5,7},{7,5},{8,10},{10,8},{9,1... | collective-permute-start | bytes 2752520 | tf_op jit(solution)/shard_map/ppermute | solution.py:166
  78.0 1.8 block_sums.7
  79.8 2.6 %collective-permute-start.7 = (bf16[4,4,112,256]{3,2,1,0:T(8,128)(2,1)S(1)}, bf16[4,4,112,256]{3,2,1,0:T(8,128)(2,1)S(1)}, u32[]{:S(2)}, u32[]{:S(2)}) collective-permute-start(bf16[4,4,112,256]{3,2,1,0:T(8,128)(2,1)S(1)} %block_sums.7), channel_id=1, source_target_pairs={{0,1},{1,0},{2,3},{3,2},{4,5},{5,4},{6,7},{7,6},{8,9},{9,8},{10,11... | collective-permute-start | bytes 2752520 | tf_op jit(solution)/shard_map/ppermute | solution.py:166
  82.4 1.9 collective-permute-start.11
  84.3 3.4 %collective-permute-start.10 = (bf16[2,128,512]{2,1,0:T(8,128)(2,1)S(1)}, bf16[2,128,512]{2,1,0:T(8,128)(2,1)S(1)}, u32[]{:S(2)}, u32[]{:S(2)}) collective-permute-start(bf16[2,128,512]{2,1,0:T(8,128)(2,1)S(1)} %pad_maximum_fusion.2), channel_id=1, source_target_pairs={{32,0},{48,16},{0,32},{16,48},{33,1},{49,17},{1,33},{17,49},{34,2}... | collective-permute-start | bytes 786440 | tf_op jit(solution)/shard_map/ppermute | solution.py:27
  87.7 3.1 %collective-permute-start.9 = (bf16[2,128,512]{2,1,0:T(8,128)(2,1)S(1)}, bf16[2,128,512]{2,1,0:T(8,128)(2,1)S(1)}, u32[]{:S(2)}, u32[]{:S(2)}) collective-permute-start(bf16[2,128,512]{2,1,0:T(8,128)(2,1)S(1)} %pad_maximum_fusion.2), channel_id=1, source_target_pairs={{16,0},{32,16},{48,32},{0,48},{17,1},{33,17},{49,33},{1,49},{18,2}... | collective-permute-start | bytes 786440 | tf_op jit(solution)/shard_map/ppermute | solution.py:27
  90.8 1.8 block_sums.6
  92.6 6.4 %collective-permute-done.11 = bf16[2,128,512]{2,1,0:T(8,128)(2,1)S(1)} collective-permute-done((bf16[2,128,512]{2,1,0:T(8,128)(2,1)S(1)}, bf16[2,128,512]{2,1,0:T(8,128)(2,1)S(1)}, u32[]{:S(2)}, u32[]{:S(2)}) %collective-permute-start.11) | collective-permute-done | bytes 262176 | tf_op jit(solution)/shard_map/ppermute | solution.py:27
  99.0 0.0 collective-permute-done.10
  99.0 2.2 %collective-permute-done.9 = bf16[2,128,512]{2,1,0:T(8,128)(2,1)S(1)} collective-permute-done((bf16[2,128,512]{2,1,0:T(8,128)(2,1)S(1)}, bf16[2,128,512]{2,1,0:T(8,128)(2,1)S(1)}, u32[]{:S(2)}, u32[]{:S(2)}) %collective-permute-start.9) | collective-permute-done | bytes 262176 | tf_op jit(solution)/shard_map/ppermute | solution.py:27
  101.2 1.1 pad_maximum_fusion
  102.4 0.0 collective-permute-done.8
  102.4 0.0 collective-permute-done.7
  102.4 1.3 add_convert_fusion
  103.6 8.5 %all-to-all-start = ((bf16[16,112,256]{2,1,0:T(8,128)(2,1)}), bf16[16,112,256]{2,1,0:T(8,128)(2,1)}, u32[]{:S(2)}, u32[]{:S(2)}) async-start(bf16[16,112,256]{2,1,0:T(8,128)(2,1)} %bitcast.13), calls=%async_computation | async-start | bytes 1835008 | tf_op jit(solution)/shard_map/all_to_all | solution.py:195
  112.2 1.6 collective-permute-start.12
  113.8 3.4 %collective-permute-start.13 = (bf16[4,2,128,512]{3,2,1,0:T(8,128)(2,1)}, bf16[4,2,128,512]{3,2,1,0:T(8,128)(2,1)}, u32[]{:S(2)}, u32[]{:S(2)}) collective-permute-start(bf16[4,2,128,512]{3,2,1,0:T(8,128)(2,1)} %pad_maximum_fusion), channel_id=1, source_target_pairs={{256,0},{386,2},{384,128},{2,130},{0,256},{130,258},{128,384},{258... | collective-permute-start | bytes 3145736 | tf_op jit(solution)/shard_map/ppermute | solution.py:161
  117.2 0.0 collective-permute-done.12
  117.2 1.4 broadcast_select_fusion.refs_0_
  118.6 37.5 %all-to-all-done = bf16[16,112,256]{2,1,0:T(8,128)(2,1)} async-done(((bf16[16,112,256]{2,1,0:T(8,128)(2,1)}), bf16[16,112,256]{2,1,0:T(8,128)(2,1)}, u32[]{:S(2)}, u32[]{:S(2)}) %all-to-all-start) | async-done | bytes 917536 | tf_op jit(solution)/shard_map/all_to_all | solution.py:195
  156.2 1.4 add_convert_fusion.2
  157.5 0.0 collective-permute-done.13.refs_1_
  157.6 34.8 %all-gather.2 = bf16[16,112,256]{2,1,0:T(8,128)(2,1)S(1)} all-gather(bf16[4,112,256]{2,1,0:T(8,128)(2,1)S(1)} %add_convert_fusion.2), channel_id=4, replica_groups=mesh['y'=4,'h'=2,'x'=4,'m'=4,'p'=2,'c'=2] {'m'}, dimensions={0}, use_global_device_ids=true | all-gather | bytes 1146880 | tf_op jit(solution)/shard_map/all_gather | solution.py:168
  192.4 2.5 %collective-permute-start.14 = (bf16[4,4,112,256]{3,2,1,0:T(8,128)(2,1)S(1)}, bf16[4,4,112,256]{3,2,1,0:T(8,128)(2,1)S(1)}, u32[]{:S(2)}, u32[]{:S(2)}) collective-permute-start(bf16[4,4,112,256]{3,2,1,0:T(8,128)(2,1)S(1)} %bitcast.36), channel_id=1, source_target_pairs={{0,1},{1,0},{2,3},{3,2},{4,5},{5,4},{6,7},{7,6},{8,9},{9,8},{10,11... | collective-permute-start | bytes 2752520 | tf_op jit(solution)/shard_map/ppermute | solution.py:166
  194.9 0.1 pad_add_fusion.where_ref
  194.9 2.3 %near_products.1 = (f32[448,512]{1,0:T(8,128)S(1)}, f32[448,512]{1,0:T(8,128)S(1)}) custom-call(s32[2]{0:T(128)S(1)} %pad_add_fusion.where_ref, bf16[4,4,112,256]{3,2,1,0:T(8,128)(2,1)S(1)} %bitcast.37, bf16[4,2,128,512]{3,2,1,0:T(8,128)(2,1)S(1)} %broadcast_select_fusion.refs_0_, bf16[4,2,128,512]{3,2,1,0:T(8,128)(2,1)} %collective-permute-done.13.refs_1_), custom_call_target="tpu_custom_call" | custom-call | flops 939524096 | bytes 5242880 | tf_op jit(solution)/shard_map/near_products/pallas_call | solution.py:124
  197.3 0.0 collective-permute-done.14.mate_ref
  197.3 1.9 far_products.3
  199.2 4.9 %collective-permute-start.15 = (bf16[2,448,256]{2,1,0:T(8,128)(2,1)S(1)}, bf16[2,448,256]{2,1,0:T(8,128)(2,1)S(1)}, u32[]{:S(2)}, u32[]{:S(2)}) collective-permute-start(bf16[2,448,256]{2,1,0:T(8,128)(2,1)S(1)} %far_products.3), channel_id=1, source_target_pairs={{0,2},{2,0},{1,3},{3,1},{4,6},{6,4},{5,7},{7,5},{8,10},{10,8},{9,1... | collective-permute-start | bytes 1376264 | tf_op jit(solution)/shard_map/ppermute | solution.py:166
  204.1 1.9 far_products.2
  206.0 9.0 %collective-permute-done.15 = bf16[2,448,256]{2,1,0:T(8,128)(2,1)S(1)} collective-permute-done((bf16[2,448,256]{2,1,0:T(8,128)(2,1)S(1)}, bf16[2,448,256]{2,1,0:T(8,128)(2,1)S(1)}, u32[]{:S(2)}, u32[]{:S(2)}) %collective-permute-start.15) | collective-permute-done | bytes 458784 | tf_op jit(solution)/shard_map/ppermute | solution.py:166
  215.0 1.0 convert_add_fusion
  (5 shorter events, 0.1 us)
Async XLA Ops:
  0.6 1.6 copy-start
  0.6 12.5 %copy-start.2 = (bf16[128,896]{1,0:T(8,128)(2,1)S(1)}, bf16[128,896]{1,0:T(8,128)(2,1)}, u32[]{:S(2)}) copy-start(bf16[128,896]{1,0:T(8,128)(2,1)} %param.6) | copy-start | bytes 688132
  2.2 21.9 %copy-start.1 = (bf16[448,896]{1,0:T(8,128)(2,1)S(1)}, bf16[448,896]{1,0:T(8,128)(2,1)}, u32[]{:S(2)}) copy-start(bf16[448,896]{1,0:T(8,128)(2,1)} %refs_2_.3) | copy-start | bytes 2408452
  4.4 19.7 %collective-permute-start = (bf16[16,128]{1,0:T(8,128)(2,1)S(1)}, bf16[16,128]{1,0:T(8,128)(2,1)S(1)}, u32[]{:S(2)}, u32[]{:S(2)}) collective-permute-start(bf16[16,128]{1,0:T(8,128)(2,1)S(1)} %slice.40), channel_id=1, source_target_pairs={{0,1},{1,0},{2,3},{3,2},{4,5},{5,4},{6,7},{7,6},{8,9},{9,8},{10,11... | collective-permute-start | bytes 12296 | tf_op jit(solution)/shard_map/ppermute | solution.py:166
  13.9 33.0 %collective-permute-start.1 = (bf16[128,1152]{1,0:T(8,128)(2,1)}, bf16[128,1152]{1,0:T(8,128)(2,1)S(1)}, u32[]{:S(2)}, u32[]{:S(2)}) collective-permute-start(bf16[128,1152]{1,0:T(8,128)(2,1)} %pad_maximum_fusion.1), channel_id=1, source_target_pairs={{0,64},{64,0},{1,65},{65,1},{2,66},{66,2},{3,67},{67,3},{4,68},{68... | collective-permute-start | bytes 884744 | tf_op jit(solution)/shard_map/ppermute | solution.py:166
  24.1 42.1 %collective-permute-start.3 = (bf16[448,896]{1,0:T(8,128)(2,1)S(1)}, bf16[448,896]{1,0:T(8,128)(2,1)S(1)}, u32[]{:S(2)}, u32[]{:S(2)}) collective-permute-start(bf16[448,896]{1,0:T(8,128)(2,1)S(1)} %copy-done.1), channel_id=1, source_target_pairs={{16,0},{32,16},{48,32},{0,48},{17,1},{33,17},{49,33},{1,49},{18,2}... | collective-permute-start | bytes 2408456 | tf_op jit(solution)/shard_map/ppermute | solution.py:27
  28.5 37.7 %collective-permute-start.4 = (bf16[448,896]{1,0:T(8,128)(2,1)S(1)}, bf16[448,896]{1,0:T(8,128)(2,1)S(1)}, u32[]{:S(2)}, u32[]{:S(2)}) collective-permute-start(bf16[448,896]{1,0:T(8,128)(2,1)S(1)} %copy-done.1), channel_id=1, source_target_pairs={{32,0},{48,16},{0,32},{16,48},{33,1},{49,17},{1,33},{17,49},{34,2}... | collective-permute-start | bytes 2408456 | tf_op jit(solution)/shard_map/ppermute | solution.py:27
  30.9 38.0 %collective-permute-start.5 = (bf16[448,896]{1,0:T(8,128)(2,1)S(1)}, bf16[448,896]{1,0:T(8,128)(2,1)S(1)}, u32[]{:S(2)}, u32[]{:S(2)}) collective-permute-start(bf16[448,896]{1,0:T(8,128)(2,1)S(1)} %copy-done.1), channel_id=1, source_target_pairs={{48,0},{0,16},{16,32},{32,48},{49,1},{1,17},{17,33},{33,49},{50,2}... | collective-permute-start | bytes 2408456 | tf_op jit(solution)/shard_map/ppermute | solution.py:27
  46.9 19.2 %collective-permute-start.2 = (bf16[2,128,256]{2,1,0:T(8,128)(2,1)S(1)}, bf16[2,128,256]{2,1,0:T(8,128)(2,1)S(1)}, u32[]{:S(2)}, u32[]{:S(2)}) collective-permute-start(bf16[2,128,256]{2,1,0:T(8,128)(2,1)S(1)} %pad_maximum_fusion.3), channel_id=1, source_target_pairs={{0,2},{2,0},{1,3},{3,1},{4,6},{6,4},{5,7},{7,5},{8,10},{10,8},{9,1... | collective-permute-start | bytes 393224 | tf_op jit(solution)/shard_map/ppermute | solution.py:166
  70.7 4.5 %collective-permute-start.6 = (bf16[4,4,112,256]{3,2,1,0:T(8,128)(2,1)S(1)}, bf16[4,4,112,256]{3,2,1,0:T(8,128)(2,1)S(1)}, u32[]{:S(2)}, u32[]{:S(2)}) collective-permute-start(bf16[4,4,112,256]{3,2,1,0:T(8,128)(2,1)S(1)} %block_sums.5), channel_id=1, source_target_pairs={{0,1},{1,0},{2,3},{3,2},{4,5},{5,4},{6,7},{7,6},{8,9},{9,8},{10,11... | collective-permute-start | bytes 2752520 | tf_op jit(solution)/shard_map/ppermute | solution.py:166
  75.4 27.0 %collective-permute-start.8 = (bf16[4,4,112,256]{3,2,1,0:T(8,128)(2,1)S(1)}, bf16[4,4,112,256]{3,2,1,0:T(8,128)(2,1)S(1)}, u32[]{:S(2)}, u32[]{:S(2)}) collective-permute-start(bf16[4,4,112,256]{3,2,1,0:T(8,128)(2,1)S(1)} %add_convert_fusion.1), channel_id=1, source_target_pairs={{0,2},{2,0},{1,3},{3,1},{4,6},{6,4},{5,7},{7,5},{8,10},{10,8},{9,1... | collective-permute-start | bytes 2752520 | tf_op jit(solution)/shard_map/ppermute | solution.py:166
  79.8 22.6 %collective-permute-start.7 = (bf16[4,4,112,256]{3,2,1,0:T(8,128)(2,1)S(1)}, bf16[4,4,112,256]{3,2,1,0:T(8,128)(2,1)S(1)}, u32[]{:S(2)}, u32[]{:S(2)}) collective-permute-start(bf16[4,4,112,256]{3,2,1,0:T(8,128)(2,1)S(1)} %block_sums.7), channel_id=1, source_target_pairs={{0,1},{1,0},{2,3},{3,2},{4,5},{5,4},{6,7},{7,6},{8,9},{9,8},{10,11... | collective-permute-start | bytes 2752520 | tf_op jit(solution)/shard_map/ppermute | solution.py:166
  82.4 16.6 %collective-permute-start.11 = (bf16[2,128,512]{2,1,0:T(8,128)(2,1)S(1)}, bf16[2,128,512]{2,1,0:T(8,128)(2,1)S(1)}, u32[]{:S(2)}, u32[]{:S(2)}) collective-permute-start(bf16[2,128,512]{2,1,0:T(8,128)(2,1)S(1)} %pad_maximum_fusion.2), channel_id=1, source_target_pairs={{48,0},{0,16},{16,32},{32,48},{49,1},{1,17},{17,33},{33,49},{50,2}... | collective-permute-start | bytes 786440 | tf_op jit(solution)/shard_map/ppermute | solution.py:27
  84.3 14.7 %collective-permute-start.10 = (bf16[2,128,512]{2,1,0:T(8,128)(2,1)S(1)}, bf16[2,128,512]{2,1,0:T(8,128)(2,1)S(1)}, u32[]{:S(2)}, u32[]{:S(2)}) collective-permute-start(bf16[2,128,512]{2,1,0:T(8,128)(2,1)S(1)} %pad_maximum_fusion.2), channel_id=1, source_target_pairs={{32,0},{48,16},{0,32},{16,48},{33,1},{49,17},{1,33},{17,49},{34,2}... | collective-permute-start | bytes 786440 | tf_op jit(solution)/shard_map/ppermute | solution.py:27
  87.7 13.5 %collective-permute-start.9 = (bf16[2,128,512]{2,1,0:T(8,128)(2,1)S(1)}, bf16[2,128,512]{2,1,0:T(8,128)(2,1)S(1)}, u32[]{:S(2)}, u32[]{:S(2)}) collective-permute-start(bf16[2,128,512]{2,1,0:T(8,128)(2,1)S(1)} %pad_maximum_fusion.2), channel_id=1, source_target_pairs={{16,0},{32,16},{48,32},{0,48},{17,1},{33,17},{49,33},{1,49},{18,2}... | collective-permute-start | bytes 786440 | tf_op jit(solution)/shard_map/ppermute | solution.py:27
  103.6 52.5 %all-to-all-start = ((bf16[16,112,256]{2,1,0:T(8,128)(2,1)}), bf16[16,112,256]{2,1,0:T(8,128)(2,1)}, u32[]{:S(2)}, u32[]{:S(2)}) async-start(bf16[16,112,256]{2,1,0:T(8,128)(2,1)} %bitcast.13), calls=%async_computation | async-start | bytes 1835008 | tf_op jit(solution)/shard_map/all_to_all | solution.py:195
  112.2 5.1 %collective-permute-start.12 = (bf16[4,2,128,512]{3,2,1,0:T(8,128)(2,1)}, bf16[4,2,128,512]{3,2,1,0:T(8,128)(2,1)}, u32[]{:S(2)}, u32[]{:S(2)}) collective-permute-start(bf16[4,2,128,512]{3,2,1,0:T(8,128)(2,1)} %pad_maximum_fusion), channel_id=1, source_target_pairs={{130,2},{258,130},{386,258},{2,386},{131,3},{259,131},{387,259},{3... | collective-permute-start | bytes 3145736 | tf_op jit(solution)/shard_map/ppermute | solution.py:159
  113.8 43.7 %collective-permute-start.13 = (bf16[4,2,128,512]{3,2,1,0:T(8,128)(2,1)}, bf16[4,2,128,512]{3,2,1,0:T(8,128)(2,1)}, u32[]{:S(2)}, u32[]{:S(2)}) collective-permute-start(bf16[4,2,128,512]{3,2,1,0:T(8,128)(2,1)} %pad_maximum_fusion), channel_id=1, source_target_pairs={{256,0},{386,2},{384,128},{2,130},{0,256},{130,258},{128,384},{258... | collective-permute-start | bytes 3145736 | tf_op jit(solution)/shard_map/ppermute | solution.py:161
  192.4 4.9 %collective-permute-start.14 = (bf16[4,4,112,256]{3,2,1,0:T(8,128)(2,1)S(1)}, bf16[4,4,112,256]{3,2,1,0:T(8,128)(2,1)S(1)}, u32[]{:S(2)}, u32[]{:S(2)}) collective-permute-start(bf16[4,4,112,256]{3,2,1,0:T(8,128)(2,1)S(1)} %bitcast.36), channel_id=1, source_target_pairs={{0,1},{1,0},{2,3},{3,2},{4,5},{5,4},{6,7},{7,6},{8,9},{9,8},{10,11... | collective-permute-start | bytes 2752520 | tf_op jit(solution)/shard_map/ppermute | solution.py:166
  199.2 15.8 %collective-permute-start.15 = (bf16[2,448,256]{2,1,0:T(8,128)(2,1)S(1)}, bf16[2,448,256]{2,1,0:T(8,128)(2,1)S(1)}, u32[]{:S(2)}, u32[]{:S(2)}) collective-permute-start(bf16[2,448,256]{2,1,0:T(8,128)(2,1)S(1)} %far_products.3), channel_id=1, source_target_pairs={{0,2},{2,0},{1,3},{3,1},{4,6},{6,4},{5,7},{7,5},{8,10},{10,8},{9,1... | collective-permute-start | bytes 1376264 | tf_op jit(solution)/shard_map/ppermute | solution.py:166

commit v7 on v6

--- a/solution.py
+++ b/solution.py
@@ -98,12 +98,11 @@
     )
 
 
-def far_kernel(keep, where_ref, mate_ref, p1_ref, p2_ref, *refs):
-    acts, outs = refs[:2], refs[2:]
-    acc1, acc2 = outs[-2:]
+def far_kernel(where_ref, mate_ref, p1_ref, p2_ref, *refs):
+    acts, (acc1, acc2) = refs[:2], refs[2:]
     here, core = where_ref[0], where_ref[1]
     half = acc1.shape[1]
-    cols = slice(0, half) if keep else slice(half, 2 * half)
+    cols = slice(0, half)
     acc1[...] = p1_ref[:, cols]
     acc2[...] = p2_ref[:, cols]
     side = pieces_of(mate_ref)
@@ -111,11 +110,7 @@
         acc1, acc2, False, lambda j: side(lax.rem(here + j, NX)), acts_of(acts, 1 - core), cols
     )
     total = 2 * NY * NX * acts[0].shape[2]
-    if keep:
-        acc2[...] = acc2[...] / total
-    else:
-        outs[0][0] = acc1[...].astype(BF16)
-        outs[0][1] = (acc2[...] / total).astype(BF16)
+    acc2[...] = acc2[...] / total
 
 
 def near_products(where, mine, acts):
@@ -132,19 +127,48 @@
     )(where, mine, *acts)
 
 
-def far_products(keep, where, mate, p1, p2, acts):
+def far_products(where, mate, p1, p2, acts):
     crows, cols = p1.shape
     shape = jax.ShapeDtypeStruct((crows, cols // 2), F32)
     return pl.pallas_call(
-        functools.partial(far_kernel, keep),
-        out_shape=(shape, shape) if keep else jax.ShapeDtypeStruct((2, crows, cols // 2), BF16),
+        far_kernel,
+        out_shape=(shape, shape),
         in_specs=[SMEM] + [VMEM] * 5,
-        out_specs=(VMEM, VMEM) if keep else VMEM,
-        scratch_shapes=[] if keep else [pltpu.VMEM((crows, cols // 2), F32)] * 2,
+        out_specs=(VMEM, VMEM),
         compiler_params=params(),
         cost_estimate=cost(2 * 448 * 1024 * 512, 5 * 2**20),
         name="far_products",
     )(where, mate, p1, p2, *acts)
+
+
+def away_kernel(squares, where_ref, mate_ref, partial_ref, acts0_ref, acts1_ref, out_ref, acc_ref):
+    here, core = where_ref[0], where_ref[1]
+    half = acc_ref.shape[1]
+    acc_ref[...] = partial_ref[:, half:]
+    acts = acts_of((acts0_ref, acts1_ref), 1 - core)
+    side = pieces_of(mate_ref)
+    for j in range(NX):
+        g, a = side(lax.rem(here + j, NX)), acts(j)[:, half:]
+        if squares:
+            gw, aw = g.astype(F32), a.astype(F32)
+            g, a = (gw * gw).astype(BF16), (aw * aw).astype(BF16)
+        acc_ref[...] += jnp.dot(g, a, preferred_element_type=F32)
+    total = 2 * NY * NX * acts0_ref.shape[2] if squares else 1
+    out_ref[...] = (acc_ref[...] / total).astype(BF16)
+
+
+def away_products(squares, where, mate, partial, acts):
+    crows, cols = partial.shape
+    return pl.pallas_call(
+        functools.partial(away_kernel, squares),
+        out_shape=jax.ShapeDtypeStruct((crows, cols // 2), BF16),
+        in_specs=[SMEM] + [VMEM] * 4,
+        out_specs=VMEM,
+        scratch_shapes=[pltpu.VMEM((crows, cols // 2), F32)],
+        compiler_params=params(),
+        cost_estimate=cost(448 * 1024 * 512, 4 * 2**20),
+        name="away_products",
+    )(where, mate, partial, *acts)
 
 
 def added(*values):
@@ -201,9 +225,10 @@
     mate = swap(mine, "c")
     where = pack(x, core)
     p1, p2 = near_products(where, mine, all_acts)
-    away = swap(far_products(False, where, mate, p1, p2, all_acts), "p")
-    grad, scale = far_products(True, where, mate, p1, p2, all_acts)
-    return grad + away[0].astype(F32), scale + away[1].astype(F32)
+    grad_away = swap(away_products(False, where, mate, p1, all_acts), "p")
+    scale_away = swap(away_products(True, where, mate, p2, all_acts), "p")
+    grad, scale = far_products(where, mate, p1, p2, all_acts)
+    return grad + grad_away.astype(F32), scale + scale_away.astype(F32)
 
 
 def solution(mesh):

time: 218 us -> 218 us (level)
  waiting for transfers between devices: 58 us -> 53.2 us
    ppermute x8 -> x9, waiting for transfers between devices: 9.21 us -> 4.39 us  [body(): swap = lambda v, axis: lax.ppermute(v, axis, [(0, 1), (1, 0)])]
    ppermute x8 -> x9, starting transfers between devices: 39.5 us -> 41.5 us  [body(): swap = lambda v, axis: lax.ppermute(v, axis, [(0, 1), (1, 0)])]
    pallas_call x2 -> x3, Pallas kernels: 3.78 us -> 5.2 us  [the longest x2 3.3 us: away_products(): pl.pallas_call(functools.partial(away_kernel, squares), out_shape=jax.Sha...]
  transfers between devices with their start and end apart: 17 -> 18, of which waited for: 6 -> 7; matrix products, arithmetic and copies ran while one was open for 2% -> 3% of each run, Pallas kernels for 4% -> 5%
where the time goes in v7:
time: 218 us; the launch traced here: 215 us
  starting transfers between devices  72.8 us (33%)
  blocking collectives  61.8 us (28%)
  waiting for transfers between devices  53.2 us (24%)
  Pallas kernels  14.6 us (7%)
  other arithmetic  8.01 us (4%)
    all_gather x3, blocking collectives, body(): gather = lambda v, axis: lax.all_gather(v, axis, axis=0, tiled=False)  61.8 us
    ppermute x9, starting transfers between devices, body(): swap = lambda v, axis: lax.ppermute(v, axis, [(0, 1), (1, 0)])  41.5 us
    all_to_all x1, waiting for transfers between devices, body(): lax.all_to_all(partial.reshape(NM * NX, piece, width), ('m', 'x'), split_...  37.5 us
    ppermute x6, starting transfers between devices, from_rel(): lax.ppermute(value, axis, [((i + step) % size, i) for i in range(size)])  17.8 us
    ppermute x6, waiting for transfers between devices, from_rel(): lax.ppermute(value, axis, [((i + step) % size, i) for i in range(size)])  11.3 us
    all_to_all x1, starting transfers between devices, body(): lax.all_to_all(partial.reshape(NM * NX, piece, width), ('m', 'x'), split_...  8.53 us
    pallas_call x4, Pallas kernels, block_sums(): pl.pallas_call(functools.partial(block_kernel, rel), out_shape=jax.ShapeD...  7.05 us
    ppermute x9, waiting for transfers between devices, body(): swap = lambda v, axis: lax.ppermute(v, axis, [(0, 1), (1, 0)])  4.39 us
  transfers between devices with their start and end apart: 18, of which 7 were waited for; matrix products, arithmetic and copies ran while one was open for 3% of the time, Pallas kernels for 5%

profile of v7, /device:TPU:1, one launch (start us, length us, event | category | flops | bytes accessed | tf_op | source)
XLA Modules:
  0.0 215.1 jit_solution(11389587274453626465)
XLA Ops:
  0.6 0.0 copy-start
  0.6 0.0 copy-start.2
  0.7 1.6 copy-done
  2.2 2.1 convolution_convert_fusion
  4.4 8.8 %collective-permute-start = (bf16[16,128]{1,0:T(8,128)(2,1)S(1)}, bf16[16,128]{1,0:T(8,128)(2,1)S(1)}, u32[]{:S(2)}, u32[]{:S(2)}) collective-permute-start(bf16[16,128]{1,0:T(8,128)(2,1)S(1)} %slice.32), channel_id=1, source_target_pairs={{0,1},{1,0},{2,3},{3,2},{4,5},{5,4},{6,7},{7,6},{8,9},{9,8},{10,11... | collective-permute-start | bytes 12296 | tf_op jit(solution)/shard_map/ppermute | solution.py:190
  13.2 0.0 copy-done.2
  13.2 0.7 pad_maximum_fusion.1
  13.9 10.1 %collective-permute-start.1 = (bf16[128,1152]{1,0:T(8,128)(2,1)}, bf16[128,1152]{1,0:T(8,128)(2,1)S(1)}, u32[]{:S(2)}, u32[]{:S(2)}) collective-permute-start(bf16[128,1152]{1,0:T(8,128)(2,1)} %pad_maximum_fusion.1), channel_id=1, source_target_pairs={{0,64},{64,0},{1,65},{65,1},{2,66},{66,2},{3,67},{67,3},{4,68},{68... | collective-permute-start | bytes 884744 | tf_op jit(solution)/shard_map/ppermute | solution.py:190
  24.0 0.1 add_add_fusion.1.where_ref
  24.1 0.0 collective-permute-done.refs_6_
  24.1 0.0 copy-done.1
  24.1 4.4 %collective-permute-start.3 = (bf16[448,896]{1,0:T(8,128)(2,1)S(1)}, bf16[448,896]{1,0:T(8,128)(2,1)S(1)}, u32[]{:S(2)}, u32[]{:S(2)}) collective-permute-start(bf16[448,896]{1,0:T(8,128)(2,1)S(1)} %copy-done.1), channel_id=1, source_target_pairs={{16,0},{32,16},{48,32},{0,48},{17,1},{33,17},{49,33},{1,49},{18,2}... | collective-permute-start | bytes 2408456 | tf_op jit(solution)/shard_map/ppermute | solution.py:27
  28.5 2.4 %collective-permute-start.4 = (bf16[448,896]{1,0:T(8,128)(2,1)S(1)}, bf16[448,896]{1,0:T(8,128)(2,1)S(1)}, u32[]{:S(2)}, u32[]{:S(2)}) collective-permute-start(bf16[448,896]{1,0:T(8,128)(2,1)S(1)} %copy-done.1), channel_id=1, source_target_pairs={{32,0},{48,16},{0,32},{16,48},{33,1},{49,17},{1,33},{17,49},{34,2}... | collective-permute-start | bytes 2408456 | tf_op jit(solution)/shard_map/ppermute | solution.py:27
  30.9 2.5 %collective-permute-start.5 = (bf16[448,896]{1,0:T(8,128)(2,1)S(1)}, bf16[448,896]{1,0:T(8,128)(2,1)S(1)}, u32[]{:S(2)}, u32[]{:S(2)}) collective-permute-start(bf16[448,896]{1,0:T(8,128)(2,1)S(1)} %copy-done.1), channel_id=1, source_target_pairs={{48,0},{0,16},{16,32},{32,48},{49,1},{1,17},{17,33},{33,49},{50,2}... | collective-permute-start | bytes 2408456 | tf_op jit(solution)/shard_map/ppermute | solution.py:27
  33.4 13.5 %all-gather = bf16[512,896]{1,0:T(8,128)(2,1)S(1)} all-gather(bf16[128,896]{1,0:T(8,128)(2,1)S(1)} %copy-done.2), channel_id=2, replica_groups=mesh['y'=4,'h'=2,'x'=4,'m'=4,'p'=2,'c'=2] {'y'}, dimensions={0}, use_global_device_ids=true | all-gather | bytes 1146880 | tf_op jit(solution)/shard_map/all_gather | solution.py:192
  46.9 0.0 collective-permute-done.1
  46.9 5.7 %collective-permute-start.2 = (bf16[2,128,256]{2,1,0:T(8,128)(2,1)S(1)}, bf16[2,128,256]{2,1,0:T(8,128)(2,1)S(1)}, u32[]{:S(2)}, u32[]{:S(2)}) collective-permute-start(bf16[2,128,256]{2,1,0:T(8,128)(2,1)S(1)} %pad_maximum_fusion.3), channel_id=1, source_target_pairs={{0,2},{2,0},{1,3},{3,1},{4,6},{6,4},{5,7},{7,5},{8,10},{10,8},{9,1... | collective-permute-start | bytes 393224 | tf_op jit(solution)/shard_map/ppermute | solution.py:190
  52.6 13.5 %all-gather.1 = bf16[512,896]{1,0:T(8,128)(2,1)S(1)} all-gather(bf16[128,896]{1,0:T(8,128)(2,1)S(1)} %slice.33), channel_id=3, replica_groups=mesh['y'=4,'h'=2,'x'=4,'m'=4,'p'=2,'c'=2] {'y'}, dimensions={0}, use_global_device_ids=true | all-gather | bytes 1146880 | tf_op jit(solution)/shard_map/all_gather | solution.py:192
  66.2 0.0 collective-permute-done.2
  66.2 0.0 collective-permute-done.3.refs_3_
  66.2 0.0 collective-permute-done.4.refs_4_
  66.2 2.7 %collective-permute-done.5.refs_5_ = bf16[448,896]{1,0:T(8,128)(2,1)S(1)} collective-permute-done((bf16[448,896]{1,0:T(8,128)(2,1)S(1)}, bf16[448,896]{1,0:T(8,128)(2,1)S(1)}, u32[]{:S(2)}, u32[]{:S(2)}) %collective-permute-start.5) | collective-permute-done | bytes 802848 | tf_op jit(solution)/shard_map/ppermute | solution.py:27
  68.9 1.8 block_sums.5
  70.7 2.4 %collective-permute-start.6 = (bf16[4,4,112,256]{3,2,1,0:T(8,128)(2,1)S(1)}, bf16[4,4,112,256]{3,2,1,0:T(8,128)(2,1)S(1)}, u32[]{:S(2)}, u32[]{:S(2)}) collective-permute-start(bf16[4,4,112,256]{3,2,1,0:T(8,128)(2,1)S(1)} %block_sums.5), channel_id=1, source_target_pairs={{0,1},{1,0},{2,3},{3,2},{4,5},{5,4},{6,7},{7,6},{8,9},{9,8},{10,11... | collective-permute-start | bytes 2752520 | tf_op jit(solution)/shard_map/ppermute | solution.py:190
  73.1 0.1 add_add_fusion.where_ref
  73.1 1.8 block_sums.4
  74.9 0.2 collective-permute-done.6
  75.1 0.2 add_convert_fusion.1
  75.4 2.6 %collective-permute-start.8 = (bf16[4,4,112,256]{3,2,1,0:T(8,128)(2,1)S(1)}, bf16[4,4,112,256]{3,2,1,0:T(8,128)(2,1)S(1)}, u32[]{:S(2)}, u32[]{:S(2)}) collective-permute-start(bf16[4,4,112,256]{3,2,1,0:T(8,128)(2,1)S(1)} %add_convert_fusion.1), channel_id=1, source_target_pairs={{0,2},{2,0},{1,3},{3,1},{4,6},{6,4},{5,7},{7,5},{8,10},{10,8},{9,1... | collective-permute-start | bytes 2752520 | tf_op jit(solution)/shard_map/ppermute | solution.py:190
  78.0 1.8 block_sums.7
  79.8 2.6 %collective-permute-start.7 = (bf16[4,4,112,256]{3,2,1,0:T(8,128)(2,1)S(1)}, bf16[4,4,112,256]{3,2,1,0:T(8,128)(2,1)S(1)}, u32[]{:S(2)}, u32[]{:S(2)}) collective-permute-start(bf16[4,4,112,256]{3,2,1,0:T(8,128)(2,1)S(1)} %block_sums.7), channel_id=1, source_target_pairs={{0,1},{1,0},{2,3},{3,2},{4,5},{5,4},{6,7},{7,6},{8,9},{9,8},{10,11... | collective-permute-start | bytes 2752520 | tf_op jit(solution)/shard_map/ppermute | solution.py:190
  82.4 1.9 collective-permute-start.11
  84.3 3.4 %collective-permute-start.10 = (bf16[2,128,512]{2,1,0:T(8,128)(2,1)S(1)}, bf16[2,128,512]{2,1,0:T(8,128)(2,1)S(1)}, u32[]{:S(2)}, u32[]{:S(2)}) collective-permute-start(bf16[2,128,512]{2,1,0:T(8,128)(2,1)S(1)} %pad_maximum_fusion.2), channel_id=1, source_target_pairs={{32,0},{48,16},{0,32},{16,48},{33,1},{49,17},{1,33},{17,49},{34,2}... | collective-permute-start | bytes 786440 | tf_op jit(solution)/shard_map/ppermute | solution.py:27
  87.7 3.1 %collective-permute-start.9 = (bf16[2,128,512]{2,1,0:T(8,128)(2,1)S(1)}, bf16[2,128,512]{2,1,0:T(8,128)(2,1)S(1)}, u32[]{:S(2)}, u32[]{:S(2)}) collective-permute-start(bf16[2,128,512]{2,1,0:T(8,128)(2,1)S(1)} %pad_maximum_fusion.2), channel_id=1, source_target_pairs={{16,0},{32,16},{48,32},{0,48},{17,1},{33,17},{49,33},{1,49},{18,2}... | collective-permute-start | bytes 786440 | tf_op jit(solution)/shard_map/ppermute | solution.py:27
  90.8 1.8 block_sums.6
  92.6 6.4 %collective-permute-done.11 = bf16[2,128,512]{2,1,0:T(8,128)(2,1)S(1)} collective-permute-done((bf16[2,128,512]{2,1,0:T(8,128)(2,1)S(1)}, bf16[2,128,512]{2,1,0:T(8,128)(2,1)S(1)}, u32[]{:S(2)}, u32[]{:S(2)}) %collective-permute-start.11) | collective-permute-done | bytes 262176 | tf_op jit(solution)/shard_map/ppermute | solution.py:27
  99.0 0.0 collective-permute-done.10
  99.0 2.2 %collective-permute-done.9 = bf16[2,128,512]{2,1,0:T(8,128)(2,1)S(1)} collective-permute-done((bf16[2,128,512]{2,1,0:T(8,128)(2,1)S(1)}, bf16[2,128,512]{2,1,0:T(8,128)(2,1)S(1)}, u32[]{:S(2)}, u32[]{:S(2)}) %collective-permute-start.9) | collective-permute-done | bytes 262176 | tf_op jit(solution)/shard_map/ppermute | solution.py:27
  101.2 1.1 pad_maximum_fusion
  102.4 0.0 collective-permute-done.8
  102.4 0.0 collective-permute-done.7
  102.4 1.3 add_convert_fusion
  103.6 8.5 %all-to-all-start = ((bf16[16,112,256]{2,1,0:T(8,128)(2,1)}), bf16[16,112,256]{2,1,0:T(8,128)(2,1)}, u32[]{:S(2)}, u32[]{:S(2)}) async-start(bf16[16,112,256]{2,1,0:T(8,128)(2,1)} %bitcast.13), calls=%async_computation | async-start | bytes 1835008 | tf_op jit(solution)/shard_map/all_to_all | solution.py:219
  112.2 1.6 collective-permute-start.12
  113.8 3.4 %collective-permute-start.13 = (bf16[4,2,128,512]{3,2,1,0:T(8,128)(2,1)}, bf16[4,2,128,512]{3,2,1,0:T(8,128)(2,1)}, u32[]{:S(2)}, u32[]{:S(2)}) collective-permute-start(bf16[4,2,128,512]{3,2,1,0:T(8,128)(2,1)} %pad_maximum_fusion), channel_id=1, source_target_pairs={{256,0},{386,2},{384,128},{2,130},{0,256},{130,258},{128,384},{258... | collective-permute-start | bytes 3145736 | tf_op jit(solution)/shard_map/ppermute | solution.py:185
  117.2 0.0 collective-permute-done.12
  117.2 1.4 broadcast_select_fusion.refs_0_.acts0_ref
  118.6 37.5 %all-to-all-done = bf16[16,112,256]{2,1,0:T(8,128)(2,1)} async-done(((bf16[16,112,256]{2,1,0:T(8,128)(2,1)}), bf16[16,112,256]{2,1,0:T(8,128)(2,1)}, u32[]{:S(2)}, u32[]{:S(2)}) %all-to-all-start) | async-done | bytes 917536 | tf_op jit(solution)/shard_map/all_to_all | solution.py:219
  156.2 1.4 add_convert_fusion.2
  157.5 0.0 collective-permute-done.13.refs_1_.acts1_ref
  157.6 34.8 %all-gather.2 = bf16[16,112,256]{2,1,0:T(8,128)(2,1)S(1)} all-gather(bf16[4,112,256]{2,1,0:T(8,128)(2,1)S(1)} %add_convert_fusion.2), channel_id=4, replica_groups=mesh['y'=4,'h'=2,'x'=4,'m'=4,'p'=2,'c'=2] {'m'}, dimensions={0}, use_global_device_ids=true | all-gather | bytes 1146880 | tf_op jit(solution)/shard_map/all_gather | solution.py:192
  192.4 2.5 %collective-permute-start.14 = (bf16[4,4,112,256]{3,2,1,0:T(8,128)(2,1)S(1)}, bf16[4,4,112,256]{3,2,1,0:T(8,128)(2,1)S(1)}, u32[]{:S(2)}, u32[]{:S(2)}) collective-permute-start(bf16[4,4,112,256]{3,2,1,0:T(8,128)(2,1)S(1)} %bitcast.26), channel_id=1, source_target_pairs={{0,1},{1,0},{2,3},{3,2},{4,5},{5,4},{6,7},{7,6},{8,9},{9,8},{10,11... | collective-permute-start | bytes 2752520 | tf_op jit(solution)/shard_map/ppermute | solution.py:190
  194.9 0.1 pad_add_fusion.where_ref
  194.9 2.3 %near_products.1 = (f32[448,512]{1,0:T(8,128)S(1)}, f32[448,512]{1,0:T(8,128)S(1)}) custom-call(s32[2]{0:T(128)S(1)} %pad_add_fusion.where_ref, bf16[4,4,112,256]{3,2,1,0:T(8,128)(2,1)S(1)} %bitcast.27, bf16[4,2,128,512]{3,2,1,0:T(8,128)(2,1)S(1)} %broadcast_select_fusion.refs_0_.acts0_ref, bf16[4,2,128,512]{3,2,1,0:T(8,128)(2,1)} %collective-permute-done.13.refs_1_.acts1_ref), custom_call_target="tpu_custom_call" | custom-call | flops 939524096 | bytes 5242880 | tf_op jit(solution)/shard_map/near_products/pallas_call | solution.py:119
  197.3 0.0 collective-permute-done.14.mate_ref
  197.3 1.6 away_products.2
  199.0 4.9 %collective-permute-start.15 = (bf16[448,256]{1,0:T(8,128)(2,1)S(1)}, bf16[448,256]{1,0:T(8,128)(2,1)S(1)}, u32[]{:S(2)}, u32[]{:S(2)}) collective-permute-start(bf16[448,256]{1,0:T(8,128)(2,1)S(1)} %away_products.2), channel_id=1, source_target_pairs={{0,2},{2,0},{1,3},{3,1},{4,6},{6,4},{5,7},{7,5},{8,10},{10,8},{9,1... | collective-permute-start | bytes 688136 | tf_op jit(solution)/shard_map/ppermute | solution.py:190
  203.9 1.7 away_products.3
  205.5 1.9 collective-permute-start.16
  207.5 1.9 far_products.1
  209.4 0.5 collective-permute-done.15
  209.8 0.8 convert_add_fusion.1
  210.6 3.7 %collective-permute-done.16 = bf16[448,256]{1,0:T(8,128)(2,1)S(1)} collective-permute-done((bf16[448,256]{1,0:T(8,128)(2,1)S(1)}, bf16[448,256]{1,0:T(8,128)(2,1)S(1)}, u32[]{:S(2)}, u32[]{:S(2)}) %collective-permute-start.16) | collective-permute-done | bytes 229408 | tf_op jit(solution)/shard_map/ppermute | solution.py:190
  214.3 0.8 convert_add_fusion
  (6 shorter events, 0.1 us)
Async XLA Ops:
  0.6 1.6 copy-start
  0.6 12.5 %copy-start.2 = (bf16[128,896]{1,0:T(8,128)(2,1)S(1)}, bf16[128,896]{1,0:T(8,128)(2,1)}, u32[]{:S(2)}) copy-start(bf16[128,896]{1,0:T(8,128)(2,1)} %param.6) | copy-start | bytes 688132
  2.2 21.9 %copy-start.1 = (bf16[448,896]{1,0:T(8,128)(2,1)S(1)}, bf16[448,896]{1,0:T(8,128)(2,1)}, u32[]{:S(2)}) copy-start(bf16[448,896]{1,0:T(8,128)(2,1)} %refs_2_.3) | copy-start | bytes 2408452
  4.4 19.7 %collective-permute-start = (bf16[16,128]{1,0:T(8,128)(2,1)S(1)}, bf16[16,128]{1,0:T(8,128)(2,1)S(1)}, u32[]{:S(2)}, u32[]{:S(2)}) collective-permute-start(bf16[16,128]{1,0:T(8,128)(2,1)S(1)} %slice.32), channel_id=1, source_target_pairs={{0,1},{1,0},{2,3},{3,2},{4,5},{5,4},{6,7},{7,6},{8,9},{9,8},{10,11... | collective-permute-start | bytes 12296 | tf_op jit(solution)/shard_map/ppermute | solution.py:190
  13.9 33.0 %collective-permute-start.1 = (bf16[128,1152]{1,0:T(8,128)(2,1)}, bf16[128,1152]{1,0:T(8,128)(2,1)S(1)}, u32[]{:S(2)}, u32[]{:S(2)}) collective-permute-start(bf16[128,1152]{1,0:T(8,128)(2,1)} %pad_maximum_fusion.1), channel_id=1, source_target_pairs={{0,64},{64,0},{1,65},{65,1},{2,66},{66,2},{3,67},{67,3},{4,68},{68... | collective-permute-start | bytes 884744 | tf_op jit(solution)/shard_map/ppermute | solution.py:190
  24.1 42.1 %collective-permute-start.3 = (bf16[448,896]{1,0:T(8,128)(2,1)S(1)}, bf16[448,896]{1,0:T(8,128)(2,1)S(1)}, u32[]{:S(2)}, u32[]{:S(2)}) collective-permute-start(bf16[448,896]{1,0:T(8,128)(2,1)S(1)} %copy-done.1), channel_id=1, source_target_pairs={{16,0},{32,16},{48,32},{0,48},{17,1},{33,17},{49,33},{1,49},{18,2}... | collective-permute-start | bytes 2408456 | tf_op jit(solution)/shard_map/ppermute | solution.py:27
  28.5 37.7 %collective-permute-start.4 = (bf16[448,896]{1,0:T(8,128)(2,1)S(1)}, bf16[448,896]{1,0:T(8,128)(2,1)S(1)}, u32[]{:S(2)}, u32[]{:S(2)}) collective-permute-start(bf16[448,896]{1,0:T(8,128)(2,1)S(1)} %copy-done.1), channel_id=1, source_target_pairs={{32,0},{48,16},{0,32},{16,48},{33,1},{49,17},{1,33},{17,49},{34,2}... | collective-permute-start | bytes 2408456 | tf_op jit(solution)/shard_map/ppermute | solution.py:27
  30.9 38.0 %collective-permute-start.5 = (bf16[448,896]{1,0:T(8,128)(2,1)S(1)}, bf16[448,896]{1,0:T(8,128)(2,1)S(1)}, u32[]{:S(2)}, u32[]{:S(2)}) collective-permute-start(bf16[448,896]{1,0:T(8,128)(2,1)S(1)} %copy-done.1), channel_id=1, source_target_pairs={{48,0},{0,16},{16,32},{32,48},{49,1},{1,17},{17,33},{33,49},{50,2}... | collective-permute-start | bytes 2408456 | tf_op jit(solution)/shard_map/ppermute | solution.py:27
  46.9 19.2 %collective-permute-start.2 = (bf16[2,128,256]{2,1,0:T(8,128)(2,1)S(1)}, bf16[2,128,256]{2,1,0:T(8,128)(2,1)S(1)}, u32[]{:S(2)}, u32[]{:S(2)}) collective-permute-start(bf16[2,128,256]{2,1,0:T(8,128)(2,1)S(1)} %pad_maximum_fusion.3), channel_id=1, source_target_pairs={{0,2},{2,0},{1,3},{3,1},{4,6},{6,4},{5,7},{7,5},{8,10},{10,8},{9,1... | collective-permute-start | bytes 393224 | tf_op jit(solution)/shard_map/ppermute | solution.py:190
  70.7 4.5 %collective-permute-start.6 = (bf16[4,4,112,256]{3,2,1,0:T(8,128)(2,1)S(1)}, bf16[4,4,112,256]{3,2,1,0:T(8,128)(2,1)S(1)}, u32[]{:S(2)}, u32[]{:S(2)}) collective-permute-start(bf16[4,4,112,256]{3,2,1,0:T(8,128)(2,1)S(1)} %block_sums.5), channel_id=1, source_target_pairs={{0,1},{1,0},{2,3},{3,2},{4,5},{5,4},{6,7},{7,6},{8,9},{9,8},{10,11... | collective-permute-start | bytes 2752520 | tf_op jit(solution)/shard_map/ppermute | solution.py:190
  75.4 27.0 %collective-permute-start.8 = (bf16[4,4,112,256]{3,2,1,0:T(8,128)(2,1)S(1)}, bf16[4,4,112,256]{3,2,1,0:T(8,128)(2,1)S(1)}, u32[]{:S(2)}, u32[]{:S(2)}) collective-permute-start(bf16[4,4,112,256]{3,2,1,0:T(8,128)(2,1)S(1)} %add_convert_fusion.1), channel_id=1, source_target_pairs={{0,2},{2,0},{1,3},{3,1},{4,6},{6,4},{5,7},{7,5},{8,10},{10,8},{9,1... | collective-permute-start | bytes 2752520 | tf_op jit(solution)/shard_map/ppermute | solution.py:190
  79.8 22.6 %collective-permute-start.7 = (bf16[4,4,112,256]{3,2,1,0:T(8,128)(2,1)S(1)}, bf16[4,4,112,256]{3,2,1,0:T(8,128)(2,1)S(1)}, u32[]{:S(2)}, u32[]{:S(2)}) collective-permute-start(bf16[4,4,112,256]{3,2,1,0:T(8,128)(2,1)S(1)} %block_sums.7), channel_id=1, source_target_pairs={{0,1},{1,0},{2,3},{3,2},{4,5},{5,4},{6,7},{7,6},{8,9},{9,8},{10,11... | collective-permute-start | bytes 2752520 | tf_op jit(solution)/shard_map/ppermute | solution.py:190
  82.4 16.6 %collective-permute-start.11 = (bf16[2,128,512]{2,1,0:T(8,128)(2,1)S(1)}, bf16[2,128,512]{2,1,0:T(8,128)(2,1)S(1)}, u32[]{:S(2)}, u32[]{:S(2)}) collective-permute-start(bf16[2,128,512]{2,1,0:T(8,128)(2,1)S(1)} %pad_maximum_fusion.2), channel_id=1, source_target_pairs={{48,0},{0,16},{16,32},{32,48},{49,1},{1,17},{17,33},{33,49},{50,2}... | collective-permute-start | bytes 786440 | tf_op jit(solution)/shard_map/ppermute | solution.py:27
  84.3 14.7 %collective-permute-start.10 = (bf16[2,128,512]{2,1,0:T(8,128)(2,1)S(1)}, bf16[2,128,512]{2,1,0:T(8,128)(2,1)S(1)}, u32[]{:S(2)}, u32[]{:S(2)}) collective-permute-start(bf16[2,128,512]{2,1,0:T(8,128)(2,1)S(1)} %pad_maximum_fusion.2), channel_id=1, source_target_pairs={{32,0},{48,16},{0,32},{16,48},{33,1},{49,17},{1,33},{17,49},{34,2}... | collective-permute-start | bytes 786440 | tf_op jit(solution)/shard_map/ppermute | solution.py:27
  87.7 13.5 %collective-permute-start.9 = (bf16[2,128,512]{2,1,0:T(8,128)(2,1)S(1)}, bf16[2,128,512]{2,1,0:T(8,128)(2,1)S(1)}, u32[]{:S(2)}, u32[]{:S(2)}) collective-permute-start(bf16[2,128,512]{2,1,0:T(8,128)(2,1)S(1)} %pad_maximum_fusion.2), channel_id=1, source_target_pairs={{16,0},{32,16},{48,32},{0,48},{17,1},{33,17},{49,33},{1,49},{18,2}... | collective-permute-start | bytes 786440 | tf_op jit(solution)/shard_map/ppermute | solution.py:27
  103.6 52.5 %all-to-all-start = ((bf16[16,112,256]{2,1,0:T(8,128)(2,1)}), bf16[16,112,256]{2,1,0:T(8,128)(2,1)}, u32[]{:S(2)}, u32[]{:S(2)}) async-start(bf16[16,112,256]{2,1,0:T(8,128)(2,1)} %bitcast.13), calls=%async_computation | async-start | bytes 1835008 | tf_op jit(solution)/shard_map/all_to_all | solution.py:219
  112.2 5.1 %collective-permute-start.12 = (bf16[4,2,128,512]{3,2,1,0:T(8,128)(2,1)}, bf16[4,2,128,512]{3,2,1,0:T(8,128)(2,1)}, u32[]{:S(2)}, u32[]{:S(2)}) collective-permute-start(bf16[4,2,128,512]{3,2,1,0:T(8,128)(2,1)} %pad_maximum_fusion), channel_id=1, source_target_pairs={{130,2},{258,130},{386,258},{2,386},{131,3},{259,131},{387,259},{3... | collective-permute-start | bytes 3145736 | tf_op jit(solution)/shard_map/ppermute | solution.py:183
  113.8 43.7 %collective-permute-start.13 = (bf16[4,2,128,512]{3,2,1,0:T(8,128)(2,1)}, bf16[4,2,128,512]{3,2,1,0:T(8,128)(2,1)}, u32[]{:S(2)}, u32[]{:S(2)}) collective-permute-start(bf16[4,2,128,512]{3,2,1,0:T(8,128)(2,1)} %pad_maximum_fusion), channel_id=1, source_target_pairs={{256,0},{386,2},{384,128},{2,130},{0,256},{130,258},{128,384},{258... | collective-permute-start | bytes 3145736 | tf_op jit(solution)/shard_map/ppermute | solution.py:185
  192.4 4.9 %collective-permute-start.14 = (bf16[4,4,112,256]{3,2,1,0:T(8,128)(2,1)S(1)}, bf16[4,4,112,256]{3,2,1,0:T(8,128)(2,1)S(1)}, u32[]{:S(2)}, u32[]{:S(2)}) collective-permute-start(bf16[4,4,112,256]{3,2,1,0:T(8,128)(2,1)S(1)} %bitcast.26), channel_id=1, source_target_pairs={{0,1},{1,0},{2,3},{3,2},{4,5},{5,4},{6,7},{7,6},{8,9},{9,8},{10,11... | collective-permute-start | bytes 2752520 | tf_op jit(solution)/shard_map/ppermute | solution.py:190
  199.0 10.9 %collective-permute-start.15 = (bf16[448,256]{1,0:T(8,128)(2,1)S(1)}, bf16[448,256]{1,0:T(8,128)(2,1)S(1)}, u32[]{:S(2)}, u32[]{:S(2)}) collective-permute-start(bf16[448,256]{1,0:T(8,128)(2,1)S(1)} %away_products.2), channel_id=1, source_target_pairs={{0,2},{2,0},{1,3},{3,1},{4,6},{6,4},{5,7},{7,5},{8,10},{10,8},{9,1... | collective-permute-start | bytes 688136 | tf_op jit(solution)/shard_map/ppermute | solution.py:190
  205.5 8.8 %collective-permute-start.16 = (bf16[448,256]{1,0:T(8,128)(2,1)S(1)}, bf16[448,256]{1,0:T(8,128)(2,1)S(1)}, u32[]{:S(2)}, u32[]{:S(2)}) collective-permute-start(bf16[448,256]{1,0:T(8,128)(2,1)S(1)} %away_products.3), channel_id=1, source_target_pairs={{0,2},{2,0},{1,3},{3,1},{4,6},{6,4},{5,7},{7,5},{8,10},{10,8},{9,1... | collective-permute-start | bytes 688136 | tf_op jit(solution)/shard_map/ppermute | solution.py:190
